TPU v7x, 128 devices: a whole 4x4x4 slice. The times are simulated.
128 devices in a mesh: gx: 8 (over y, core), gy: 16 (over z, x).
Axes of the slice: x: 4, y: 4, z: 4, core: 2. Of those that a mesh axis runs over, the one named last changes fastest.
Arguments:
- material: int32 [4, 2048, 4096], P(None, 'gx', 'gy'), may hold values from 0 to 15
- material_table: float32 [2, 16], replicated, may hold values from 0.5 to 4
- sink_cond: float32 [2048, 4096], P('gx', 'gy'), may hold values from 0.05 to 0.5
- drain_current: float32 [2048, 4096], P('gx', 'gy'), may hold values from 0.05 to 0.5
- instance_tile: int32 [262144], P(('gx', 'gy')), may hold values from 0 to 131071, as said below
- instance_power: float32 [262144], P(('gx', 'gy')), may hold values from 4 to 40
Outputs:
- thermal_rise: float32 [4, 2048, 4096], P(None, 'gx', 'gy')
- dynamic_wattage: float32 [2048, 4096], P('gx', 'gy')
Inputs may be any that keep to these rules, and one draw needn't show every extreme that they name: Instance i adds its power to tile instance_tile[i]; in each aligned block of 2048 instances (the list of one device) at most 32 instances have tiles of one subdomain (instance_tile // 1024), and in every draw some subdomain gets exactly 32 from every block.
All inputs are finite; a program needn't handle non-finite values.
Results may differ from a plain program's by a relative error of at most 0.0003.
Values sent between devices are 32-bit elements; how exact they have to be, the bound alone decides.
A program may use at most 128 MiB of HBM per device.

v0:
```python
import jax
import jax.numpy as jnp
from jax import lax
from jax.sharding import PartitionSpec as P

PB = 8
SUBX = 8
SUBY = 8
OV = 2
SWEEPS = 2
CJ = 8
OUTER = 2
INNER = 2


DAMPING = 0.8
DRAIN_SLOPE = 0.5
FACE_FLOOR = 0.5
BALANCE_WEIGHT = 0.5


def extended(cells, sides, width):
    for axis, dim in sides:
        count = lax.axis_size(axis)
        ends = count - 1
        head = lax.slice_in_dim(cells, 0, width, axis=dim)
        tail = lax.slice_in_dim(cells, cells.shape[dim] - width, cells.shape[dim], axis=dim)
        cells = jnp.concatenate(
            [
                lax.ppermute(tail, axis, [(i, (i + 1) % count) for i in range(ends)]),
                cells,
                lax.ppermute(head, axis, [((i + 1) % count, i) for i in range(ends)]),
            ],
            axis=dim,
        )
    return cells


def lookup(material, table_row):
    summed = jnp.zeros(material.shape, jnp.float32)
    for number in range(table_row.shape[0]):
        summed = summed + jnp.where(material == number, table_row[number], jnp.float32(0.0))
    return summed


def harmonic(left_value, right_value):
    return 2.0 * left_value * right_value / jnp.maximum(left_value + right_value, FACE_FLOOR)


def diagonal(coeffs, sink_ext):
    upper_face, lower_face, left_face, right_face, vertical = coeffs
    zero_layer = jnp.zeros_like(vertical[:1])
    summed = upper_face + lower_face + left_face + right_face
    summed = (
        summed
        + jnp.concatenate([zero_layer, vertical], 0)
        + jnp.concatenate([vertical, zero_layer], 0)
    )
    summed = summed + jnp.concatenate([jnp.zeros_like(summed[:-1]), sink_ext[None]], 0)
    return jnp.maximum(summed, FACE_FLOOR)


def face_terms(lateral, vertical_cond, sink_padded, margin):
    face_row = harmonic(lateral[:, :-1, :], lateral[:, 1:, :])
    face_col = harmonic(lateral[:, :, :-1], lateral[:, :, 1:])
    face_ver = harmonic(vertical_cond[:-1], vertical_cond[1:])
    ext_rows = lateral.shape[1] - 2
    ext_cols = lateral.shape[2] - 2
    coeffs = (
        face_row[:, 0:ext_rows, 1 : ext_cols + 1],
        face_row[:, 1 : ext_rows + 1, 1 : ext_cols + 1],
        face_col[:, 1 : ext_rows + 1, 0:ext_cols],
        face_col[:, 1 : ext_rows + 1, 1 : ext_cols + 1],
        face_ver[:, 1 : ext_rows + 1, 1 : ext_cols + 1],
    )
    sink_ext = sink_padded[1 : ext_rows + 1, 1 : ext_cols + 1]
    rim_width = margin + 1
    overall_height = ext_rows - 2 * margin
    width_cells = ext_cols - 2 * margin
    inner_faces = (
        face_row[:, rim_width : rim_width + overall_height, rim_width : rim_width + width_cells],
        face_col[:, rim_width : rim_width + overall_height, rim_width : rim_width + width_cells],
        face_ver[:, rim_width : rim_width + overall_height, rim_width : rim_width + width_cells],
        sink_padded[rim_width : rim_width + overall_height, rim_width : rim_width + width_cells],
    )
    return (coeffs, diagonal(coeffs, sink_ext), inner_faces)


def couple(margined_array, coeffs):
    upper_face, lower_face, left_face, right_face, vertical = coeffs
    centre = margined_array[:, 1:-1, 1:-1]
    lateral = (
        upper_face * margined_array[:, :-2, 1:-1]
        + lower_face * margined_array[:, 2:, 1:-1]
        + left_face * margined_array[:, 1:-1, :-2]
        + right_face * margined_array[:, 1:-1, 2:]
    )
    zero_layer = jnp.zeros_like(vertical[:1])
    from_above = jnp.concatenate([zero_layer, vertical * centre[:-1]], 0)
    from_below = jnp.concatenate([vertical * centre[1:], zero_layer], 0)
    return lateral + from_above + from_below


def residual_of(thermal_forcing, margined_array, coeffs, diagonal_term):
    return thermal_forcing - (
        diagonal_term * margined_array[:, 1:-1, 1:-1] - couple(margined_array, coeffs)
    )


def smooth(residual, coeffs, diagonal_term, sweeps):
    correction = jnp.zeros_like(residual)
    for number in range(sweeps):
        margined_array = jnp.pad(correction, ((0, 0), (1, 1), (1, 1)))
        correction = (1.0 - DAMPING) * correction + DAMPING * (
            residual + couple(margined_array, coeffs)
        ) / diagonal_term
    return correction


def assemble_forcing(dynamic_wattage, drain_current, thermal_rise):
    topmost_ply = dynamic_wattage + drain_current * jnp.exp(DRAIN_SLOPE * thermal_rise[0])
    leftover = jnp.zeros((thermal_rise.shape[0] - 1,) + topmost_ply.shape, topmost_ply.dtype)
    return jnp.concatenate([topmost_ply[None], leftover], 0)


def coarse_terms(inner_faces, row_blocks, col_blocks):
    face_row, face_col, face_ver, sink_inner = inner_faces
    number_plies, overall_height, width_cells = face_row.shape
    block_row_count = overall_height // row_blocks
    block_column_count = width_cells // col_blocks
    east_face = face_row.reshape(
        number_plies, row_blocks, block_row_count, col_blocks, block_column_count
    )[:, :, block_row_count - 1].sum(axis=-1)
    north_face = face_col.reshape(
        number_plies, row_blocks, block_row_count, col_blocks, block_column_count
    )[:, :, :, :, block_column_count - 1].sum(axis=2)
    vertical_sum = face_ver.reshape(
        number_plies - 1, row_blocks, block_row_count, col_blocks, block_column_count
    ).sum(axis=(2, 4))
    sink_sums = sink_inner.reshape(row_blocks, block_row_count, col_blocks, block_column_count).sum(
        axis=(1, 3)
    )
    return jnp.concatenate([east_face, north_face, vertical_sum, sink_sums[None]], 0)


def unpack_coarse(coarse_stack, number_plies):
    east_face = coarse_stack[:number_plies]
    north_face = coarse_stack[number_plies : 2 * number_plies]
    vertical = coarse_stack[2 * number_plies : 3 * number_plies - 1]
    sink_sums = coarse_stack[3 * number_plies - 1]
    east_prev = jnp.pad(east_face, ((0, 0), (1, 0), (0, 0)))[:, :-1]
    north_prev = jnp.pad(north_face, ((0, 0), (0, 0), (1, 0)))[:, :, :-1]
    return (east_face, east_prev, north_face, north_prev, vertical, sink_sums)


def coarse_diagonal(coarse_stack, number_plies):
    east_face, east_prev, north_face, north_prev, vertical, sink_sums = unpack_coarse(
        coarse_stack, number_plies
    )
    zero_layer = jnp.zeros_like(vertical[:1])
    summed = east_face + east_prev + north_face + north_prev
    summed = (
        summed
        + jnp.concatenate([zero_layer, vertical], 0)
        + jnp.concatenate([vertical, zero_layer], 0)
    )
    return summed + jnp.concatenate([jnp.zeros_like(summed[:-1]), sink_sums[None]], 0)


def coarse_solve(coarse_resid, coarse_stack, coarse_diag, number_plies, sweeps):
    east_face, east_prev, north_face, north_prev, vertical, sink_sums = unpack_coarse(
        coarse_stack, number_plies
    )
    zero_layer = jnp.zeros_like(vertical[:1])
    solution = jnp.zeros_like(coarse_resid)
    for number in range(sweeps):
        margined_array = jnp.pad(solution, ((0, 0), (1, 1), (1, 1)))
        neighbours = (
            east_face * margined_array[:, 2:, 1:-1]
            + east_prev * margined_array[:, :-2, 1:-1]
            + north_face * margined_array[:, 1:-1, 2:]
            + north_prev * margined_array[:, 1:-1, :-2]
        )
        neighbours = neighbours + jnp.concatenate([zero_layer, vertical * solution[:-1]], 0)
        neighbours = neighbours + jnp.concatenate([vertical * solution[1:], zero_layer], 0)
        solution = (1.0 - DAMPING) * solution + DAMPING * (coarse_resid + neighbours) / coarse_diag
    balance = BALANCE_WEIGHT * jnp.sum(coarse_resid) / jnp.sum(coarse_diag)
    return solution + balance


def distribute(values, row_rep, col_rep):
    leading = values.shape[:-2]
    overall_height, width_cells = (values.shape[-2], values.shape[-1])
    expanded = jnp.broadcast_to(
        values[..., :, None, :, None], leading + (overall_height, row_rep, width_cells, col_rep)
    )
    return expanded.reshape(leading + (overall_height * row_rep, width_cells * col_rep))


def place_blocks(own_blocks, row_index, col_index, row_devices, col_devices):
    channels, row_blocks, col_blocks = own_blocks.shape
    whole = jnp.zeros((channels, row_blocks * row_devices, col_blocks * col_devices), jnp.float32)
    return lax.dynamic_update_slice(
        whole, own_blocks, (jnp.int32(0), row_index * row_blocks, col_index * col_blocks)
    )


def collect_matrix(own_blocks, row_index, col_index, row_devices, col_devices):
    whole = place_blocks(own_blocks, row_index, col_index, row_devices, col_devices)
    return lax.psum(whole, ("gx", "gy"))


def collect_residual(own_blocks, row_index, col_index, row_devices, col_devices):
    whole = place_blocks(own_blocks, row_index, col_index, row_devices, col_devices)
    return lax.psum(whole, ("gx", "gy"))


def owned_tile_power(instance_tile, instance_power, tiles_dev, devices):
    tile_sums = jax.ops.segment_sum(instance_power, instance_tile, num_segments=tiles_dev * devices)
    return lax.psum_scatter(tile_sums, ("gx", "gy"), scatter_dimension=0, tiled=True)


def local(material, material_table, sink_cond, drain_current, instance_tile, instance_power):
    number_plies, overall_height, width_cells = material.shape
    rim_width = OV + 1
    stacked = jnp.concatenate(
        [lookup(material, material_table[0]), lookup(material, material_table[1]), sink_cond[None]],
        0,
    )
    widened = extended(stacked, (("gx", 1), ("gy", 2)), rim_width)
    coeffs, diagonal_term, inner_faces = face_terms(
        widened[:number_plies],
        widened[number_plies : 2 * number_plies],
        widened[2 * number_plies],
        OV,
    )
    row_index = lax.axis_index("gx")
    col_index = lax.axis_index("gy")
    row_devices = lax.axis_size("gx")
    col_devices = lax.axis_size("gy")
    own_matrix = coarse_terms(inner_faces, SUBX, SUBY)
    coarse_stack = collect_matrix(own_matrix, row_index, col_index, row_devices, col_devices)
    coarse_diag = coarse_diagonal(coarse_stack, number_plies)
    tile_rows = overall_height // PB
    tile_cols = width_cells // PB
    own_tiles = owned_tile_power(
        instance_tile, instance_power, tile_rows * tile_cols, row_devices * col_devices
    )
    dynamic_wattage = distribute(own_tiles.reshape(tile_rows, tile_cols) / (PB * PB), PB, PB)
    own_coeffs = tuple(
        (coefficient[:, OV : OV + overall_height, OV : OV + width_cells] for coefficient in coeffs)
    )
    own_diagonal = diagonal_term[:, OV : OV + overall_height, OV : OV + width_cells]
    block_row_count = overall_height // SUBX
    block_column_count = width_cells // SUBY
    thermal_rise = jnp.zeros((number_plies, overall_height, width_cells), jnp.float32)
    for outer_step in range(OUTER):
        thermal_forcing = assemble_forcing(dynamic_wattage, drain_current, thermal_rise)
        for inner_step in range(INNER):
            seal_margin = extended(thermal_rise, (("gx", 1), ("gy", 2)), 1)
            own_resid = residual_of(thermal_forcing, seal_margin, own_coeffs, own_diagonal)
            residual = extended(own_resid, (("gx", 1), ("gy", 2)), OV)
            subdomain_piece = smooth(residual, coeffs, diagonal_term, SWEEPS)[
                :, OV : OV + overall_height, OV : OV + width_cells
            ]
            coarse_own = own_resid.reshape(
                number_plies, SUBX, block_row_count, SUBY, block_column_count
            ).sum(axis=(2, 4))
            coarse_resid = collect_residual(
                coarse_own, row_index, col_index, row_devices, col_devices
            )
            aggregate_estimate = coarse_solve(
                coarse_resid, coarse_stack, coarse_diag, number_plies, CJ
            )
            owned_value = lax.dynamic_slice(
                aggregate_estimate,
                (jnp.int32(0), row_index * SUBX, col_index * SUBY),
                (number_plies, SUBX, SUBY),
            )
            thermal_rise = (
                thermal_rise
                + subdomain_piece
                + distribute(owned_value, block_row_count, block_column_count)
            )
    return (thermal_rise, dynamic_wattage)


def solution(mesh):
    return jax.shard_map(
        local,
        mesh=mesh,
        in_specs=(
            P(None, "gx", "gy"),
            P(),
            P("gx", "gy"),
            P("gx", "gy"),
            P(("gx", "gy")),
            P(("gx", "gy")),
        ),
        out_specs=(P(None, "gx", "gy"), P("gx", "gy")),
        check_vma=False,
    )
```

profile of v0, /device:TPU:1, one launch (start us, length us, event | category | flops | bytes accessed | tf_op | source)
XLA Modules:
  0.0 1054.6 jit_solution(10852109782917673455)
XLA Ops:
  7.2 4.7 collective-permute-start.4
  13.9 12.2 %scatter_custom_fusion = f32[131072]{0:T(1024)} fusion(s32[2048]{0:T(1024)} %param.10, f32[2048]{0:T(1024)} %param.11, f32[]{:T(128)} %constant.27.clone.1), kind=kCustom, calls=%fused_computation.304 | custom fusion | flops 2048 | bytes 524800 | tf_op jit(solution)/shard_map/scatter-add | solution.py:219
  30.1 13.9 %select_add_fusion.1 = (f32[4,256,256]{2,1,0:T(8,128)S(1)}, pred[4,256,256]{2,1,0:T(8,128)(4,1)S(1)}, pred[4,256,256]{2,1,0:T(8,128)(4,1)S(1)}, pred[4,256,256]{...) fusion(f32[]{:T(128)} %bitcast.16, f32[]{:T(128)} %bitcast.15, ...), kind=kLoop, calls=%fused_computation.149 | loop fusion | flops 12320768 | bytes 6291520 | tf_op jit(solution)/shard_map/add | solution.py:42
  44.0 12.2 %select_add_fusion = f32[4,256,256]{2,1,0:T(8,128)S(1)} fusion(pred[4,256,256]{2,1,0:T(8,128)(4,1)S(1)} %get-tuple-element.33, pred[4,256,256]{2,1,0:T(8,128)(4,1)S(1)} %get-tuple-element.32, pred[4,256,256]{2,1,0:T(8,128)(4,1)S(1)} %get-tuple-element.31, pred[4,256,256]{2,1,0:T(8,128)(4,1)S(1)} %get-tuple-element.30, ...), kind=kLoop, calls=%fused_computation.148 | loop fusion | flops 8126464 | bytes 5242944 | tf_op jit(solution)/shard_map/add | solution.py:42
  58.9 3.6 collective-permute-start
  65.5 4.0 collective-permute-start.6
  75.5 4.8 collective-permute-start.2
  86.6 5.0 pad_maximum_fusion
  97.5 3.7 reshape.125
  102.5 3.8 reshape.124
  108.4 2.6 add_maximum_fusion
  112.2 61.7 %all-reduce.136.cloned.1.call-done = f32[131072]{0:T(1024)} async-done(((f32[131072]{0:T(1024)}), f32[131072]{0:T(1024)}) %all-reduce.136.cloned.1.call-update) | async-done | bytes 524304
  174.6 2.6 broadcast_in_dim.190
  177.2 4.2 reshape.122
  182.6 5.4 pad_subtract_fusion.3
  191.6 3.6 collective-permute-start.8
  197.6 3.1 reshape.126
  210.7 4.0 collective-permute-start.10
  217.7 3.7 reshape.123
  221.5 2.6 reduce_sum.129
  227.4 6.6 multiply_divide_fusion.3
  234.0 3.4 multiply_add_fusion.3
  239.3 134.3 %all-reduce.138.cloned.1.call-done = (f32[12,64,128]{2,1,0:T(8,128)}, f32[4,64,128]{2,1,0:T(8,128)}) async-done(((f32[12,64,128]{2,1,0:T(8,128)}, f32[4,64,128]{2,1,0:T(8,128)}), (f32[12,64,128]{2,1,0:T(8,128)}, f32[4,64,128]{2,1,0:T(8,128)})) %all-reduce.138.cloned.1.call-update) | async-done | bytes 524304 | tf_op jit(solution)/shard_map/psum | solution.py:210
  386.7 4.2 reshape.128
  390.8 5.7 fusion.54
  398.4 3.6 collective-permute-start.12
  408.1 4.0 collective-permute-start.14
  412.1 3.3 slice_multiply_fusion.17
  417.4 6.0 pad_subtract_fusion.2
  425.4 4.7 collective-permute-start.16
  436.8 4.6 collective-permute-start.18
  441.3 3.7 reshape.129
  445.1 2.6 reduce_sum.136
  454.0 4.4 multiply_divide_fusion.2
  458.4 3.4 multiply_add_fusion.2
  463.7 130.3 %all-reduce.130.cloned.1.call-done = f32[4,64,128]{2,1,0:T(8,128)} async-done(((f32[4,64,128]{2,1,0:T(8,128)}), f32[4,64,128]{2,1,0:T(8,128)}) %all-reduce.130.cloned.1.call-update) | async-done | bytes 131088 | tf_op jit(solution)/shard_map/psum | solution.py:215
  604.9 4.2 reshape.130
  609.1 6.0 fusion.40
  615.1 2.7 collective-permute-start.21
  617.8 2.8 collective-permute-start.20
  627.3 4.0 collective-permute-start.22
  635.3 5.8 pad_subtract_fusion.1
  643.2 3.8 collective-permute-start.24
  653.6 4.6 collective-permute-start.26
  658.2 3.7 reshape.131
  661.9 2.6 reduce_sum.138
  671.3 4.4 multiply_divide_fusion.1
  675.7 3.4 multiply_add_fusion.1
  681.0 130.4 %all-reduce.132.cloned.1.call-done = f32[4,64,128]{2,1,0:T(8,128)} async-done(((f32[4,64,128]{2,1,0:T(8,128)}), f32[4,64,128]{2,1,0:T(8,128)}) %all-reduce.132.cloned.1.call-update) | async-done | bytes 131088 | tf_op jit(solution)/shard_map/psum | solution.py:215
  822.3 4.2 reshape.132
  826.5 5.9 fusion.25
  832.4 2.7 collective-permute-start.29
  835.1 2.8 collective-permute-start.28
  844.0 4.0 collective-permute-start.30
  848.0 3.3 slice_multiply_fusion.13
  853.3 5.8 pad_subtract_fusion
  861.3 4.6 collective-permute-start.32
  872.4 4.7 collective-permute-start.34
  877.2 3.7 reshape.133
  889.1 4.4 multiply_divide_fusion
  893.5 3.5 multiply_add_fusion
  898.9 130.8 %all-reduce.134.cloned.1.call-done = f32[4,64,128]{2,1,0:T(8,128)} async-done(((f32[4,64,128]{2,1,0:T(8,128)}), f32[4,64,128]{2,1,0:T(8,128)}) %all-reduce.134.cloned.1.call-update) | async-done | bytes 131088 | tf_op jit(solution)/shard_map/psum | solution.py:215
  1037.5 4.3 reshape.134
  1041.8 6.1 fusion.10
  (340 shorter events, 179.0 us)
Async XLA Ops:
  7.2 22.9 %copy-start.48 = (s32[4,256,256]{2,1,0:T(8,128)S(1)}, s32[4,256,256]{2,1,0:T(8,128)}, u32[]{:S(2)}) copy-start(s32[4,256,256]{2,1,0:T(8,128)} %param.6) | copy-start | bytes 3145732
  7.2 166.7 %all-reduce.136.cloned.1.call-start = ((), (), s32[]{:S(2)}) async-start(), calls=%async_computation.3 | async-start | bytes 1048576
  7.2 55.3 %collective-permute-start.4 = (f32[4,1,256]{2,1,0:T(1,128)S(1)}, f32[4,1,256]{2,1,0:T(1,128)S(1)}, u32[]{:S(2)}, u32[]{:S(2)}) collective-permute-start(f32[4,1,256]{2,1,0:T(1,128)S(1)} %broadcast.359), channel_id=1, source_target_pairs={{0,16},{16,32},{32,48},{48,64},{64,80},{80,96},{96,112},{1,17},{17... | collective-permute-start | bytes 12296 | tf_op jit(solution)/shard_map/ppermute | solution.py:30
  12.0 50.6 %collective-permute-start.5 = (f32[4,1,256]{2,1,0:T(1,128)S(1)}, f32[4,1,256]{2,1,0:T(1,128)S(1)}, u32[]{:S(2)}, u32[]{:S(2)}) collective-permute-start(f32[4,1,256]{2,1,0:T(1,128)S(1)} %broadcast.359), channel_id=1, source_target_pairs={{16,0},{32,16},{48,32},{64,48},{80,64},{96,80},{112,96},{17,1},{33... | collective-permute-start | bytes 12296 | tf_op jit(solution)/shard_map/ppermute | solution.py:32
  26.1 347.4 %all-reduce.138.cloned.1.call-start = ((), (), s32[]{:S(2)}) async-start(), calls=%async_computation.4 | async-start | bytes 1048576 | tf_op jit(solution)/shard_map/psum | solution.py:210
  44.0 42.6 %copy-start.24 = (f32[4,256,256]{2,1,0:T(8,128)}, f32[4,256,256]{2,1,0:T(8,128)S(1)}, u32[]{:S(2)}) copy-start(f32[4,256,256]{2,1,0:T(8,128)S(1)} %get-tuple-element.17) | copy-start | bytes 3145732
  44.0 12.3 %copy-start.37 = (f32[256,256]{1,0:T(8,128)S(1)}, f32[256,256]{1,0:T(8,128)}, u32[]{:S(2)}) copy-start(f32[256,256]{1,0:T(8,128)} %param.8) | copy-start | bytes 786436
  56.3 30.4 %copy-start.23 = (f32[4,256,256]{2,1,0:T(8,128)}, f32[4,256,256]{2,1,0:T(8,128)S(1)}, u32[]{:S(2)}) copy-start(f32[4,256,256]{2,1,0:T(8,128)S(1)} %select_add_fusion) | copy-start | bytes 3145732
  57.0 12.5 %collective-permute-start.1 = (f32[9,3,256]{2,1,0:T(4,128)}, f32[9,3,256]{2,1,0:T(4,128)S(1)}, u32[]{:S(2)}, u32[]{:S(2)}) collective-permute-start(f32[9,3,256]{2,1,0:T(4,128)} %get-tuple-element.45), channel_id=1, source_target_pairs={{16,0},{32,16},{48,32},{64,48},{80,64},{96,80},{112,96},{17,1},{33... | collective-permute-start | bytes 82952 | tf_op jit(solution)/shard_map/ppermute | solution.py:32
  58.9 10.6 %collective-permute-start = (f32[9,3,256]{2,1,0:T(4,128)}, f32[9,3,256]{2,1,0:T(4,128)S(1)}, u32[]{:S(2)}, u32[]{:S(2)}) collective-permute-start(f32[9,3,256]{2,1,0:T(4,128)} %get-tuple-element.44), channel_id=1, source_target_pairs={{0,16},{16,32},{32,48},{48,64},{64,80},{80,96},{96,112},{1,17},{17... | collective-permute-start | bytes 82952 | tf_op jit(solution)/shard_map/ppermute | solution.py:30
  63.9 17.8 %collective-permute-start.7 = (f32[4,258,1]{1,0,2:T(4,128)S(1)}, f32[4,258,1]{1,0,2:T(4,128)S(1)}, u32[]{:S(2)}, u32[]{:S(2)}) collective-permute-start(f32[4,258,1]{1,0,2:T(4,128)S(1)} %copy.14), channel_id=1, source_target_pairs={{1,0},{2,1},{3,2},{4,3},{5,4},{6,5},{7,6},{8,7},{9,8},{10,9},{11,1... | collective-permute-start | bytes 12392 | tf_op jit(solution)/shard_map/ppermute | solution.py:32
  65.5 17.3 %collective-permute-start.6 = (f32[4,258,1]{1,0,2:T(4,128)S(1)}, f32[4,258,1]{1,0,2:T(4,128)S(1)}, u32[]{:S(2)}, u32[]{:S(2)}) collective-permute-start(f32[4,258,1]{1,0,2:T(4,128)S(1)} %copy.12), channel_id=1, source_target_pairs={{0,1},{1,2},{2,3},{3,4},{4,5},{5,6},{6,7},{7,8},{8,9},{9,10},{10,1... | collective-permute-start | bytes 12392 | tf_op jit(solution)/shard_map/ppermute | solution.py:30
  69.5 17.1 %copy-start.50 = (f32[9,3,256]{2,1,0:T(4,128)}, f32[9,3,256]{2,1,0:T(4,128)S(1)}, u32[]{:S(2)}) copy-start(f32[9,3,256]{2,1,0:T(4,128)S(1)} %collective-permute-done) | copy-start | bytes 82948
  73.0 10.8 %collective-permute-start.3 = (f32[9,262,3]{1,2,0:T(4,128)S(1)}, f32[9,262,3]{1,2,0:T(4,128)S(1)}, u32[]{:S(2)}, u32[]{:S(2)}) collective-permute-start(f32[9,262,3]{1,2,0:T(4,128)S(1)} %copy.9), channel_id=1, source_target_pairs={{1,0},{2,1},{3,2},{4,3},{5,4},{6,5},{7,6},{8,7},{9,8},{10,9},{11,1... | collective-permute-start | bytes 84896 | tf_op jit(solution)/shard_map/ppermute | solution.py:32
  75.5 8.8 collective-permute-start.2
  84.2 7.4 copy-start.30
  181.5 6.6 copy-start.42
  182.6 5.5 copy-start.41
  182.6 13.7 %copy-start.40 = (f32[262,262]{1,0:T(8,128)S(1)}, f32[262,262]{1,0:T(8,128)}, u32[]{:S(2)}) copy-start(f32[262,262]{1,0:T(8,128)} %copy-done.39) | copy-start | bytes 823732
  189.6 14.6 %collective-permute-start.9 = (f32[4,2,256]{2,1,0:T(2,128)}, f32[4,2,256]{2,1,0:T(2,128)S(1)}, u32[]{:S(2)}, u32[]{:S(2)}) collective-permute-start(f32[4,2,256]{2,1,0:T(2,128)} %get-tuple-element.85), channel_id=1, source_target_pairs={{16,0},{32,16},{48,32},{64,48},{80,64},{96,80},{112,96},{17,1},{33... | collective-permute-start | bytes 24584 | tf_op jit(solution)/shard_map/ppermute | solution.py:32
  191.6 12.7 %collective-permute-start.8 = (f32[4,2,256]{2,1,0:T(2,128)}, f32[4,2,256]{2,1,0:T(2,128)S(1)}, u32[]{:S(2)}, u32[]{:S(2)}) collective-permute-start(f32[4,2,256]{2,1,0:T(2,128)} %get-tuple-element.84), channel_id=1, source_target_pairs={{0,16},{16,32},{32,48},{48,64},{64,80},{80,96},{96,112},{1,17},{17... | collective-permute-start | bytes 24584 | tf_op jit(solution)/shard_map/ppermute | solution.py:30
  208.0 17.2 %collective-permute-start.11 = (f32[4,260,2]{1,0,2:T(4,128)S(1)}, f32[4,260,2]{1,0,2:T(4,128)S(1)}, u32[]{:S(2)}, u32[]{:S(2)}) collective-permute-start(f32[4,260,2]{1,0,2:T(4,128)S(1)} %copy.17), channel_id=1, source_target_pairs={{1,0},{2,1},{3,2},{4,3},{5,4},{6,5},{7,6},{8,7},{9,8},{10,9},{11,1... | collective-permute-start | bytes 24968 | tf_op jit(solution)/shard_map/ppermute | solution.py:32
  210.7 15.7 %collective-permute-start.10 = (f32[4,260,2]{1,0,2:T(4,128)S(1)}, f32[4,260,2]{1,0,2:T(4,128)S(1)}, u32[]{:S(2)}, u32[]{:S(2)}) collective-permute-start(f32[4,260,2]{1,0,2:T(4,128)S(1)} %copy.16), channel_id=1, source_target_pairs={{0,1},{1,2},{2,3},{3,4},{4,5},{5,6},{6,7},{7,8},{8,9},{9,10},{10,1... | collective-permute-start | bytes 24968 | tf_op jit(solution)/shard_map/ppermute | solution.py:30
  225.2 368.8 %all-reduce.130.cloned.1.call-start = ((), (), s32[]{:S(2)}) async-start(), calls=%async_computation | async-start | bytes 262144 | tf_op jit(solution)/shard_map/psum | solution.py:215
  373.5 4.4 copy-start
  373.5 4.5 copy-start.32
  396.5 7.7 copy-start.16
  396.5 5.6 collective-permute-start.13
  398.4 4.4 collective-permute-start.12
  405.5 9.9 collective-permute-start.15
  408.1 8.3 collective-permute-start.14
  423.4 8.8 copy-start.25
  423.5 6.7 collective-permute-start.17
  425.4 5.5 collective-permute-start.16
  433.5 16.9 %collective-permute-start.19 = (f32[4,260,2]{1,0,2:T(4,128)S(1)}, f32[4,260,2]{1,0,2:T(4,128)}, u32[]{:S(2)}, u32[]{:S(2)}) collective-permute-start(f32[4,260,2]{1,0,2:T(4,128)S(1)} %copy.25), channel_id=1, source_target_pairs={{1,0},{2,1},{3,2},{4,3},{5,4},{6,5},{7,6},{8,7},{9,8},{10,9},{11,1... | collective-permute-start | bytes 24968 | tf_op jit(solution)/shard_map/ppermute | solution.py:32
  436.8 15.4 %collective-permute-start.18 = (f32[4,260,2]{1,0,2:T(4,128)}, f32[4,260,2]{1,0,2:T(4,128)}, u32[]{:S(2)}, u32[]{:S(2)}) collective-permute-start(f32[4,260,2]{1,0,2:T(4,128)} %copy.24), channel_id=1, source_target_pairs={{0,1},{1,2},{2,3},{3,4},{4,5},{5,6},{6,7},{7,8},{8,9},{9,10},{10,1... | collective-permute-start | bytes 24968 | tf_op jit(solution)/shard_map/ppermute | solution.py:30
  450.4 361.0 %all-reduce.132.cloned.1.call-start = ((), (), s32[]{:S(2)}) async-start(), calls=%async_computation.1 | async-start | bytes 262144 | tf_op jit(solution)/shard_map/psum | solution.py:215
  609.1 11.6 %copy-start.12 = (f32[3,262,262]{2,1,0:T(8,128)S(1)}, f32[3,262,262]{2,1,0:T(8,128)}, u32[]{:S(2)}) copy-start(f32[3,262,262]{2,1,0:T(8,128)} %copy-done.9) | copy-start | bytes 2471188
  615.0 7.1 copy-start.15
  615.1 7.1 collective-permute-start.21
  617.8 4.4 collective-permute-start.20
  624.7 8.5 collective-permute-start.23
  627.3 6.9 collective-permute-start.22
  641.1 8.0 copy-start.27
  641.1 5.9 collective-permute-start.25
  643.2 4.6 collective-permute-start.24
  650.4 17.3 %collective-permute-start.27 = (f32[4,260,2]{1,0,2:T(4,128)S(1)}, f32[4,260,2]{1,0,2:T(4,128)}, u32[]{:S(2)}, u32[]{:S(2)}) collective-permute-start(f32[4,260,2]{1,0,2:T(4,128)S(1)} %copy.33), channel_id=1, source_target_pairs={{1,0},{2,1},{3,2},{4,3},{5,4},{6,5},{7,6},{8,7},{9,8},{10,9},{11,1... | collective-permute-start | bytes 24968 | tf_op jit(solution)/shard_map/ppermute | solution.py:32
  653.6 15.8 %collective-permute-start.26 = (f32[4,260,2]{1,0,2:T(4,128)}, f32[4,260,2]{1,0,2:T(4,128)}, u32[]{:S(2)}, u32[]{:S(2)}) collective-permute-start(f32[4,260,2]{1,0,2:T(4,128)} %copy.32), channel_id=1, source_target_pairs={{0,1},{1,2},{2,3},{3,4},{4,5},{5,6},{6,7},{7,8},{8,9},{9,10},{10,1... | collective-permute-start | bytes 24968 | tf_op jit(solution)/shard_map/ppermute | solution.py:30
  667.3 362.5 %all-reduce.134.cloned.1.call-start = ((), (), s32[]{:S(2)}) async-start(), calls=%async_computation.2 | async-start | bytes 262144 | tf_op jit(solution)/shard_map/psum | solution.py:215
  832.4 7.7 copy-start.17
  832.4 5.6 collective-permute-start.29
  835.1 3.6 collective-permute-start.28
  841.4 9.9 collective-permute-start.31
  844.0 8.3 collective-permute-start.30
  859.1 8.8 copy-start.26
  859.2 6.7 collective-permute-start.33
  861.3 5.3 collective-permute-start.32
  869.2 16.3 %collective-permute-start.35 = (f32[4,260,2]{1,0,2:T(4,128)S(1)}, f32[4,260,2]{1,0,2:T(4,128)}, u32[]{:S(2)}, u32[]{:S(2)}) collective-permute-start(f32[4,260,2]{1,0,2:T(4,128)S(1)} %copy.41), channel_id=1, source_target_pairs={{1,0},{2,1},{3,2},{4,3},{5,4},{6,5},{7,6},{8,7},{9,8},{10,9},{11,1... | collective-permute-start | bytes 24968 | tf_op jit(solution)/shard_map/ppermute | solution.py:32
  872.4 14.9 %collective-permute-start.34 = (f32[4,260,2]{1,0,2:T(4,128)}, f32[4,260,2]{1,0,2:T(4,128)}, u32[]{:S(2)}, u32[]{:S(2)}) collective-permute-start(f32[4,260,2]{1,0,2:T(4,128)} %copy.40), channel_id=1, source_target_pairs={{0,1},{1,2},{2,3},{3,4},{4,5},{5,6},{6,7},{7,8},{8,9},{9,10},{10,1... | collective-permute-start | bytes 24968 | tf_op jit(solution)/shard_map/ppermute | solution.py:30
  897.0 132.7 %copy-start.8 = (f32[4,64,128]{2,1,0:T(8,128)S(1)}, f32[4,64,128]{2,1,0:T(8,128)}, u32[]{:S(2)}) copy-start(f32[4,64,128]{2,1,0:T(8,128)} %copy-done.5) | copy-start | bytes 393220
  897.0 132.7 %copy-start.43 = (f32[4,64,128]{2,1,0:T(8,128)S(1)}, f32[4,64,128]{2,1,0:T(8,128)}, u32[]{:S(2)}) copy-start(f32[4,64,128]{2,1,0:T(8,128)} %get-tuple-element.16) | copy-start | bytes 393220
  897.0 133.7 %copy-start.3 = (f32[12,64,128]{2,1,0:T(8,128)S(1)}, f32[12,64,128]{2,1,0:T(8,128)}, u32[]{:S(2)}) copy-start(f32[12,64,128]{2,1,0:T(8,128)} %get-tuple-element.2) | copy-start | bytes 1179652
  1037.5 4.3 copy-start.4
  1037.5 4.3 copy-start.18
  (28 other events, 71.0 us)
Sparse Core Ops, SparseCore 0:
  26.2 147.5 all-reduce.135
  225.3 148.1 all-reduce.137
  450.5 143.4 all-reduce.129
  667.4 143.9 all-reduce.131
  885.7 143.9 all-reduce.133
where the time goes:
time: 1070 us; the launch traced here: 1050 us
  waiting for transfers between devices  591 us (55%)
  other arithmetic  196 us (18%)
  local copies, waits for them, and re-layouts  142 us (13%)
  starting transfers between devices  104 us (10%)
  between operations  20.5 us (2%)
    psum x3, waiting for transfers between devices, collect_residual(): return lax.psum(whole, ('gx', 'gy'))  391 us
    psum x1, waiting for transfers between devices, collect_matrix(): return lax.psum(whole, ('gx', 'gy'))  134 us
    ppermute x18, starting transfers between devices, extended(): lax.ppermute(tail, axis, [(i, (i + 1) % count) for i in range(ends)])  73 us
    unnamed x6, waiting for transfers between devices  61.7 us
    ppermute x18, starting transfers between devices, extended(): lax.ppermute(head, axis, [((i + 1) % count, i) for i in range(ends)])  30.8 us
    add x2, other arithmetic, lookup(): summed + jnp.where(material == number, table_row[number], jnp.float32(0.0))  26.1 us
    add x4, other arithmetic, local(): thermal_rise + subdomain_piece  23.6 us
    sub x4, other arithmetic, residual_of(): thermal_forcing - (diagonal_term * margined_array[:, 1:-1, 1:-1] - couple...  23 us
  transfers between devices with their start and end apart: 41, of which 10 were waited for; matrix products, arithmetic and copies ran while one was open for 19% of the time, Pallas kernels for 0%

commit v1 on v0

v1 whole, which is shorter than its diff:
```python
import functools

import jax
import jax.numpy as jnp
from jax import lax
from jax.experimental import pallas as pl
from jax.experimental.pallas import tpu as pltpu
from jax.sharding import PartitionSpec as P

MESH = pl.DeviceIdType.MESH
F32 = jnp.float32
BF16 = jnp.bfloat16

NL = 4
N = 256
LN = 128
RO = 16
NR = N + 2 * RO
SW = 512
OUTER = 2
INNER = 2
CJ = 8
DAMPING = 0.8
DRAIN_SLOPE = 0.5
FACE_FLOOR = 0.5
BALANCE_WEIGHT = 0.5
DIRS = ((-1, -1), (-1, 0), (-1, 1), (0, -1), (0, 1), (1, -1), (1, 0), (1, 1))
DIAG = tuple(d for d in DIRS if d[0] and d[1])
OFF_LINE = tuple(d for d in DIRS if d[1])


def iota(shape, dim):
    return lax.broadcasted_iota(jnp.int32, shape, dim)


def harmonic(a, b):
    return 2.0 * a * b / jnp.maximum(a + b, FACE_FLOOR)


def shift(x, amount, axis):
    return pltpu.roll(x, amount % x.shape[axis], axis)


def lookup(ids, table):
    level = list(table)
    for bit in range(4):
        odd = ((ids >> bit) & 1) == 1
        level = [jnp.where(odd, level[2 * k + 1], level[2 * k]) for k in range(len(level) // 2)]
    return level[0]


def exact_dot(a, b):
    return lax.dot_general(
        a, b, (((1,), (0,)), ((), ())), precision=lax.Precision.HIGHEST, preferred_element_type=F32
    )


def pieces(x, count):
    out = []
    for _ in range(count - 1):
        part = x.astype(BF16)
        out.append(part)
        x = x - part.astype(F32)
    return out + [x.astype(BF16)]


def pick_dot(x, ones):
    return sum(jnp.dot(part, ones, preferred_element_type=F32) for part in pieces(x, 3))


class Layout:
    def __init__(self):
        self.count = 0

    def take(self):
        self.count += 1
        return self.count - 1


def kernel(nx, ny, *refs):
    (mat, tab, sink, drain, inst_tile, inst_power, out, dyn_out) = refs[:8]
    (
        lat, ver, fr, fc, fv, dg, wg, src, dyn, drn, snk, t_, r_, e1_,
        cf_t, cf_e, cf_f, acc, acc_n, pk, onehot_a, onehot_b, cb, cbn,
        tsum, tin1, tred, tin2,
        sq_row, rq_row, sq_e, rq_we, rq_o,
        cm, cmr, coef, ct, ln, nb, s2, ls2, cv, xt,
        st_row, rt_row, es, rt_we, rt_d,
        ssem, rsem,
    ) = refs[8:]
    mx, my = lax.axis_index("gx"), lax.axis_index("gy")

    def at(dx, dy):
        return {"gx": lax.rem(mx + (dx + nx), nx), "gy": lax.rem(my + (dy + ny), ny)}

    partners = [(d, 0) for d in range(1, nx)] + [(0, d) for d in range(1, ny)] + list(DIAG)
    barrier = pltpu.get_barrier_semaphore()
    for d in partners:
        pl.semaphore_signal(barrier, inc=1, device_id=at(*d), device_id_type=MESH)

    numbers = Layout()
    started = []

    def send(a, b, to):
        k = numbers.take()
        copy = pltpu.make_async_remote_copy(
            src_ref=a, dst_ref=b, send_sem=ssem.at[k], recv_sem=rsem.at[k],
            device_id=at(*to), device_id_type=MESH,
        )
        copy.start()
        started.append(copy)
        return copy

    lane8 = iota((8, LN), 1)
    first_lane = lane8 == 0
    last_lane = lane8 == LN - 1
    low_half = lane8 < LN // 2

    cols_all, rows_all = 32 * ny, 32 * nx
    n_inst = inst_tile.shape[0] * LN
    sub_c = iota((cols_all, LN), 0)
    sub_r = iota((rows_all, LN), 0)
    for k in range(n_inst // LN):
        t = inst_tile[k : k + 1, :]
        s = t >> 10
        row = (s // ny) * 32 + ((t >> 5) & 31)
        col = (s % ny) * 32 + (t & 31)
        span = slice(k * LN, (k + 1) * LN)
        onehot_a[:, span] = jnp.where(sub_c == col, 1.0, 0.0).astype(BF16)
        hit = sub_r == row
        for q, part in enumerate(pieces(inst_power[k : k + 1, :], 3)):
            onehot_b[q, :, span] = jnp.where(hit, part.astype(F32), 0.0).astype(BF16)
    total = None
    for q in range(3):
        term = lax.dot_general(
            onehot_a[...], onehot_b[q], (((1,), (1,)), ((), ())), preferred_element_type=F32
        )
        total = term if total is None else total + term
    tsum[0:8, :] = jnp.zeros((8, rows_all), F32)
    tsum[8 : 8 + cols_all, :] = total
    tsum[8 + cols_all :, :] = jnp.zeros((8, rows_all), F32)

    def window(j):
        return tsum.at[pl.ds(pl.multiple_of(j * 32, 32), 48), :]

    def pack(values):
        packed = jnp.zeros((8, LN), F32)
        for q, (a, b) in enumerate(values):
            both = shift(jnp.where(low_half, a, b), -(4 * q + 2), 1)
            mine = (lane8 >= 124 - 4 * q) & (lane8 < 128 - 4 * q)
            packed = jnp.where(mine, both, packed)
        return packed

    halves = (slice(0, LN), slice(LN, N))

    def raw(rows):
        mats = [tuple(mat[l, rows, h].astype(F32) for h in halves) for l in range(NL)]
        return mats + [tuple(a[rows, h] for h in halves) for a in (sink, drain)]

    @pl.loop(0, N // 8)
    def _(k):
        rows = pl.ds(pl.multiple_of(k * 8, 8), 8)
        pk[rows, :] = pack(raw(rows))

    for k in range(2):
        sq_e[:, k * LN : (k + 1) * LN] = pk[k * LN : (k + 1) * LN, :].T[104:128, :]
    for side, rows in enumerate((slice(0, 8), slice(N - 8, N))):
        for q, (a, b) in enumerate(raw(rows)):
            sq_row[side, q, 0] = a
            sq_row[side, q, 1] = b

    pl.semaphore_wait(barrier, len(partners))

    tile_in = []
    for d in range(1, ny):
        j = lax.rem(my + d, ny)
        tile_in.append(send(window(j), tin1.at[d - 1], (0, d)))
    margin_row = [send(sq_row.at[s], rq_row.at[s], (2 * s - 1, 0)) for s in range(2)]
    margin_we = [send(sq_e, rq_we.at[s], (0, 2 * s - 1)) for s in range(2)]
    margin_o = {}
    for k, d in enumerate([(-1, 0), (1, 0)] + list(DIAG)):
        half = 0 if d[0] < 0 else 1
        margin_o[d] = (k, send(sq_e.at[:, pl.ds(half * LN, LN)], rq_o.at[k], d))

    col_n = iota((LN, LN), 1)
    row_n = iota((LN, LN), 0)
    for l in range(NL):
        for h in range(2):
            span = pl.ds((2 * l + h) * LN, LN)
            goal = l * 32 + 8 + h * 4 + (row_n >> 5)
            cb[span, :] = jnp.where(col_n == goal, 1.0, 0.0).astype(BF16)
            hit = ((row_n & 31) == 31) & (col_n == goal)
            if h == 0:
                hit = hit | ((row_n == 0) & (col_n == l * 32 + 7))
            cbn[span, :] = jnp.where(hit, 1.0, 0.0).astype(BF16)
    table = [[tab[q, k] for k in range(16)] for q in range(2)]

    zero8 = jnp.zeros((8, LN), F32)
    for ref, places in ((t_, (0, NR - 8)), (fr, (0,)), (lat, (NR - 8,))):
        for l in range(NL):
            for h in range(2):
                for place in places:
                    ref[l, h, place : place + 8, :] = zero8

    @pl.loop(0, N // 8)
    def _(k):
        rows = pl.ds(pl.multiple_of(k * 8, 8), 8)
        into = pl.ds(pl.multiple_of(k * 8 + RO, 8), 8)
        for h in range(2):
            for l in range(NL):
                ids = mat[l, rows, halves[h]]
                lat[l, h, into, :] = lookup(ids, table[0])
                ver[l, h, into, :] = lookup(ids, table[1])
            snk[h, into, :] = sink[rows, halves[h]]
            drn[h, into, :] = drain[rows, halves[h]]

    total = window(my)[...]
    for d in range(1, ny):
        tile_in[d - 1].wait_recv()
        total = total + tin1[d - 1]
    for x in range(nx):
        tred[x] = shift(total, -(32 * x - 1), 1)[:, :LN]
    tile_in2 = []
    for d in range(1, nx):
        x = lax.rem(mx + d, nx)
        tile_in2.append(send(tred.at[x], tin2.at[d - 1], (d, 0)))

    edge_n = jnp.where(mx == 0, 0.0, 1.0)
    edge_s = jnp.where(mx == nx - 1, 0.0, 1.0)
    edge_w = jnp.where(my == 0, 0.0, 1.0)
    edge_e = jnp.where(my == ny - 1, 0.0, 1.0)
    for c in margin_row:
        c.wait_recv()
    for slot, base, keep in ((1, RO - 8, edge_n), (0, RO + N, edge_s)):
        rows = slice(base, base + 8)
        for h in range(2):
            for l in range(NL):
                ids = rq_row[slot, l, h].astype(jnp.int32)
                lat[l, h, rows, :] = lookup(ids, table[0]) * keep
                ver[l, h, rows, :] = lookup(ids, table[1]) * keep
            snk[h, rows, :] = rq_row[slot, 4, h] * keep
            drn[h, rows, :] = rq_row[slot, 5, h] * keep
    for c in margin_we:
        c.wait_recv()
    for _, c in margin_o.values():
        c.wait_recv()

    def from_dir(d):
        return rq_o[margin_o[(-d[0], -d[1])][0]]

    west = jnp.concatenate([from_dir((-1, -1)), rq_we[1], from_dir((1, -1))], axis=1)
    east = jnp.concatenate([from_dir((-1, 1)), rq_we[0], from_dir((1, 1))], axis=1)
    inner = jnp.concatenate([from_dir((-1, 0)), sq_e[...], from_dir((1, 0))], axis=1)
    c24 = iota((24, SW), 0) & 3
    outer = jnp.where(c24 < 2, west, east)
    strip_lane = iota((16, SW), 1)
    c16 = iota((16, SW), 0) & 3
    one = jnp.ones((16, SW), F32)
    keep_rows = jnp.where(strip_lane < LN, one * edge_n, jnp.where(strip_lane >= LN + N, one * edge_s, one))
    keep_outer = keep_rows * jnp.where(c16 < 2, one * edge_w, one * edge_e)
    sm_ids = outer[8:24, :].astype(jnp.int32)
    se_ids = inner[8:24, :].astype(jnp.int32)
    lat_m = lookup(sm_ids, table[0]) * keep_outer
    ver_m = lookup(sm_ids, table[1]) * keep_outer
    lat_e = lookup(se_ids, table[0]) * keep_rows
    row8 = iota((8, SW), 0)
    zero_s = jnp.zeros((8, SW), F32)
    mixed = shift(outer[0:8, :], 4, 0)
    sink_s = jnp.concatenate([jnp.where(row8 < 4, mixed, 0.0), zero_s], axis=0)
    drain_s = jnp.concatenate([zero_s, jnp.where(row8 >= 4, mixed, 0.0)], axis=0)

    def from_outside(x):
        return jnp.where(c16 == 1, shift(x, 1, 0), shift(x, -1, 0))

    def from_inside(x):
        return jnp.where(c16 == 1, shift(x, -1, 0), shift(x, 1, 0))

    fs_out = harmonic(lat_m, from_outside(lat_m))
    fs_in = harmonic(lat_m, from_inside(lat_e))
    fs_row = harmonic(lat_m, shift(lat_m, -1, 1))
    fs_row_prev = shift(fs_row, 1, 1)
    layer_rows = iota((16, SW), 0)
    fs_ver = jnp.where(layer_rows >= 4, harmonic(ver_m, shift(ver_m, 4, 0)), 0.0)
    fs_ver_prev = shift(fs_ver, -4, 0)
    d_s = jnp.maximum(fs_out + fs_in + fs_row + fs_row_prev + fs_ver + fs_ver_prev + sink_s, FACE_FLOOR)
    w_s = DAMPING / d_s

    def column_form(x, ref):
        x = jnp.where(c16 == 1, shift(x, -1, 0), jnp.where(c16 == 2, shift(x, 1, 0), 0.0))
        for k in range(SW // LN):
            block = jnp.concatenate(
                [x[:, k * LN : (k + 1) * LN], jnp.zeros((LN - 16, LN), F32)], axis=0
            )
            ref[k * LN : (k + 1) * LN, :] = block.T

    def columns(ref, base):
        tile = ref[pl.ds(base + (LN - RO), 8), :]
        return [shift(tile, 114 + 4 * l, 1) for l in range(NL)]

    column_form(fs_in, cf_f)

    def faces(base, sums):
        bf = columns(cf_f, base)
        here, below = pl.ds(base, 8), pl.ds(base + 1, 8)
        vs = [[ver[l, h, here, :] for h in range(2)] for l in range(NL)]
        for l in range(NL):
            a0, a1 = lat[l, 0, here, :], lat[l, 1, here, :]
            ra0, ra1 = shift(a0, -1, 1), shift(a1, -1, 1)
            c0 = harmonic(a0, jnp.where(last_lane, ra1, ra0))
            c1 = jnp.where(last_lane, bf[l], harmonic(a1, ra1))
            fc[l, 0, here, :] = c0
            fc[l, 1, here, :] = c1
            for h, a in ((0, a0), (1, a1)):
                fr[l, h, here, :] = harmonic(a, lat[l, h, below, :])
            if sums is not None:
                sums[0][2 * l] += jnp.where(first_lane, bf[l], c0)
                sums[0][2 * l + 1] += c1
            for h in range(2):
                if l < NL - 1:
                    v = harmonic(vs[l][h], vs[l + 1][h])
                    fv[l, h, here, :] = v
                else:
                    v = snk[h, here, :]
                if sums is not None:
                    sums[1][2 * l + h] += v

    faces(RO - 8, None)
    faces(RO + N, None)

    @pl.loop(0, N // 32)
    def _(a):
        sums = [[zero8] * 8, [zero8] * 8]
        for k in range(4):
            faces(pl.multiple_of(RO + 32 * a + 8 * k, 8), sums)
        rows = pl.ds(pl.multiple_of(a * 8, 8), 8)
        for q in range(8):
            acc_n[rows, q * LN : (q + 1) * LN] = sums[0][q]
            acc[rows, q * LN : (q + 1) * LN] = sums[1][q]

    @pl.loop(0, N // 8 + 2)
    def _(k):
        base = pl.multiple_of(RO - 8 + 8 * k, 8)
        here, above = pl.ds(base, 8), pl.ds(base - 1, 8)
        bf = columns(cf_f, base)
        for l in range(NL):
            c0, c1 = fc[l, 0, here, :], fc[l, 1, here, :]
            rc0, rc1 = shift(c0, 1, 1), shift(c1, 1, 1)
            west_face = (jnp.where(first_lane, bf[l], rc0), jnp.where(first_lane, rc0, rc1))
            for h, c in ((0, c0), (1, c1)):
                d = fr[l, h, above, :] + fr[l, h, here, :] + west_face[h] + c
                if l > 0:
                    d = d + fv[l - 1, h, here, :]
                if l < NL - 1:
                    d = d + fv[l, h, here, :]
                else:
                    d = d + snk[h, here, :]
                d = jnp.maximum(d, FACE_FLOOR)
                dg[l, h, here, :] = d
                wg[l, h, here, :] = DAMPING / d

    block_lane = lane8 & 31
    own_block = (block_lane >= 8) & (block_lane < 16)

    def block_rows(x):
        return x.reshape(8, 8, LN).sum(axis=1)

    def edge_sums(start):
        rows = [fr[l, h, pl.ds(start, 8, stride=32), :] for l in range(NL) for h in range(2)]
        return pick_dot(jnp.concatenate(rows, axis=1), cb[...])

    c_east = edge_sums(RO + 31)
    c_east_prev = edge_sums(RO - 1)
    c_north_wide = block_rows(pick_dot(acc_n[...], cbn[...]))
    c_north = jnp.where(own_block, c_north_wide, 0.0)
    c_north_prev = jnp.where(own_block, shift(c_north_wide, 1, 1), 0.0)
    up_sink = block_rows(pick_dot(acc[...], cb[...]))
    c_up = jnp.where(lane8 < 96, up_sink, 0.0)
    c_sink = jnp.where(lane8 >= 96, up_sink, 0.0)
    c_diag = c_east + c_east_prev + c_north + c_north_prev + c_up + shift(c_up, 32, 1) + c_sink
    for q, x in enumerate((c_east, c_north, c_up, c_diag)):
        cm[q] = x
    ct[0, 1] = c_diag
    cm_in = {d: (k, send(cm, cmr.at[k], d)) for k, d in enumerate(DIRS)}

    total = tred[mx]
    for d in range(1, nx):
        tile_in2[d - 1].wait_recv()
        total = total + tin2[d - 1]
    total = total * (1.0 / 64.0)
    wide = jnp.concatenate([total, jnp.zeros((LN - 48, LN), F32)], axis=0)
    to_rows = jnp.where(iota((LN, SW), 0) == ((iota((LN, SW), 1) - 120) >> 3), 1.0, 0.0)
    dyn_t = exact_dot(wide[:48, :], to_rows)
    dyn_s = jnp.where(layer_rows == 13, dyn_t[7:8, :], jnp.where(layer_rows == 14, dyn_t[40:41, :], 0.0))
    spread_rows = jnp.where(iota((NR, LN), 1) == ((iota((NR, LN), 0) - 8) >> 3), 1.0, 0.0)
    spread_cols = jnp.where(iota((LN, N), 0) == (iota((LN, N), 1) >> 3) + 8, 1.0, 0.0)
    dyn_all = exact_dot(exact_dot(spread_rows, wide.T), spread_cols)
    for h in range(2):
        dyn[h] = dyn_all[:, halves[h]]
    dyn_out[...] = dyn_all[RO : RO + N, :]

    for _, c in cm_in.values():
        c.wait_recv()

    def assemble(own, other):
        rows = []
        for dx in (-1, 0, 1):
            centre = own if dx == 0 else other((dx, 0))
            rows.append(centre + shift(other((dx, -1)), -8, 1) + shift(other((dx, 1)), 8, 1))
        return jnp.concatenate(rows, axis=0)

    w_east, w_north, w_up, w_diag = (
        assemble(cm[q], lambda d, q=q: cmr[cm_in[(-d[0], -d[1])][0], q]) for q in range(4)
    )
    gain = jnp.where((iota((24, LN), 1) & 31) < 24, DAMPING / jnp.maximum(w_diag, 1e-30), 0.0)
    coef[0] = gain
    coef[1] = gain * w_east
    coef[2] = gain * shift(w_east, 1, 0)
    coef[3] = gain * w_north
    coef[4] = gain * shift(w_north, 1, 1)
    coef[5] = gain * w_up
    coef[6] = gain * shift(w_up, 32, 1)

    def couple(ref, base, edge, live):
        here, above, below = pl.ds(base, 8), pl.ds(base - 1, 8), pl.ds(base + 1, 8)
        res = [[None, None] for _ in range(NL)]
        mid = [[ref[l, h, here, :] for h in range(2)] for l in range(live)]
        for l in range(live):
            a0, a1 = mid[l]
            f0, f1 = fc[l, 0, here, :], fc[l, 1, here, :]
            ra0, ra1 = shift(a0, -1, 1), shift(a1, -1, 1)
            p0, p1 = shift(f0 * a0, 1, 1), shift(f1 * a1, 1, 1)
            lateral = (
                f0 * jnp.where(last_lane, ra1, ra0) + jnp.where(first_lane, edge[l], p0),
                jnp.where(last_lane, edge[l], f1 * ra1) + jnp.where(first_lane, p0, p1),
            )
            for h in range(2):
                res[l][h] = (
                    lateral[h]
                    + fr[l, h, above, :] * ref[l, h, above, :]
                    + fr[l, h, here, :] * ref[l, h, below, :]
                )
        for l in range(live):
            for h in range(2):
                for face, to in ((l - 1, l - 1), (l, l + 1)):
                    if 0 <= to < NL:
                        term = fv[face, h, here, :] * mid[l][h]
                        res[to][h] = term if res[to][h] is None else res[to][h] + term
        return mid, res

    strip_top = layer_rows >= 12

    def source_strip(tm):
        return jnp.where(strip_top, dyn_s + drain_s * jnp.exp(DRAIN_SLOPE * jnp.where(strip_top, tm, 0.0)), 0.0)

    tm = te = source_s = None
    sweeps = OUTER * INNER
    for it in range(sweeps):
        first, last = it == 0, it == sweeps - 1
        fresh = it % INNER == 0
        if fresh:
            source_s = dyn_s + drain_s if first else source_strip(tm)
        if first:
            r_s = source_s
        else:
            r_s = source_s - (
                d_s * tm
                - fs_out * from_outside(tm)
                - fs_in * from_inside(te)
                - fs_row * shift(tm, -1, 1)
                - fs_row_prev * shift(tm, 1, 1)
                - fs_ver * shift(tm, 4, 0)
                - fs_ver_prev * shift(tm, -4, 0)
            )
            column_form(fs_in * tm, cf_t)
        column_form(fs_in * (w_s * r_s), cf_e)

        def residual(base, sums):
            here = pl.ds(base, 8)
            if first:
                for h in range(2):
                    r = dyn[h, here, :] + drn[h, here, :]
                    src[h, here, :] = r
                    r_[0, h, here, :] = r
                    e1_[0, h, here, :] = wg[0, h, here, :] * r
                    if sums is not None:
                        sums[h] += r
                return
            mid, res = couple(t_, base, columns(cf_t, base), NL)
            for l in range(NL):
                for h in range(2):
                    r = res[l][h] - dg[l, h, here, :] * mid[l][h]
                    if l == 0:
                        if fresh:
                            s = dyn[h, here, :] + drn[h, here, :] * jnp.exp(DRAIN_SLOPE * mid[0][h])
                            src[h, here, :] = s
                        else:
                            s = src[h, here, :]
                        r = r + s
                    r_[l, h, here, :] = r
                    e1_[l, h, here, :] = wg[l, h, here, :] * r
                    if sums is not None:
                        sums[2 * l + h] += r

        residual(RO - 8, None)
        residual(RO + N, None)

        @pl.loop(0, N // 32)
        def _(a):
            sums = [zero8] * 8
            for k in range(4):
                residual(pl.multiple_of(RO + 32 * a + 8 * k, 8), sums)
            rows = pl.ds(pl.multiple_of(a * 8, 8), 8)
            for q in range(8):
                acc[rows, q * LN : (q + 1) * LN] = sums[q]

        own_c = block_rows(pick_dot(acc[...], cb[...]))
        ct[it, 0] = own_c
        parts = 2 if first else 1
        line = [
            send(ct.at[it, pl.ds(0, parts)], ln.at[it, d - 1, pl.ds(0, parts)], (d, 0)) for d in range(1, nx)
        ]
        side = {
            d: (k, send(ct.at[it, 0], nb.at[it, k], d)) for k, d in enumerate(OFF_LINE)
        }

        live = 1 if first else NL

        @pl.loop(0, N // 8)
        def _(k):
            base = pl.multiple_of(RO + 8 * k, 8)
            here = pl.ds(base, 8)
            mid, res = couple(e1_, base, columns(cf_e, base), live)
            tops = []
            for l in range(NL):
                pair = []
                for h in range(2):
                    u = None
                    if l < live:
                        u = (1.0 - DAMPING) * mid[l][h] + wg[l, h, here, :] * (r_[l, h, here, :] + res[l][h])
                    elif res[l][h] is not None:
                        u = wg[l, h, here, :] * res[l][h]
                    else:
                        u = zero8
                    if not first:
                        u = u + t_[l, h, here, :]
                    t_[l, h, here, :] = u
                    pair.append(u)
                tops.append(tuple(pair))
            if not last:
                pk[pl.ds(pl.multiple_of(8 * k, 8), 8), :] = pack(tops)

        if not last:
            for k in range(2):
                es[it, :, k * LN : (k + 1) * LN] = pk[k * LN : (k + 1) * LN, :].T[112:128, :]
            for s, base in enumerate((RO, RO + N - 8)):
                for l in range(NL):
                    for h in range(2):
                        st_row[it, s, l, h] = t_[l, h, base : base + 8, :]
            row_in = [send(st_row.at[it, s], rt_row.at[it, s], (2 * s - 1, 0)) for s in range(2)]
            we_in = [send(es.at[it], rt_we.at[it, s], (0, 2 * s - 1)) for s in range(2)]
            diag_in = {}
            for k, d in enumerate(DIAG):
                half = 0 if d[0] < 0 else 1
                diag_in[d] = (k, send(es.at[it, :, pl.ds(half * LN, LN)], rt_d.at[it, k], d))

        total = [ct[it, q] for q in range(parts)]
        for d in range(1, nx):
            line[d - 1].wait_recv()
            for q in range(parts):
                total[q] = total[q] + ln[it, d - 1, q]
        sub8 = iota((8, LN), 0)
        packed = jnp.where(sub8 == 0, total[0].sum(axis=0, keepdims=True), 0.0)
        if first:
            packed = jnp.where(sub8 == 1, total[1].sum(axis=0, keepdims=True), packed)
        s2[it] = packed
        gather = [send(s2.at[it], ls2.at[it, d - 1], (0, d)) for d in range(1, ny)]
        for _, c in side.values():
            c.wait_recv()

        def other(d):
            if d[1] == 0:
                return ln[it, 0 if d[0] < 0 else nx - 2, 0]
            return nb[it, side[(-d[0], -d[1])][0]]

        rw = coef[0] * assemble(own_c, other)
        x = rw
        for _ in range(CJ - 1):
            x = (
                (1.0 - DAMPING) * x + rw
                + coef[1] * shift(x, -1, 0) + coef[2] * shift(x, 1, 0)
                + coef[3] * shift(x, -1, 1) + coef[4] * shift(x, 1, 1)
                + coef[5] * shift(x, -32, 1) + coef[6] * shift(x, 32, 1)
            )
        total = packed
        for d in range(1, ny):
            gather[d - 1].wait_recv()
            total = total + ls2[it, d - 1]
        sums = total.sum(axis=1, keepdims=True)
        if first:
            diag_total = sums[1:2, :]
        x = x + BALANCE_WEIGHT * sums[0:1, :] / diag_total

        lane24 = iota((24, LN), 1)
        for l in range(NL):
            for h in range(2):
                cv[l, h] = jnp.take_along_axis(x, l * 32 + 8 + h * 4 + (lane24 >> 5), axis=1)

        if last:
            @pl.loop(0, N // 32)
            def _(a):
                for l in range(NL):
                    for h in range(2):
                        add = cv[l, h, pl.ds(8 + a, 1), :]
                        for k in range(4):
                            rows = pl.ds(pl.multiple_of(32 * a + 8 * k, 8), 8)
                            here = pl.ds(pl.multiple_of(RO + 32 * a + 8 * k, 8), 8)
                            out[l, rows, halves[h]] = t_[l, h, here, :] + add
            break

        @pl.loop(0, N // 32)
        def _(a):
            for l in range(NL):
                for h in range(2):
                    add = cv[l, h, pl.ds(8 + a, 1), :]
                    for k in range(4):
                        here = pl.ds(pl.multiple_of(RO + 32 * a + 8 * k, 8), 8)
                        t_[l, h, here, :] = t_[l, h, here, :] + add

        xt[...] = jnp.concatenate([x, jnp.zeros((LN - 24, LN), F32)], axis=0).T
        row16 = iota((16, LN), 0)
        ring = jnp.zeros((16, LN), F32)
        own_v = ring
        for l in range(NL):
            for pair in range(2):
                mine = (row16 >> 1) == 2 * (NL - 1 - l) + pair
                ring = jnp.where(mine, xt[l * 32 + (7, 16)[pair] : l * 32 + (7, 16)[pair] + 1, :], ring)
                own_v = jnp.where(mine, xt[l * 32 + (15, 8)[pair] : l * 32 + (15, 8)[pair] + 1, :], own_v)
        lane16 = iota((16, LN), 1)

        def along(v):
            return jnp.concatenate(
                [jnp.take_along_axis(v, 4 + 4 * k + (lane16 >> 5), axis=1) for k in range(SW // LN)], axis=1
            )

        for c in row_in:
            c.wait_recv()
        for slot, base, at_row in ((1, RO - 8, 7), (0, RO + N, 16)):
            for l in range(NL):
                for h in range(2):
                    t_[l, h, base : base + 8, :] = rt_row[it, slot, l, h] + cv[l, h, at_row : at_row + 1, :]
        for c in we_in:
            c.wait_recv()
        for _, c in diag_in.values():
            c.wait_recv()

        def corner(d):
            return rt_d[it, diag_in[(-d[0], -d[1])][0]]

        west = jnp.concatenate([corner((-1, -1)), rt_we[it, 1], corner((1, -1))], axis=1)
        east = jnp.concatenate([corner((-1, 1)), rt_we[it, 0], corner((1, 1))], axis=1)
        tm = jnp.where(c16 < 2, west, east) + along(ring)
        blank = jnp.zeros((16, LN), F32)
        te = jnp.concatenate([blank, es[it], blank], axis=1) + along(own_v)

    for c in started:
        c.wait_send()


def n_copies(nx, ny):
    setup = (ny - 1) + 2 + 2 + 6 + (nx - 1) + 8
    each = (nx - 1) + 6 + (ny - 1)
    return setup + OUTER * INNER * each + (OUTER * INNER - 1) * 8


def solution(mesh):
    nx, ny = mesh.shape["gx"], mesh.shape["gy"]
    its = OUTER * INNER

    def step(material, material_table, sink_cond, drain_current, instance_tile, instance_power):
        n_inst = instance_tile.shape[0]
        field = pltpu.VMEM((NL, 2, NR, LN), F32)
        single = pltpu.VMEM((2, NR, LN), F32)
        vm = lambda *shape: pltpu.VMEM(shape, F32)
        copies = n_copies(nx, ny)
        scratch = [
            field, field, field, field, pltpu.VMEM((NL - 1, 2, NR, LN), F32), field, field,
            single, single, single, single, field, field, field,
            vm(SW, LN), vm(SW, LN), vm(SW, LN), vm(64, 8 * LN), vm(64, 8 * LN), vm(N, LN),
            pltpu.VMEM((32 * ny, n_inst), BF16), pltpu.VMEM((3, 32 * nx, n_inst), BF16),
            pltpu.VMEM((8 * LN, LN), BF16), pltpu.VMEM((8 * LN, LN), BF16),
            vm(32 * ny + 16, 32 * nx), vm(ny - 1, 48, 32 * nx), vm(nx, 48, LN), vm(nx - 1, 48, LN),
            vm(2, 6, 2, 8, LN), vm(2, 6, 2, 8, LN), vm(24, N), vm(2, 24, N), vm(6, 24, LN),
            vm(4, 8, LN), vm(8, 4, 8, LN), vm(7, 24, LN), vm(its, 2, 8, LN), vm(its, nx - 1, 2, 8, LN),
            vm(its, 6, 8, LN), vm(its, 8, LN), vm(its, ny - 1, 8, LN), vm(NL, 2, 24, LN), vm(LN, LN),
            vm(its - 1, 2, NL, 2, 8, LN), vm(its - 1, 2, NL, 2, 8, LN),
            vm(its - 1, 16, N), vm(its - 1, 2, 16, N), vm(its - 1, 4, 16, LN),
            pltpu.SemaphoreType.DMA((copies,)), pltpu.SemaphoreType.DMA((copies,)),
        ]
        vmem = pl.BlockSpec(memory_space=pltpu.VMEM)
        smem = pl.BlockSpec(memory_space=pltpu.SMEM)
        return pl.pallas_call(
            functools.partial(kernel, nx, ny),
            out_shape=(
                jax.ShapeDtypeStruct((NL, N, N), F32),
                jax.ShapeDtypeStruct((N, N), F32),
            ),
            in_specs=[vmem, smem, vmem, vmem, vmem, vmem],
            out_specs=(vmem, vmem),
            scratch_shapes=scratch,
            compiler_params=pltpu.CompilerParams(
                collective_id=0, has_side_effects=True, vmem_limit_bytes=56 * 1024 * 1024
            ),
        )(
            material,
            material_table,
            sink_cond,
            drain_current,
            instance_tile.reshape(n_inst // LN, LN),
            instance_power.reshape(n_inst // LN, LN),
        )

    return jax.shard_map(
        step,
        mesh=mesh,
        in_specs=(
            P(None, "gx", "gy"),
            P(),
            P("gx", "gy"),
            P("gx", "gy"),
            P(("gx", "gy")),
            P(("gx", "gy")),
        ),
        out_specs=(P(None, "gx", "gy"), P("gx", "gy")),
        check_vma=False,
    )
```

time: 1070 us -> 93 us (0.09); the launches traced: 1050 us -> 92.8 us
  waiting for transfers between devices: 591 us -> 0 us
  other arithmetic: 196 us -> 0 us
  local copies, waits for them, and re-layouts: 142 us -> 3.03 us
  starting transfers between devices: 104 us -> 0 us
  Pallas kernels: 0 us -> 89.1 us
  between operations: 20.5 us -> 0.65 us
    psum x4 -> x0, waiting for transfers between devices: 526 us -> none  [the longest x3 391 us: collect_residual(): return lax.psum(whole, ('gx', 'gy'))]
    ppermute x36 -> x0, starting transfers between devices: 104 us -> none  [the longest x18 73 us: extended(): lax.ppermute(tail, axis, [(i, (i + 1) % count) for i in range(ends)])]
    pallas_call x0 -> x1, Pallas kernels: none -> 89.1 us  [step(): pl.pallas_call(functools.partial(kernel, nx, ny), out_shape=(jax.ShapeDty...]
    add x38 -> x0, other arithmetic: 75.4 us -> none  [the longest x2 26.1 us: lookup(): summed + jnp.where(material == number, table_row[number], jnp.float32(0.0))]
    unnamed x6 -> x0, waiting for transfers between devices: 61.7 us -> none
    reshape x13 -> x0, local copies, waits for them, and re-layouts: 47.8 us -> none  [the longest x5 21.1 us: distribute(): expanded.reshape(leading + (overall_height * row_rep, width_cells * col_r...]
    slice x43 -> x0, local copies, waits for them, and re-layouts: 44.1 us -> none  [the longest x25 23 us: extended(): lax.slice_in_dim(cells, cells.shape[dim] - width, cells.shape[dim], axis=...]
    div x12 -> x0, other arithmetic: 25.8 us -> none  [the longest x4 19.9 us: smooth(): DAMPING * (residual + couple(margined_array, coeffs)) / diagonal_term]
  transfers between devices with their start and end apart: 41 -> 0, of which waited for: 10 -> 0; matrix products, arithmetic and copies ran while one was open for 19% -> 0% of each run, Pallas kernels for 0% -> 0%
where the time goes in v1:
time: 93 us; the launch traced here: 92.8 us
  Pallas kernels  89.1 us (96%)
  local copies, waits for them, and re-layouts  3.03 us (3%)
    pallas_call x1, Pallas kernels, step(): pl.pallas_call(functools.partial(kernel, nx, ny), out_shape=(jax.ShapeDty...  89.1 us
    unnamed x4, local copies, waits for them, and re-layouts  3.03 us

profile of v1, /device:TPU:1, one launch (start us, length us, event | category | flops | bytes accessed | tf_op | source)
XLA Modules:
  0.0 92.8 jit_solution(14079803799456458180)
XLA Ops:
  0.6 89.1 %shard_map.77 = (f32[4,256,256]{2,1,0:T(8,128)}, f32[256,256]{1,0:T(8,128)}) custom-call(s32[4,256,256]{2,1,0:T(8,128)} %refs_0_.1, f32[2,16]{1,0:T(2,128)} %refs_1_.1, f32[256,256]{1,0:T(8,128)} %refs_2_.1, f32[256,256]{1,0:T(8,128)} %refs_3_.1, s32[16,128]{1,0:T(8,128)} %bitcast.2, f32[16,128]{1,0:T(8,128)} %bitcast.3), custom_call_target="tpu_custom_call" | custom-call | tf_op jit(solution)/shard_map/pallas_call | solution.py:701
  89.7 0.0 copy-start
  89.8 2.3 %copy.10 = f32[4,256,256]{2,1,0:T(8,128)} copy(f32[4,256,256]{2,1,0:T(8,128)} %get-tuple-element.4) | data formatting | bytes 2097152
  92.1 0.0 copy-done
  92.1 0.7 copy.11
Async XLA Ops:
  89.7 2.3 %copy-start = (f32[256,256]{1,0:T(8,128)S(1)}, f32[256,256]{1,0:T(8,128)}, u32[]{:S(2)}) copy-start(f32[256,256]{1,0:T(8,128)} %get-tuple-element.5) | copy-start | bytes 786436

commit v2 on v1

--- a/solution.py
+++ b/solution.py
@@ -78,15 +78,16 @@
 
 
 def kernel(nx, ny, *refs):
-    (mat, tab, sink, drain, inst_tile, inst_power, out, dyn_out) = refs[:8]
+    (mat_hbm, tab, sink_hbm, drain_hbm, inst_tile, inst_power, out_hbm, dyn_hbm) = refs[:8]
     (
-        lat, ver, fr, fc, fv, dg, wg, src, dyn, drn, snk, t_, r_, e1_,
-        cf_t, cf_e, cf_f, acc, acc_n, pk, onehot_a, onehot_b, cb, cbn,
-        tsum, tin1, tred, tin2,
+        mat, sink, drain, out, dyn_out,
+        lat, ver, fr, fc, fv, dg, wg, src, drn, snk, t_, r_, e1_,
+        cf_t, cf_e, cf_f, acc, acc_n, pk, cb, cbn,
+        dest, slots, sout, tin1, tred, tin2, dense_a, dense_b, ts, tst, th, dynr,
         sq_row, rq_row, sq_e, rq_we, rq_o,
-        cm, cmr, coef, ct, ln, nb, s2, ls2, cv, xt,
+        cm, cmr, coef, ct, nb, s1, ls1, s2, ls2, cv, xt,
         st_row, rt_row, es, rt_we, rt_d,
-        ssem, rsem,
+        ssem, rsem, lsem,
     ) = refs[8:]
     mx, my = lax.axis_index("gx"), lax.axis_index("gy")
 
@@ -97,6 +98,13 @@
     barrier = pltpu.get_barrier_semaphore()
     for d in partners:
         pl.semaphore_signal(barrier, inc=1, device_id=at(*d), device_id_type=MESH)
+
+    fetch = [
+        pltpu.make_async_copy(a, b, lsem.at[k])
+        for k, (a, b) in enumerate(((mat_hbm, mat), (sink_hbm, sink), (drain_hbm, drain)))
+    ]
+    for c in fetch:
+        c.start()
 
     numbers = Layout()
     started = []
@@ -116,32 +124,48 @@
     last_lane = lane8 == LN - 1
     low_half = lane8 < LN // 2
 
-    cols_all, rows_all = 32 * ny, 32 * nx
-    n_inst = inst_tile.shape[0] * LN
-    sub_c = iota((cols_all, LN), 0)
-    sub_r = iota((rows_all, LN), 0)
-    for k in range(n_inst // LN):
+    devices = nx * ny
+    chunks = inst_tile.shape[0]
+    sub_d = iota((devices, LN), 0)
+    lane_d = iota((devices, LN), 1)
+    up_to = jnp.where(iota((LN, LN), 0) <= iota((LN, LN), 1), 1.0, 0.0).astype(BF16)
+    for k in range(chunks):
+        s = inst_tile[k : k + 1, :] >> 10
+        owner = (s % ny) * nx + s // ny
+        dest[:, k * LN : (k + 1) * LN] = jnp.where(sub_d == owner, 1.0, 0.0).astype(BF16)
+    before = jnp.zeros((devices, 1), F32)
+    slot_row = iota((64, LN), 0)
+    for k in range(chunks):
+        span = slice(k * LN, (k + 1) * LN)
+        d = dest[:, span]
+        within = jnp.dot(d, up_to, preferred_element_type=F32)
+        rank = jnp.sum(d.astype(F32) * (within + before), axis=0, keepdims=True)
+        before = before + within[:, LN - 1 : LN]
+        at_slot = (slot_row & 31) == rank.astype(jnp.int32) - 1
         t = inst_tile[k : k + 1, :]
-        s = t >> 10
-        row = (s // ny) * 32 + ((t >> 5) & 31)
-        col = (s % ny) * 32 + (t & 31)
-        span = slice(k * LN, (k + 1) * LN)
-        onehot_a[:, span] = jnp.where(sub_c == col, 1.0, 0.0).astype(BF16)
-        hit = sub_r == row
+        ids = ((t & 992).astype(F32), (t & 31).astype(F32), jnp.zeros((1, LN), F32))
         for q, part in enumerate(pieces(inst_power[k : k + 1, :], 3)):
-            onehot_b[q, :, span] = jnp.where(hit, part.astype(F32), 0.0).astype(BF16)
+            value = jnp.where(slot_row < 32, part.astype(F32), ids[q])
+            slots[q, :, span] = jnp.where(at_slot, value, 0.0).astype(BF16)
     total = None
     for q in range(3):
         term = lax.dot_general(
-            onehot_a[...], onehot_b[q], (((1,), (1,)), ((), ())), preferred_element_type=F32
+            dest[...], slots[q], (((1,), (1,)), ((), ())), preferred_element_type=F32
         )
         total = term if total is None else total + term
-    tsum[0:8, :] = jnp.zeros((8, rows_all), F32)
-    tsum[8 : 8 + cols_all, :] = total
-    tsum[8 + cols_all :, :] = jnp.zeros((8, rows_all), F32)
-
-    def window(j):
-        return tsum.at[pl.ds(pl.multiple_of(j * 32, 32), 48), :]
+    sout[...] = jnp.concatenate([total, jnp.zeros((devices, LN - 64), F32)], axis=1)
+    power_sum = jnp.zeros((8, LN), F32)
+    for k in range(chunks // 8):
+        power_sum = power_sum + inst_power[8 * k : 8 * k + 8, :]
+
+    def bundle(j):
+        return sout.at[pl.ds(pl.multiple_of(j * nx, nx), nx), :]
+
+    pl.semaphore_wait(barrier, len(partners))
+    tile_in = []
+    for d in range(1, ny):
+        tile_in.append(send(bundle(lax.rem(my + d, ny)), tin1.at[pl.ds(d * nx, nx)], (0, d)))
+    tin1[0:nx, :] = bundle(my)[...]
 
     def pack(values):
         packed = jnp.zeros((8, LN), F32)
@@ -157,10 +181,14 @@
         mats = [tuple(mat[l, rows, h].astype(F32) for h in halves) for l in range(NL)]
         return mats + [tuple(a[rows, h] for h in halves) for a in (sink, drain)]
 
-    @pl.loop(0, N // 8)
-    def _(k):
-        rows = pl.ds(pl.multiple_of(k * 8, 8), 8)
-        pk[rows, :] = pack(raw(rows))
+    for c in fetch:
+        c.wait()
+
+    @pl.loop(0, N // 32)
+    def _(a):
+        for k in range(4):
+            rows = pl.ds(pl.multiple_of(a * 32 + k * 8, 8), 8)
+            pk[rows, :] = pack(raw(rows))
 
     for k in range(2):
         sq_e[:, k * LN : (k + 1) * LN] = pk[k * LN : (k + 1) * LN, :].T[104:128, :]
@@ -169,12 +197,6 @@
             sq_row[side, q, 0] = a
             sq_row[side, q, 1] = b
 
-    pl.semaphore_wait(barrier, len(partners))
-
-    tile_in = []
-    for d in range(1, ny):
-        j = lax.rem(my + d, ny)
-        tile_in.append(send(window(j), tin1.at[d - 1], (0, d)))
     margin_row = [send(sq_row.at[s], rq_row.at[s], (2 * s - 1, 0)) for s in range(2)]
     margin_we = [send(sq_e, rq_we.at[s], (0, 2 * s - 1)) for s in range(2)]
     margin_o = {}
@@ -202,8 +224,8 @@
                 for place in places:
                     ref[l, h, place : place + 8, :] = zero8
 
-    @pl.loop(0, N // 8)
-    def _(k):
+    @pl.loop(0, N // 8, init_carry=power_sum)
+    def source_sum(k, source_sum):
         rows = pl.ds(pl.multiple_of(k * 8, 8), 8)
         into = pl.ds(pl.multiple_of(k * 8 + RO, 8), 8)
         for h in range(2):
@@ -212,18 +234,20 @@
                 lat[l, h, into, :] = lookup(ids, table[0])
                 ver[l, h, into, :] = lookup(ids, table[1])
             snk[h, into, :] = sink[rows, halves[h]]
-            drn[h, into, :] = drain[rows, halves[h]]
-
-    total = window(my)[...]
-    for d in range(1, ny):
-        tile_in[d - 1].wait_recv()
-        total = total + tin1[d - 1]
+            d = drain[rows, halves[h]]
+            drn[h, into, :] = d
+            source_sum = source_sum + d
+        return source_sum
+
+    for c in tile_in:
+        c.wait_recv()
     for x in range(nx):
-        tred[x] = shift(total, -(32 * x - 1), 1)[:, :LN]
+        tred[x] = tin1[pl.ds(x, ny, stride=nx), :]
     tile_in2 = []
     for d in range(1, nx):
         x = lax.rem(mx + d, nx)
-        tile_in2.append(send(tred.at[x], tin2.at[d - 1], (d, 0)))
+        tile_in2.append(send(tred.at[x], tin2.at[pl.ds(d * ny, ny)], (d, 0)))
+    tin2[0:ny, :] = tred[mx]
 
     edge_n = jnp.where(mx == 0, 0.0, 1.0)
     edge_s = jnp.where(mx == nx - 1, 0.0, 1.0)
@@ -337,9 +361,58 @@
             acc_n[rows, q * LN : (q + 1) * LN] = sums[0][q]
             acc[rows, q * LN : (q + 1) * LN] = sums[1][q]
 
-    @pl.loop(0, N // 8 + 2)
-    def _(k):
-        base = pl.multiple_of(RO - 8 + 8 * k, 8)
+    for c in tile_in2:
+        c.wait_recv()
+    quarter = devices // 4
+    lane_q = iota((quarter, LN), 1)
+    power = jnp.zeros((quarter, LN), F32)
+    ids = power
+    for k in range(4):
+        part = tin2[k * quarter : (k + 1) * quarter, :]
+        mine = (lane_q >> 5) == k
+        power = jnp.where(mine, shift(part, 32 * k, 1), power)
+        ids = jnp.where(mine, shift(part, 32 * k - 32, 1), ids)
+    ids = ids.astype(jnp.int32)
+    powers = [part.astype(F32) for part in pieces(power, 3)]
+    sub32 = iota((32, LN), 0)
+    for k in range(quarter):
+        span = slice(k * LN, (k + 1) * LN)
+        one_id = ids[k : k + 1, :]
+        dense_a[:, span] = jnp.where(sub32 == (one_id >> 5), 1.0, 0.0).astype(BF16)
+        hit = sub32 == (one_id & 31)
+        for q in range(3):
+            dense_b[q, :, span] = jnp.where(hit, powers[q][k : k + 1, :], 0.0).astype(BF16)
+    total = None
+    for q in range(3):
+        term = lax.dot_general(
+            dense_a[...], dense_b[q], (((1,), (1,)), ((), ())), preferred_element_type=F32
+        )
+        total = term if total is None else total + term
+    total = jnp.concatenate([total * (1.0 / 64.0), jnp.zeros((32, LN - 32), F32)], axis=1)
+    ts[...] = total
+    tst[...] = jnp.concatenate([total, jnp.zeros((LN - 32, LN), F32)], axis=0).T[0:32, :]
+    th_in = [
+        send(a.at[pl.ds(24 * s, 8)], th.at[2 * q + s], d)
+        for q, a in enumerate((ts, tst))
+        for s, d in enumerate(((-1, 0), (1, 0)) if q == 0 else ((0, -1), (0, 1)))
+    ]
+    spread_cols = jnp.where(iota((LN, N), 0) == (iota((LN, N), 1) >> 3), 1.0, 0.0).astype(BF16)
+    wide = pick_dot(total, spread_cols)
+    for h in range(2):
+        dynr[h, 8:40, :] = wide[:, halves[h]]
+
+    @pl.loop(0, N // 32)
+    def _(a):
+        for k in range(4):
+            for h in range(2):
+                dyn_out[pl.ds(pl.multiple_of(a * 32 + k * 8, 8), 8), halves[h]] = jnp.broadcast_to(
+                    dynr[h, pl.ds(8 + 4 * a + k, 1), :], (8, LN)
+                )
+
+    dyn_copy = pltpu.make_async_copy(dyn_out, dyn_hbm, lsem.at[0])
+    dyn_copy.start()
+
+    def diagonal(base):
         here, above = pl.ds(base, 8), pl.ds(base - 1, 8)
         bf = columns(cf_f, base)
         for l in range(NL):
@@ -358,6 +431,14 @@
                 dg[l, h, here, :] = d
                 wg[l, h, here, :] = DAMPING / d
 
+    diagonal(RO - 8)
+    diagonal(RO + N)
+
+    @pl.loop(0, N // 32)
+    def _(a):
+        for k in range(4):
+            diagonal(pl.multiple_of(RO + 32 * a + 8 * k, 8))
+
     block_lane = lane8 & 31
     own_block = (block_lane >= 8) & (block_lane < 16)
 
@@ -379,27 +460,35 @@
     c_diag = c_east + c_east_prev + c_north + c_north_prev + c_up + shift(c_up, 32, 1) + c_sink
     for q, x in enumerate((c_east, c_north, c_up, c_diag)):
         cm[q] = x
-    ct[0, 1] = c_diag
     cm_in = {d: (k, send(cm, cmr.at[k], d)) for k, d in enumerate(DIRS)}
 
-    total = tred[mx]
-    for d in range(1, nx):
-        tile_in2[d - 1].wait_recv()
-        total = total + tin2[d - 1]
-    total = total * (1.0 / 64.0)
-    wide = jnp.concatenate([total, jnp.zeros((LN - 48, LN), F32)], axis=0)
-    to_rows = jnp.where(iota((LN, SW), 0) == ((iota((LN, SW), 1) - 120) >> 3), 1.0, 0.0)
-    dyn_t = exact_dot(wide[:48, :], to_rows)
-    dyn_s = jnp.where(layer_rows == 13, dyn_t[7:8, :], jnp.where(layer_rows == 14, dyn_t[40:41, :], 0.0))
-    spread_rows = jnp.where(iota((NR, LN), 1) == ((iota((NR, LN), 0) - 8) >> 3), 1.0, 0.0)
-    spread_cols = jnp.where(iota((LN, N), 0) == (iota((LN, N), 1) >> 3) + 8, 1.0, 0.0)
-    dyn_all = exact_dot(exact_dot(spread_rows, wide.T), spread_cols)
-    for h in range(2):
-        dyn[h] = dyn_all[:, halves[h]]
-    dyn_out[...] = dyn_all[RO : RO + N, :]
-
-    for _, c in cm_in.values():
-        c.wait_recv()
+    def sum_along_gx(it, *tiles):
+        parts = len(tiles)
+        for q, x in enumerate(tiles):
+            s1[it, q] = x
+        span = pl.ds(0, parts)
+        return [send(s1.at[it, span], ls1.at[it, d - 1, span], (d, 0)) for d in range(1, nx)]
+
+    def sum_along_gy(it, arriving, parts):
+        span = pl.ds(0, parts)
+        total = [s1[it, q] for q in range(parts)]
+        for d in range(1, nx):
+            arriving[d - 1].wait_recv()
+            for q in range(parts):
+                total[q] = total[q] + ls1[it, d - 1, q]
+        for q in range(parts):
+            s2[it, q] = total[q]
+        return [send(s2.at[it, span], ls2.at[it, d - 1, span], (0, d)) for d in range(1, ny)]
+
+    def sum_end(it, arriving, parts):
+        total = [s2[it, q] for q in range(parts)]
+        for d in range(1, ny):
+            arriving[d - 1].wait_recv()
+            for q in range(parts):
+                total[q] = total[q] + ls2[it, d - 1, q]
+        return [x.sum(axis=0, keepdims=True).sum(axis=1, keepdims=True) for x in total]
+
+    sums_gx = sum_along_gx(0, source_sum, c_diag)
 
     def assemble(own, other):
         rows = []
@@ -408,17 +497,20 @@
             rows.append(centre + shift(other((dx, -1)), -8, 1) + shift(other((dx, 1)), 8, 1))
         return jnp.concatenate(rows, axis=0)
 
-    w_east, w_north, w_up, w_diag = (
-        assemble(cm[q], lambda d, q=q: cmr[cm_in[(-d[0], -d[1])][0], q]) for q in range(4)
-    )
-    gain = jnp.where((iota((24, LN), 1) & 31) < 24, DAMPING / jnp.maximum(w_diag, 1e-30), 0.0)
-    coef[0] = gain
-    coef[1] = gain * w_east
-    coef[2] = gain * shift(w_east, 1, 0)
-    coef[3] = gain * w_north
-    coef[4] = gain * shift(w_north, 1, 1)
-    coef[5] = gain * w_up
-    coef[6] = gain * shift(w_up, 32, 1)
+    def couplings():
+        for _, c in cm_in.values():
+            c.wait_recv()
+        w_east, w_north, w_up, w_diag = (
+            assemble(cm[q], lambda d, q=q: cmr[cm_in[(-d[0], -d[1])][0], q]) for q in range(4)
+        )
+        gain = jnp.where((iota((24, LN), 1) & 31) < 24, DAMPING / jnp.maximum(w_diag, 1e-30), 0.0)
+        coef[0] = gain
+        coef[1] = gain * w_east
+        coef[2] = gain * shift(w_east, 1, 0)
+        coef[3] = gain * w_north
+        coef[4] = gain * shift(w_north, 1, 1)
+        coef[5] = gain * w_up
+        coef[6] = gain * shift(w_up, 32, 1)
 
     def couple(ref, base, edge, live):
         here, above, below = pl.ds(base, 8), pl.ds(base - 1, 8), pl.ds(base + 1, 8)
@@ -447,38 +539,24 @@
                         res[to][h] = term if res[to][h] is None else res[to][h] + term
         return mid, res
 
+    def dyn_rows(base, h):
+        return dynr[h, pl.ds(base // 8 + 6, 1), :]
+
     strip_top = layer_rows >= 12
-
-    def source_strip(tm):
-        return jnp.where(strip_top, dyn_s + drain_s * jnp.exp(DRAIN_SLOPE * jnp.where(strip_top, tm, 0.0)), 0.0)
-
-    tm = te = source_s = None
+    row16 = iota((16, LN), 0)
+    lane16 = iota((16, LN), 1)
+    lane24 = iota((24, LN), 1)
+    tm = te = source_s = dyn_s = diag_total = None
     sweeps = OUTER * INNER
     for it in range(sweeps):
         first, last = it == 0, it == sweeps - 1
-        fresh = it % INNER == 0
-        if fresh:
-            source_s = dyn_s + drain_s if first else source_strip(tm)
-        if first:
-            r_s = source_s
-        else:
-            r_s = source_s - (
-                d_s * tm
-                - fs_out * from_outside(tm)
-                - fs_in * from_inside(te)
-                - fs_row * shift(tm, -1, 1)
-                - fs_row_prev * shift(tm, 1, 1)
-                - fs_ver * shift(tm, 4, 0)
-                - fs_ver_prev * shift(tm, -4, 0)
-            )
-            column_form(fs_in * tm, cf_t)
-        column_form(fs_in * (w_s * r_s), cf_e)
+        parts = 2 if first else 1
 
         def residual(base, sums):
             here = pl.ds(base, 8)
             if first:
                 for h in range(2):
-                    r = dyn[h, here, :] + drn[h, here, :]
+                    r = dyn_rows(base, h) + drn[h, here, :]
                     src[h, here, :] = r
                     r_[0, h, here, :] = r
                     e1_[0, h, here, :] = wg[0, h, here, :] * r
@@ -490,19 +568,24 @@
                 for h in range(2):
                     r = res[l][h] - dg[l, h, here, :] * mid[l][h]
                     if l == 0:
-                        if fresh:
-                            s = dyn[h, here, :] + drn[h, here, :] * jnp.exp(DRAIN_SLOPE * mid[0][h])
-                            src[h, here, :] = s
-                        else:
-                            s = src[h, here, :]
-                        r = r + s
+                        r = r + src[h, here, :]
                     r_[l, h, here, :] = r
                     e1_[l, h, here, :] = wg[l, h, here, :] * r
                     if sums is not None:
                         sums[2 * l + h] += r
 
-        residual(RO - 8, None)
-        residual(RO + N, None)
+        if not first:
+            r_s = source_s - (
+                d_s * tm
+                - fs_out * from_outside(tm)
+                - fs_in * from_inside(te)
+                - fs_row * shift(tm, -1, 1)
+                - fs_row_prev * shift(tm, 1, 1)
+                - fs_ver * shift(tm, 4, 0)
+                - fs_ver_prev * shift(tm, -4, 0)
+            )
+            column_form(fs_in * tm, cf_t)
+            column_form(fs_in * (w_s * r_s), cf_e)
 
         @pl.loop(0, N // 32)
         def _(a):
@@ -514,75 +597,76 @@
                 acc[rows, q * LN : (q + 1) * LN] = sums[q]
 
         own_c = block_rows(pick_dot(acc[...], cb[...]))
-        ct[it, 0] = own_c
-        parts = 2 if first else 1
-        line = [
-            send(ct.at[it, pl.ds(0, parts)], ln.at[it, d - 1, pl.ds(0, parts)], (d, 0)) for d in range(1, nx)
-        ]
-        side = {
-            d: (k, send(ct.at[it, 0], nb.at[it, k], d)) for k, d in enumerate(OFF_LINE)
-        }
+        ct[it] = own_c
+        side = {d: (k, send(ct.at[it], nb.at[it, k], d)) for k, d in enumerate(DIRS)}
+
+        if first:
+            for c in th_in:
+                c.wait_recv()
+            sub8 = iota((8, LN), 0)
+            rims = jnp.where(sub8 == 0, th[1, 7:8, :], jnp.where(sub8 == 1, th[0, 0:1, :], 0.0))
+            wide_rims = pick_dot(rims, spread_cols)
+            for h in range(2):
+                dynr[h, 0:8, :] = jnp.broadcast_to(wide_rims[0:1, halves[h]], (8, LN))
+                dynr[h, 40:48, :] = jnp.broadcast_to(wide_rims[1:2, halves[h]], (8, LN))
+            rims = jnp.where(sub8 == 0, th[3, 7:8, :], jnp.where(sub8 == 1, th[2, 0:1, :], 0.0))
+            spread_rows = iota((LN, SW), 0) == ((iota((LN, SW), 1) - LN) >> 3)
+            tall_rims = pick_dot(rims, jnp.where(spread_rows, 1.0, 0.0).astype(BF16))
+            dyn_s = jnp.where(
+                layer_rows == 13, tall_rims[0:1, :], jnp.where(layer_rows == 14, tall_rims[1:2, :], 0.0)
+            )
+            source_s = dyn_s + drain_s
+            column_form(fs_in * (w_s * source_s), cf_e)
+        residual(RO - 8, None)
+        residual(RO + N, None)
+
+        sums_gy = sum_along_gy(it, sums_gx, parts)
 
         live = 1 if first else NL
 
-        @pl.loop(0, N // 8)
-        def _(k):
-            base = pl.multiple_of(RO + 8 * k, 8)
-            here = pl.ds(base, 8)
-            mid, res = couple(e1_, base, columns(cf_e, base), live)
-            tops = []
-            for l in range(NL):
-                pair = []
-                for h in range(2):
-                    u = None
-                    if l < live:
-                        u = (1.0 - DAMPING) * mid[l][h] + wg[l, h, here, :] * (r_[l, h, here, :] + res[l][h])
-                    elif res[l][h] is not None:
-                        u = wg[l, h, here, :] * res[l][h]
-                    else:
-                        u = zero8
-                    if not first:
-                        u = u + t_[l, h, here, :]
-                    t_[l, h, here, :] = u
-                    pair.append(u)
-                tops.append(tuple(pair))
-            if not last:
-                pk[pl.ds(pl.multiple_of(8 * k, 8), 8), :] = pack(tops)
+        @pl.loop(0, N // 32)
+        def _(a):
+            for k in range(4):
+                base = pl.multiple_of(RO + 32 * a + 8 * k, 8)
+                here = pl.ds(base, 8)
+                mid, res = couple(e1_, base, columns(cf_e, base), live)
+                tops = []
+                for l in range(NL):
+                    pair = []
+                    for h in range(2):
+                        if l < live:
+                            u = (1.0 - DAMPING) * mid[l][h] + wg[l, h, here, :] * (r_[l, h, here, :] + res[l][h])
+                        elif res[l][h] is not None:
+                            u = wg[l, h, here, :] * res[l][h]
+                        else:
+                            u = zero8
+                        if not first:
+                            u = u + t_[l, h, here, :]
+                        t_[l, h, here, :] = u
+                        pair.append(u)
+                    tops.append(tuple(pair))
+                if not last:
+                    pk[pl.ds(pl.multiple_of(32 * a + 8 * k, 8), 8), :] = pack(tops)
 
         if not last:
-            for k in range(2):
-                es[it, :, k * LN : (k + 1) * LN] = pk[k * LN : (k + 1) * LN, :].T[112:128, :]
             for s, base in enumerate((RO, RO + N - 8)):
                 for l in range(NL):
                     for h in range(2):
                         st_row[it, s, l, h] = t_[l, h, base : base + 8, :]
             row_in = [send(st_row.at[it, s], rt_row.at[it, s], (2 * s - 1, 0)) for s in range(2)]
+            for k in range(2):
+                es[it, :, k * LN : (k + 1) * LN] = pk[k * LN : (k + 1) * LN, :].T[112:128, :]
             we_in = [send(es.at[it], rt_we.at[it, s], (0, 2 * s - 1)) for s in range(2)]
             diag_in = {}
             for k, d in enumerate(DIAG):
                 half = 0 if d[0] < 0 else 1
                 diag_in[d] = (k, send(es.at[it, :, pl.ds(half * LN, LN)], rt_d.at[it, k], d))
 
-        total = [ct[it, q] for q in range(parts)]
-        for d in range(1, nx):
-            line[d - 1].wait_recv()
-            for q in range(parts):
-                total[q] = total[q] + ln[it, d - 1, q]
-        sub8 = iota((8, LN), 0)
-        packed = jnp.where(sub8 == 0, total[0].sum(axis=0, keepdims=True), 0.0)
         if first:
-            packed = jnp.where(sub8 == 1, total[1].sum(axis=0, keepdims=True), packed)
-        s2[it] = packed
-        gather = [send(s2.at[it], ls2.at[it, d - 1], (0, d)) for d in range(1, ny)]
+            couplings()
         for _, c in side.values():
             c.wait_recv()
-
-        def other(d):
-            if d[1] == 0:
-                return ln[it, 0 if d[0] < 0 else nx - 2, 0]
-            return nb[it, side[(-d[0], -d[1])][0]]
-
-        rw = coef[0] * assemble(own_c, other)
+        rw = coef[0] * assemble(own_c, lambda d: nb[it, side[(-d[0], -d[1])][0]])
         x = rw
         for _ in range(CJ - 1):
             x = (
@@ -591,43 +675,62 @@
                 + coef[3] * shift(x, -1, 1) + coef[4] * shift(x, 1, 1)
                 + coef[5] * shift(x, -32, 1) + coef[6] * shift(x, 32, 1)
             )
-        total = packed
-        for d in range(1, ny):
-            gather[d - 1].wait_recv()
-            total = total + ls2[it, d - 1]
-        sums = total.sum(axis=1, keepdims=True)
+        sums = sum_end(it, sums_gy, parts)
         if first:
-            diag_total = sums[1:2, :]
-        x = x + BALANCE_WEIGHT * sums[0:1, :] / diag_total
-
-        lane24 = iota((24, LN), 1)
+            diag_total = sums[1]
+        x = x + BALANCE_WEIGHT * sums[0] / diag_total
+
         for l in range(NL):
             for h in range(2):
                 cv[l, h] = jnp.take_along_axis(x, l * 32 + 8 + h * 4 + (lane24 >> 5), axis=1)
 
         if last:
-            @pl.loop(0, N // 32)
-            def _(a):
-                for l in range(NL):
-                    for h in range(2):
-                        add = cv[l, h, pl.ds(8 + a, 1), :]
-                        for k in range(4):
-                            rows = pl.ds(pl.multiple_of(32 * a + 8 * k, 8), 8)
-                            here = pl.ds(pl.multiple_of(RO + 32 * a + 8 * k, 8), 8)
-                            out[l, rows, halves[h]] = t_[l, h, here, :] + add
+            writes = []
+            for part in range(4):
+
+                @pl.loop(2 * part, 2 * part + 2)
+                def _(a):
+                    for l in range(NL):
+                        for h in range(2):
+                            add = cv[l, h, pl.ds(8 + a, 1), :]
+                            for k in range(4):
+                                rows = pl.ds(pl.multiple_of(32 * a + 8 * k, 8), 8)
+                                here = pl.ds(pl.multiple_of(RO + 32 * a + 8 * k, 8), 8)
+                                out[l, rows, halves[h]] = t_[l, h, here, :] + add
+
+                span = pl.ds(64 * part, 64)
+                writes.append(
+                    pltpu.make_async_copy(out.at[:, span, :], out_hbm.at[:, span, :], lsem.at[3 + part])
+                )
+                writes[-1].start()
             break
 
-        @pl.loop(0, N // 32)
-        def _(a):
+        fresh = (it + 1) % INNER == 0
+
+        @pl.loop(0, N // 32, init_carry=zero8)
+        def source_sum(a, source_sum):
             for l in range(NL):
                 for h in range(2):
                     add = cv[l, h, pl.ds(8 + a, 1), :]
                     for k in range(4):
-                        here = pl.ds(pl.multiple_of(RO + 32 * a + 8 * k, 8), 8)
-                        t_[l, h, here, :] = t_[l, h, here, :] + add
+                        base = pl.multiple_of(RO + 32 * a + 8 * k, 8)
+                        here = pl.ds(base, 8)
+                        u = t_[l, h, here, :] + add
+                        t_[l, h, here, :] = u
+                        if l == 0:
+                            if fresh:
+                                s = dyn_rows(base, h) + drn[h, here, :] * jnp.exp(DRAIN_SLOPE * u)
+                                src[h, here, :] = s
+                            else:
+                                s = src[h, here, :]
+                            source_sum = source_sum + s
+                        if l == NL - 1:
+                            source_sum = source_sum - snk[h, here, :] * u
+            return source_sum
+
+        sums_gx = sum_along_gx(it + 1, source_sum)
 
         xt[...] = jnp.concatenate([x, jnp.zeros((LN - 24, LN), F32)], axis=0).T
-        row16 = iota((16, LN), 0)
         ring = jnp.zeros((16, LN), F32)
         own_v = ring
         for l in range(NL):
@@ -635,7 +738,6 @@
                 mine = (row16 >> 1) == 2 * (NL - 1 - l) + pair
                 ring = jnp.where(mine, xt[l * 32 + (7, 16)[pair] : l * 32 + (7, 16)[pair] + 1, :], ring)
                 own_v = jnp.where(mine, xt[l * 32 + (15, 8)[pair] : l * 32 + (15, 8)[pair] + 1, :], own_v)
-        lane16 = iota((16, LN), 1)
 
         def along(v):
             return jnp.concatenate(
@@ -647,7 +749,12 @@
         for slot, base, at_row in ((1, RO - 8, 7), (0, RO + N, 16)):
             for l in range(NL):
                 for h in range(2):
-                    t_[l, h, base : base + 8, :] = rt_row[it, slot, l, h] + cv[l, h, at_row : at_row + 1, :]
+                    u = rt_row[it, slot, l, h] + cv[l, h, at_row : at_row + 1, :]
+                    t_[l, h, base : base + 8, :] = u
+                    if l == 0 and fresh:
+                        src[h, base : base + 8, :] = dyn_rows(base, h) + drn[
+                            h, base : base + 8, :
+                        ] * jnp.exp(DRAIN_SLOPE * u)
         for c in we_in:
             c.wait_recv()
         for _, c in diag_in.values():
@@ -661,51 +768,72 @@
         tm = jnp.where(c16 < 2, west, east) + along(ring)
         blank = jnp.zeros((16, LN), F32)
         te = jnp.concatenate([blank, es[it], blank], axis=1) + along(own_v)
+        if fresh:
+            source_s = jnp.where(
+                strip_top, dyn_s + drain_s * jnp.exp(DRAIN_SLOPE * jnp.where(strip_top, tm, 0.0)), 0.0
+            )
 
     for c in started:
         c.wait_send()
+    dyn_copy.wait()
+    for c in writes:
+        c.wait()
+
+
+def hand_over(a, b, to_a, to_b, sem):
+    copies = [
+        pltpu.make_async_copy(a.at[l], to_a.at[l], sem.at[l]) for l in range(NL)
+    ] + [pltpu.make_async_copy(b, to_b, sem.at[NL])]
+    for c in copies:
+        c.start()
+    for c in copies:
+        c.wait()
 
 
 def n_copies(nx, ny):
-    setup = (ny - 1) + 2 + 2 + 6 + (nx - 1) + 8
-    each = (nx - 1) + 6 + (ny - 1)
+    setup = (ny - 1) + 2 + 2 + 6 + (nx - 1) + 4 + 8
+    each = 8 + (nx - 1) + (ny - 1)
     return setup + OUTER * INNER * each + (OUTER * INNER - 1) * 8
 
 
 def solution(mesh):
     nx, ny = mesh.shape["gx"], mesh.shape["gy"]
     its = OUTER * INNER
+    devices = nx * ny
 
     def step(material, material_table, sink_cond, drain_current, instance_tile, instance_power):
         n_inst = instance_tile.shape[0]
         field = pltpu.VMEM((NL, 2, NR, LN), F32)
         single = pltpu.VMEM((2, NR, LN), F32)
         vm = lambda *shape: pltpu.VMEM(shape, F32)
+        half = lambda *shape: pltpu.VMEM(shape, BF16)
         copies = n_copies(nx, ny)
         scratch = [
+            pltpu.VMEM((NL, N, N), jnp.int32), vm(N, N), vm(N, N), vm(NL, N, N), vm(N, N),
             field, field, field, field, pltpu.VMEM((NL - 1, 2, NR, LN), F32), field, field,
-            single, single, single, single, field, field, field,
+            single, single, single, field, field, field,
             vm(SW, LN), vm(SW, LN), vm(SW, LN), vm(64, 8 * LN), vm(64, 8 * LN), vm(N, LN),
-            pltpu.VMEM((32 * ny, n_inst), BF16), pltpu.VMEM((3, 32 * nx, n_inst), BF16),
-            pltpu.VMEM((8 * LN, LN), BF16), pltpu.VMEM((8 * LN, LN), BF16),
-            vm(32 * ny + 16, 32 * nx), vm(ny - 1, 48, 32 * nx), vm(nx, 48, LN), vm(nx - 1, 48, LN),
+            half(8 * LN, LN), half(8 * LN, LN),
+            half(devices, n_inst), half(3, 64, n_inst), vm(devices, LN), vm(devices, LN),
+            vm(nx, ny, LN), vm(devices, LN), half(32, 32 * devices), half(3, 32, 32 * devices),
+            vm(32, LN), vm(32, LN), vm(4, 8, LN), vm(2, 48, LN),
             vm(2, 6, 2, 8, LN), vm(2, 6, 2, 8, LN), vm(24, N), vm(2, 24, N), vm(6, 24, LN),
-            vm(4, 8, LN), vm(8, 4, 8, LN), vm(7, 24, LN), vm(its, 2, 8, LN), vm(its, nx - 1, 2, 8, LN),
-            vm(its, 6, 8, LN), vm(its, 8, LN), vm(its, ny - 1, 8, LN), vm(NL, 2, 24, LN), vm(LN, LN),
+            vm(4, 8, LN), vm(8, 4, 8, LN), vm(7, 24, LN), vm(its, 8, LN), vm(its, 8, 8, LN),
+            vm(its, 2, 8, LN), vm(its, nx - 1, 2, 8, LN), vm(its, 2, 8, LN), vm(its, ny - 1, 2, 8, LN),
+            vm(NL, 2, 24, LN), vm(LN, LN),
             vm(its - 1, 2, NL, 2, 8, LN), vm(its - 1, 2, NL, 2, 8, LN),
             vm(its - 1, 16, N), vm(its - 1, 2, 16, N), vm(its - 1, 4, 16, LN),
-            pltpu.SemaphoreType.DMA((copies,)), pltpu.SemaphoreType.DMA((copies,)),
+            pltpu.SemaphoreType.DMA((copies,)), pltpu.SemaphoreType.DMA((copies,)), pltpu.SemaphoreType.DMA((7,)),
         ]
         vmem = pl.BlockSpec(memory_space=pltpu.VMEM)
         smem = pl.BlockSpec(memory_space=pltpu.SMEM)
-        return pl.pallas_call(
+        hbm = pl.BlockSpec(memory_space=pl.ANY)
+        shapes = (jax.ShapeDtypeStruct((NL, N, N), F32), jax.ShapeDtypeStruct((N, N), F32))
+        results = pl.pallas_call(
             functools.partial(kernel, nx, ny),
-            out_shape=(
-                jax.ShapeDtypeStruct((NL, N, N), F32),
-                jax.ShapeDtypeStruct((N, N), F32),
-            ),
-            in_specs=[vmem, smem, vmem, vmem, vmem, vmem],
-            out_specs=(vmem, vmem),
+            out_shape=shapes,
+            in_specs=[hbm, smem, hbm, hbm, vmem, vmem],
+            out_specs=(hbm, hbm),
             scratch_shapes=scratch,
             compiler_params=pltpu.CompilerParams(
                 collective_id=0, has_side_effects=True, vmem_limit_bytes=56 * 1024 * 1024
@@ -718,6 +846,13 @@
             instance_tile.reshape(n_inst // LN, LN),
             instance_power.reshape(n_inst // LN, LN),
         )
+        return pl.pallas_call(
+            hand_over,
+            out_shape=shapes,
+            in_specs=[vmem, vmem],
+            out_specs=(hbm, hbm),
+            scratch_shapes=[pltpu.SemaphoreType.DMA((NL + 1,))],
+        )(*results)
 
     return jax.shard_map(
         step,

time: 93 us -> 65.4 us (0.70)
  Pallas kernels: 89.1 us -> 64.6 us
  local copies, waits for them, and re-layouts: 3.03 us -> 0 us
    pallas_call x1 -> x2, Pallas kernels: 89.1 us -> 64.6 us  [the longest x1 62.2 us: step(): pl.pallas_call(functools.partial(kernel, nx, ny), out_shape=shapes, in_sp...]
    unnamed x4 -> x0, local copies, waits for them, and re-layouts: 3.03 us -> none
where the time goes in v2:
time: 65.4 us; the launch traced here: 65.2 us
  Pallas kernels  64.6 us (99%)
    pallas_call x1, Pallas kernels, step(): pl.pallas_call(functools.partial(kernel, nx, ny), out_shape=shapes, in_sp...  62.2 us
    pallas_call x1, Pallas kernels, step(): pl.pallas_call(hand_over, out_shape=shapes, in_specs=[vmem, vmem], out_sp...  2.36 us

profile of v2, /device:TPU:1, one launch (start us, length us, event | category | flops | bytes accessed | tf_op | source)
XLA Modules:
  0.0 65.2 jit_solution(10616706755585200941)
XLA Ops:
  0.6 62.2 %shard_map.77 = (f32[4,256,256]{2,1,0:T(8,128)}, f32[256,256]{1,0:T(8,128)}) custom-call(s32[4,256,256]{2,1,0:T(8,128)} %refs_0_.1, f32[2,16]{1,0:T(2,128)} %refs_1_.1, f32[256,256]{1,0:T(8,128)} %refs_2_.1, f32[256,256]{1,0:T(8,128)} %refs_3_.1, s32[16,128]{1,0:T(8,128)} %bitcast.2, f32[16,128]{1,0:T(8,128)} %bitcast.3), custom_call_target="tpu_custom_call" | custom-call | tf_op jit(solution)/shard_map/pallas_call | solution.py:832
  62.8 2.4 %shard_map.78 = (f32[4,256,256]{2,1,0:T(8,128)}, f32[256,256]{1,0:T(8,128)}) custom-call(f32[4,256,256]{2,1,0:T(8,128)} %get-tuple-element.4.a, f32[256,256]{1,0:T(8,128)} %get-tuple-element.5.b), custom_call_target="tpu_custom_call" | custom-call | tf_op jit(solution)/shard_map/pallas_call | solution.py:849

commit v3 on v2

v3 whole, which is shorter than its diff:
```python
import functools

import jax
import jax.numpy as jnp
from jax import lax
from jax.experimental import pallas as pl
from jax.experimental.pallas import tpu as pltpu
from jax.sharding import PartitionSpec as P

MESH = pl.DeviceIdType.MESH
F32 = jnp.float32
BF16 = jnp.bfloat16

NL = 4
N = 256
LN = 128
RO = 16
NR = N + 2 * RO
NQ = 6
SL = 384
SO = 64
OUTER = 2
INNER = 2
CJ = 8
DAMPING = 0.8
DRAIN_SLOPE = 0.5
FACE_FLOOR = 0.5
BALANCE_WEIGHT = 0.5
DIRS = ((-1, -1), (-1, 0), (-1, 1), (0, -1), (0, 1), (1, -1), (1, 0), (1, 1))
DIAG = tuple(d for d in DIRS if d[0] and d[1])
OFF_LINE = tuple(d for d in DIRS if d[1])


def iota(shape, dim):
    return lax.broadcasted_iota(jnp.int32, shape, dim)


def harmonic(a, b):
    return 2.0 * a * b / jnp.maximum(a + b, FACE_FLOOR)


def shift(x, amount, axis):
    return pltpu.roll(x, amount % x.shape[axis], axis)


def lookup(ids, table):
    level = list(table)
    for bit in range(4):
        odd = ((ids >> bit) & 1) == 1
        level = [jnp.where(odd, level[2 * k + 1], level[2 * k]) for k in range(len(level) // 2)]
    return level[0]


def exact_dot(a, b):
    return lax.dot_general(
        a, b, (((1,), (0,)), ((), ())), precision=lax.Precision.HIGHEST, preferred_element_type=F32
    )


def pieces(x, count):
    out = []
    for _ in range(count - 1):
        part = x.astype(BF16)
        out.append(part)
        x = x - part.astype(F32)
    return out + [x.astype(BF16)]


def pick_dot(x, ones):
    return sum(jnp.dot(part, ones, preferred_element_type=F32) for part in pieces(x, 3))


class Layout:
    def __init__(self):
        self.count = 0

    def take(self):
        self.count += 1
        return self.count - 1


def kernel(nx, ny, *refs):
    (mat_hbm, tab, sink_hbm, drain_hbm, inst_tile, inst_power, out_hbm, dyn_hbm) = refs[:8]
    (
        mat, sink, drain, out, dyn_out,
        lat, ver, fr, fc, fl, fv, dg, wg, src, drn, snk, t_, r_, e1_,
        cf_t, cf_e, cf_f, acc, acc_n, pk, cb, cbn,
        dest, slots, sout, tin1, tred, tin2, dense_a, dense_b, ts, th, dynr,
        sq_row, rq_row, sq_c, rq_c, sq_s, rq_s,
        fcs, frs, fvs, dgs, wgs, drn_s, dys, srs,
        cm, cmr, coef, ct, nb, s1, ls1, s2, ls2, cv, cvr, cvl, xt,
        ssem, rsem, lsem,
    ) = refs[8:]
    mx, my = lax.axis_index("gx"), lax.axis_index("gy")

    def at(dx, dy):
        return {"gx": lax.rem(mx + (dx + nx), nx), "gy": lax.rem(my + (dy + ny), ny)}

    partners = [(d, 0) for d in range(1, nx)] + [(0, d) for d in range(1, ny)] + list(DIAG)
    barrier = pltpu.get_barrier_semaphore()
    for d in partners:
        pl.semaphore_signal(barrier, inc=1, device_id=at(*d), device_id_type=MESH)

    fetch = [
        pltpu.make_async_copy(a, b, lsem.at[k])
        for k, (a, b) in enumerate(((mat_hbm, mat), (sink_hbm, sink), (drain_hbm, drain)))
    ]
    for c in fetch:
        c.start()

    numbers = Layout()
    started = []

    def send(a, b, to):
        k = numbers.take()
        copy = pltpu.make_async_remote_copy(
            src_ref=a, dst_ref=b, send_sem=ssem.at[k], recv_sem=rsem.at[k],
            device_id=at(*to), device_id_type=MESH,
        )
        copy.start()
        started.append(copy)
        return copy

    lane8 = iota((8, LN), 1)
    first_lane = lane8 == 0
    last_lane = lane8 == LN - 1
    low_half = lane8 < LN // 2

    devices = nx * ny
    chunks = inst_tile.shape[0]
    sub_d = iota((devices, LN), 0)
    lane_d = iota((devices, LN), 1)
    up_to = jnp.where(iota((LN, LN), 0) <= iota((LN, LN), 1), 1.0, 0.0).astype(BF16)
    for k in range(chunks):
        s = inst_tile[k : k + 1, :] >> 10
        owner = (s % ny) * nx + s // ny
        dest[:, k * LN : (k + 1) * LN] = jnp.where(sub_d == owner, 1.0, 0.0).astype(BF16)
    before = jnp.zeros((devices, 1), F32)
    slot_row = iota((64, LN), 0)
    for k in range(chunks):
        span = slice(k * LN, (k + 1) * LN)
        d = dest[:, span]
        within = jnp.dot(d, up_to, preferred_element_type=F32)
        rank = jnp.sum(d.astype(F32) * (within + before), axis=0, keepdims=True)
        before = before + within[:, LN - 1 : LN]
        at_slot = (slot_row & 31) == rank.astype(jnp.int32) - 1
        t = inst_tile[k : k + 1, :]
        ids = ((t & 992).astype(F32), (t & 31).astype(F32), jnp.zeros((1, LN), F32))
        for q, part in enumerate(pieces(inst_power[k : k + 1, :], 3)):
            value = jnp.where(slot_row < 32, part.astype(F32), ids[q])
            slots[q, :, span] = jnp.where(at_slot, value, 0.0).astype(BF16)
    total = None
    for q in range(3):
        term = lax.dot_general(
            dest[...], slots[q], (((1,), (1,)), ((), ())), preferred_element_type=F32
        )
        total = term if total is None else total + term
    sout[...] = jnp.concatenate([total, jnp.zeros((devices, LN - 64), F32)], axis=1)
    power_sum = jnp.zeros((8, LN), F32)
    for k in range(chunks // 8):
        power_sum = power_sum + inst_power[8 * k : 8 * k + 8, :]

    def bundle(j):
        return sout.at[pl.ds(pl.multiple_of(j * nx, nx), nx), :]

    pl.semaphore_wait(barrier, len(partners))
    tile_in = []
    for d in range(1, ny):
        tile_in.append(send(bundle(lax.rem(my + d, ny)), tin1.at[pl.ds(d * nx, nx)], (0, d)))
    tin1[0:nx, :] = bundle(my)[...]

    def pack(values):
        packed = jnp.zeros((8, LN), F32)
        for q, (a, b) in enumerate(values):
            both = shift(jnp.where(low_half, a, b), 16 * q + 8, 1)
            packed = jnp.where((lane8 >> 4) == q, both, packed)
        return packed

    halves = (slice(0, LN), slice(LN, N))

    def raw(rows):
        mats = [tuple(mat[l, rows, h].astype(F32) for h in halves) for l in range(NL)]
        return mats + [tuple(a[rows, h] for h in halves) for a in (sink, drain)]

    for c in fetch:
        c.wait()
    for side, rows in enumerate((slice(0, 8), slice(N - 8, N))):
        values = raw(rows)
        for q, (a, b) in enumerate(values):
            sq_row[side, q, 0] = a
            sq_row[side, q, 1] = b
        sq_c[side] = pack(values)
    margin_row = [send(sq_row.at[s], rq_row.at[s], (2 * s - 1, 0)) for s in range(2)]
    corner_dirs = ((-1, 0), (1, 0)) + DIAG
    margin_c = {
        d: (k, send(sq_c.at[0 if d[0] < 0 else 1], rq_c.at[k], d)) for k, d in enumerate(corner_dirs)
    }

    @pl.loop(0, N // 32)
    def _(a):
        for k in range(4):
            rows = pl.ds(pl.multiple_of(a * 32 + k * 8, 8), 8)
            pk[pl.ds(pl.multiple_of(a * 32 + k * 8 + SO, 8), 8), :] = pack(raw(rows))

    pk[0:SO, :] = jnp.zeros((SO, LN), F32)
    pk[SO + N :, :] = jnp.zeros((SL - N - SO, LN), F32)
    for k in range(SL // LN):
        span = slice(k * LN, (k + 1) * LN)
        block = pk[span, :].T
        for q in range(NQ):
            sq_s[0, 8 * q : 8 * q + 8, span] = block[16 * q + 8 : 16 * q + 16, :]
            sq_s[1, 8 * q : 8 * q + 8, span] = block[16 * q : 16 * q + 8, :]
    margin_we = [send(sq_s.at[s], rq_s.at[s], (0, 2 * s - 1)) for s in range(2)]

    col_n = iota((LN, LN), 1)
    row_n = iota((LN, LN), 0)
    for l in range(NL):
        for h in range(2):
            span = pl.ds((2 * l + h) * LN, LN)
            goal = l * 32 + 8 + h * 4 + (row_n >> 5)
            cb[span, :] = jnp.where(col_n == goal, 1.0, 0.0).astype(BF16)
            hit = ((row_n & 31) == 31) & (col_n == goal)
            if h == 0:
                hit = hit | ((row_n == 0) & (col_n == l * 32 + 7))
            cbn[span, :] = jnp.where(hit, 1.0, 0.0).astype(BF16)
    table = [[tab[q, k] for k in range(16)] for q in range(2)]

    zero8 = jnp.zeros((8, LN), F32)
    for ref, places in ((t_, (0, NR - 8)), (e1_, (0, NR - 8)), (fr, (0,)), (lat, (NR - 8,))):
        for l in range(NL):
            for h in range(2):
                for place in places:
                    ref[l, h, place : place + 8, :] = zero8

    @pl.loop(0, N // 8, init_carry=power_sum)
    def source_sum(k, source_sum):
        rows = pl.ds(pl.multiple_of(k * 8, 8), 8)
        into = pl.ds(pl.multiple_of(k * 8 + RO, 8), 8)
        for h in range(2):
            for l in range(NL):
                ids = mat[l, rows, halves[h]]
                lat[l, h, into, :] = lookup(ids, table[0])
                ver[l, h, into, :] = lookup(ids, table[1])
            snk[h, into, :] = sink[rows, halves[h]]
            d = drain[rows, halves[h]]
            drn[h, into, :] = d
            source_sum = source_sum + d
        return source_sum

    for c in tile_in:
        c.wait_recv()
    for x in range(nx):
        tred[x] = tin1[pl.ds(x, ny, stride=nx), :]
    tile_in2 = []
    for d in range(1, nx):
        x = lax.rem(mx + d, nx)
        tile_in2.append(send(tred.at[x], tin2.at[pl.ds(d * ny, ny)], (d, 0)))
    tin2[0:ny, :] = tred[mx]

    edge_n = jnp.where(mx == 0, 0.0, 1.0)
    edge_s = jnp.where(mx == nx - 1, 0.0, 1.0)
    edge_w = jnp.where(my == 0, 0.0, 1.0)
    edge_e = jnp.where(my == ny - 1, 0.0, 1.0)
    for c in margin_row:
        c.wait_recv()
    for slot, base, keep in ((1, RO - 8, edge_n), (0, RO + N, edge_s)):
        rows = slice(base, base + 8)
        for h in range(2):
            for l in range(NL):
                ids = rq_row[slot, l, h].astype(jnp.int32)
                lat[l, h, rows, :] = lookup(ids, table[0]) * keep
                ver[l, h, rows, :] = lookup(ids, table[1]) * keep
            snk[h, rows, :] = rq_row[slot, 4, h] * keep
            drn[h, rows, :] = rq_row[slot, 5, h] * keep
    for c in margin_we:
        c.wait_recv()
    for _, c in margin_c.values():
        c.wait_recv()

    def corner_block(dy):
        top, low = (rq_c[margin_c[(-dx, -dy)][0]] for dx in (-1, 1))
        pad = jnp.zeros((SO - 8, LN), F32)
        return jnp.concatenate([pad, top, low, pad], axis=0).T

    blocks = {dy: corner_block(dy) for dy in (-1, 0, 1)}

    def merge(body, corners):
        return jnp.concatenate(
            [
                jnp.where((lane8 >> 3) == SO // 8 - 1, corners, body[:, :LN]),
                body[:, LN : 2 * LN],
                jnp.where((lane8 >> 3) == SO // 8, corners, body[:, 2 * LN :]),
            ],
            axis=1,
        )

    def raw_strip(q, side):
        own, got = slice(8 * q, 8 * q + 8), slice(16 * q, 16 * q + 16)
        if side == 0:
            outside = merge(rq_s[1, own, :], blocks[-1][got, :][0:8, :])
            inside = merge(sq_s[0, own, :], blocks[0][got, :][8:16, :])
            return jnp.concatenate([outside, inside], axis=0)
        outside = merge(rq_s[0, own, :], blocks[1][got, :][8:16, :])
        inside = merge(sq_s[1, own, :], blocks[0][got, :][0:8, :])
        return jnp.concatenate([inside, outside], axis=0)

    sl_lane = iota((16, SL), 1)
    sl_row = iota((16, SL), 0)
    one = jnp.ones((16, SL), F32)
    keep_rows = jnp.where(sl_lane < SO, one * edge_n, jnp.where(sl_lane >= SO + N, one * edge_s, one))
    keep = (
        keep_rows * jnp.where(sl_row < 8, one * edge_w, one),
        keep_rows * jnp.where(sl_row >= 8, one * edge_e, one),
    )
    sides = range(2)
    for g in sides:
        lats, vers = [], []
        for l in range(NL):
            ids = raw_strip(l, g).astype(jnp.int32)
            lats.append(lookup(ids, table[0]) * keep[g])
            vers.append(lookup(ids, table[1]) * keep[g])
        sink_s = raw_strip(4, g) * keep[g]
        drn_s[g] = raw_strip(5, g) * keep[g]
        up = None
        for l in range(NL):
            c = harmonic(lats[l], shift(lats[l], -1, 0))
            r = harmonic(lats[l], shift(lats[l], -1, 1))
            fcs[l, g] = c
            frs[l, g] = r
            d = c + shift(c, 1, 0) + r + shift(r, 1, 1)
            if l > 0:
                d = d + up
            if l < NL - 1:
                up = harmonic(vers[l], vers[l + 1])
                fvs[l, g] = up
                d = d + up
            else:
                d = d + sink_s
            d = jnp.maximum(d, FACE_FLOOR)
            dgs[l, g] = d
            wgs[l, g] = DAMPING / d

    row_z = iota((8, SL), 0)

    def column_form(west, east, ref):
        z = jnp.zeros((8, SL), F32)
        for l in range(NL):
            z = jnp.where(row_z == 2 * l + 1, west[l], jnp.where(row_z == 2 * l, east[l], z))
        for k in range(SL // LN):
            block = jnp.concatenate([z[:, k * LN : (k + 1) * LN], jnp.zeros((LN - 8, LN), F32)], axis=0)
            ref[k * LN : (k + 1) * LN, :] = block.T

    def columns(ref, base):
        tile = ref[pl.ds(base + (SO - RO), 8), :]
        return [shift(tile, -(2 * l + 1), 1) for l in range(NL)]

    def edge_terms(v, ref):
        column_form(
            [(fcs[l, 0] * v[l][0])[7:8, :] for l in range(NL)],
            [fcs[l, 1][7:8, :] * v[l][1][8:9, :] for l in range(NL)],
            ref,
        )

    column_form([fcs[l, 0, 7:8, :] for l in range(NL)], [fcs[l, 1, 7:8, :] for l in range(NL)], cf_f)

    def faces(base, sums):
        bf = columns(cf_f, base)
        here, below = pl.ds(base, 8), pl.ds(base + 1, 8)
        vs = [[ver[l, h, here, :] for h in range(2)] for l in range(NL)]
        for l in range(NL):
            a0, a1 = lat[l, 0, here, :], lat[l, 1, here, :]
            ra0, ra1 = shift(a0, -1, 1), shift(a1, -1, 1)
            c0 = harmonic(a0, jnp.where(last_lane, ra1, ra0))
            c1 = jnp.where(last_lane, bf[l], harmonic(a1, ra1))
            rc0, rc1 = shift(c0, 1, 1), shift(c1, 1, 1)
            fc[l, 0, here, :] = c0
            fc[l, 1, here, :] = c1
            fl[l, 0, here, :] = jnp.where(first_lane, bf[l], rc0)
            fl[l, 1, here, :] = jnp.where(first_lane, rc0, rc1)
            for h, a in ((0, a0), (1, a1)):
                fr[l, h, here, :] = harmonic(a, lat[l, h, below, :])
            if sums is not None:
                sums[0][2 * l] += jnp.where(first_lane, bf[l], c0)
                sums[0][2 * l + 1] += c1
            for h in range(2):
                if l < NL - 1:
                    v = harmonic(vs[l][h], vs[l + 1][h])
                    fv[l, h, here, :] = v
                else:
                    v = snk[h, here, :]
                if sums is not None:
                    sums[1][2 * l + h] += v

    faces(RO - 8, None)
    faces(RO + N, None)

    @pl.loop(0, N // 32)
    def _(a):
        sums = [[zero8] * 8, [zero8] * 8]
        for k in range(4):
            faces(pl.multiple_of(RO + 32 * a + 8 * k, 8), sums)
        rows = pl.ds(pl.multiple_of(a * 8, 8), 8)
        for q in range(8):
            acc_n[rows, q * LN : (q + 1) * LN] = sums[0][q]
            acc[rows, q * LN : (q + 1) * LN] = sums[1][q]

    block_lane = lane8 & 31
    own_block = (block_lane >= 8) & (block_lane < 16)

    def block_rows(x):
        return x.reshape(8, 8, LN).sum(axis=1)

    def edge_sums(start):
        rows = [fr[l, h, pl.ds(start, 8, stride=32), :] for l in range(NL) for h in range(2)]
        return pick_dot(jnp.concatenate(rows, axis=1), cb[...])

    c_east = edge_sums(RO + 31)
    c_east_prev = edge_sums(RO - 1)
    c_north_wide = block_rows(pick_dot(acc_n[...], cbn[...]))
    c_north = jnp.where(own_block, c_north_wide, 0.0)
    c_north_prev = jnp.where(own_block, shift(c_north_wide, 1, 1), 0.0)
    up_sink = block_rows(pick_dot(acc[...], cb[...]))
    c_up = jnp.where(lane8 < 96, up_sink, 0.0)
    c_sink = jnp.where(lane8 >= 96, up_sink, 0.0)
    c_diag = c_east + c_east_prev + c_north + c_north_prev + c_up + shift(c_up, 32, 1) + c_sink
    for q, x in enumerate((c_east, c_north, c_up, c_diag, c_sink)):
        cm[q] = x
    cm_in = {d: (k, send(cm, cmr.at[k], d)) for k, d in enumerate(DIRS)}

    def sum_along_gx(it, *tiles):
        parts = len(tiles)
        for q, x in enumerate(tiles):
            s1[it, q] = x
        span = pl.ds(0, parts)
        return [send(s1.at[it, span], ls1.at[it, d - 1, span], (d, 0)) for d in range(1, nx)]

    def sum_along_gy(it, arriving, parts):
        span = pl.ds(0, parts)
        total = [s1[it, q] for q in range(parts)]
        for d in range(1, nx):
            arriving[d - 1].wait_recv()
            for q in range(parts):
                total[q] = total[q] + ls1[it, d - 1, q]
        for q in range(parts):
            s2[it, q] = total[q]
        return [send(s2.at[it, span], ls2.at[it, d - 1, span], (0, d)) for d in range(1, ny)]

    def sum_end(it, arriving, parts):
        total = [s2[it, q] for q in range(parts)]
        for d in range(1, ny):
            arriving[d - 1].wait_recv()
            for q in range(parts):
                total[q] = total[q] + ls2[it, d - 1, q]
        return [x.sum(axis=0, keepdims=True).sum(axis=1, keepdims=True) for x in total]

    sums_gx = sum_along_gx(0, source_sum, c_diag, c_sink)

    def diagonal(base):
        here, above = pl.ds(base, 8), pl.ds(base - 1, 8)
        for l in range(NL):
            for h in range(2):
                d = fr[l, h, above, :] + fr[l, h, here, :] + fl[l, h, here, :] + fc[l, h, here, :]
                if l > 0:
                    d = d + fv[l - 1, h, here, :]
                if l < NL - 1:
                    d = d + fv[l, h, here, :]
                else:
                    d = d + snk[h, here, :]
                d = jnp.maximum(d, FACE_FLOOR)
                dg[l, h, here, :] = d
                wg[l, h, here, :] = DAMPING / d

    diagonal(RO - 8)
    diagonal(RO + N)

    @pl.loop(0, N // 32)
    def _(a):
        for k in range(4):
            diagonal(pl.multiple_of(RO + 32 * a + 8 * k, 8))

    for c in tile_in2:
        c.wait_recv()
    quarter = devices // 4
    lane_q = iota((quarter, LN), 1)
    power = jnp.zeros((quarter, LN), F32)
    ids = power
    for k in range(4):
        part = tin2[k * quarter : (k + 1) * quarter, :]
        mine = (lane_q >> 5) == k
        power = jnp.where(mine, shift(part, 32 * k, 1), power)
        ids = jnp.where(mine, shift(part, 32 * k - 32, 1), ids)
    ids = ids.astype(jnp.int32)
    powers = [part.astype(F32) for part in pieces(power, 3)]
    sub32 = iota((32, LN), 0)
    for k in range(quarter):
        span = slice(k * LN, (k + 1) * LN)
        one_id = ids[k : k + 1, :]
        dense_a[:, span] = jnp.where(sub32 == (one_id >> 5), 1.0, 0.0).astype(BF16)
        hit = sub32 == (one_id & 31)
        for q in range(3):
            dense_b[q, :, span] = jnp.where(hit, powers[q][k : k + 1, :], 0.0).astype(BF16)
    total = None
    for q in range(3):
        term = lax.dot_general(
            dense_a[...], dense_b[q], (((1,), (1,)), ((), ())), preferred_element_type=F32
        )
        total = term if total is None else total + term
    total = jnp.concatenate([total * (1.0 / 64.0), jnp.zeros((32, LN - 32), F32)], axis=1)
    total_t = jnp.concatenate([total, jnp.zeros((LN - 32, LN), F32)], axis=0).T
    sub8 = iota((8, LN), 0)

    def stack(*rows):
        out8 = zero8
        for k, x in enumerate(rows):
            out8 = jnp.where(sub8 == k, x, out8)
        return out8

    ts[...] = stack(total_t[0:1, :], total_t[31:32, :], total[0:1, :], total[31:32, :])
    th_in = {d: (k, send(ts, th.at[k], d)) for k, d in enumerate(DIRS)}
    spread_cols = jnp.where(iota((LN, N), 0) == (iota((LN, N), 1) >> 3), 1.0, 0.0).astype(BF16)
    wide = pick_dot(total, spread_cols)
    for h in range(2):
        dynr[h, 8:40, :] = wide[:, halves[h]]

    def couple(ref, base, edge, live):
        here, above, below = pl.ds(base, 8), pl.ds(base - 1, 8), pl.ds(base + 1, 8)
        res = [[None, None] for _ in range(NL)]
        mid = [[ref[l, h, here, :] for h in range(2)] for l in range(live)]
        for l in range(live):
            a0, a1 = mid[l]
            f0, f1 = fc[l, 0, here, :], fc[l, 1, here, :]
            ra0, ra1 = shift(a0, -1, 1), shift(a1, -1, 1)
            p0, p1 = shift(f0 * a0, 1, 1), shift(f1 * a1, 1, 1)
            lateral = (
                f0 * jnp.where(last_lane, ra1, ra0) + jnp.where(first_lane, edge[l], p0),
                jnp.where(last_lane, edge[l], f1 * ra1) + jnp.where(first_lane, p0, p1),
            )
            for h in range(2):
                res[l][h] = (
                    lateral[h]
                    + fr[l, h, above, :] * ref[l, h, above, :]
                    + fr[l, h, here, :] * ref[l, h, below, :]
                )
        for l in range(live):
            for h in range(2):
                for face, to in ((l - 1, l - 1), (l, l + 1)):
                    if 0 <= to < NL:
                        term = fv[face, h, here, :] * mid[l][h]
                        res[to][h] = term if res[to][h] is None else res[to][h] + term
        return mid, res

    def strip_couple(v, g, live):
        res = []
        for l in range(live):
            p, r = fcs[l, g] * v[l], frs[l, g]
            res.append(
                fcs[l, g] * shift(v[l], -1, 0) + shift(p, 1, 0) + r * shift(v[l], -1, 1) + shift(r * v[l], 1, 1)
            )
        res += [None] * (NL - live)
        for l in range(live):
            for face, to in ((l - 1, l - 1), (l, l + 1)):
                if 0 <= to < NL:
                    term = fvs[face, g] * v[l]
                    res[to] = term if res[to] is None else res[to] + term
        return res

    def dyn_rows(base, h):
        return dynr[h, pl.ds(base // 8 + 6, 1), :]

    def over_rows(body, margins=True, carry=None):
        if margins:
            body(RO - 8, None, -1, 3)
            body(RO + N, None, 8, 0)

        @pl.loop(0, N // 32)
        def _(a):
            sums = [zero8] * 8
            for k in range(4):
                body(pl.multiple_of(RO + 32 * a + 8 * k, 8), sums, a, k)
            rows = pl.ds(pl.multiple_of(a * 8, 8), 8)
            for q in range(8):
                if sums[q] is not zero8:
                    acc[rows, q * LN : (q + 1) * LN] = sums[q]

    lane16 = iota((16, LN), 1)
    lane24 = iota((24, LN), 1)

    def sweep_neighbours(x):
        return (
            coef[1] * shift(x, -1, 0) + coef[2] * shift(x, 1, 0)
            + coef[3] * shift(x, -1, 1) + coef[4] * shift(x, 1, 1)
            + coef[5] * shift(x, -32, 1) + coef[6] * shift(x, 32, 1)
        )

    def coarse_sweeps(right):
        rw = coef[0] * right
        x = rw
        for _ in range(CJ - 1):
            x = (1.0 - DAMPING) * x + rw + sweep_neighbours(x)
        return x

    def assemble(own, other):
        rows = []
        for dx in (-1, 0, 1):
            centre = own if dx == 0 else other((dx, 0))
            rows.append(centre + shift(other((dx, -1)), -8, 1) + shift(other((dx, 1)), 8, 1))
        return jnp.concatenate(rows, axis=0)

    def send_coarse(it, own):
        ct[it] = own
        return {d: (k, send(ct.at[it], nb.at[it, k], d)) for k, d in enumerate(DIRS)}

    def first_residual(base, sums, a, k):
        here = pl.ds(base, 8)
        for h in range(2):
            r = dyn_rows(base, h) + drn[h, here, :]
            src[h, here, :] = r
            r_[0, h, here, :] = r
            e1_[0, h, here, :] = wg[0, h, here, :] * r
            if sums is not None:
                sums[h] += r

    over_rows(first_residual, margins=False)
    own_c = block_rows(pick_dot(acc[:, 0 : 2 * LN], cb[0 : 2 * LN, :]))
    side = send_coarse(0, own_c)
    sums_gy = sum_along_gy(0, sums_gx, 3)

    @pl.loop(0, N // 32)
    def _(a):
        for k in range(4):
            for h in range(2):
                dyn_out[pl.ds(pl.multiple_of(a * 32 + k * 8, 8), 8), halves[h]] = jnp.broadcast_to(
                    dynr[h, pl.ds(8 + 4 * a + k, 1), :], (8, LN)
                )

    dyn_copy = pltpu.make_async_copy(dyn_out, dyn_hbm, lsem.at[0])
    dyn_copy.start()
    for _, c in th_in.values():
        c.wait_recv()

    def rim(d, k):
        return th[th_in[(-d[0], -d[1])][0], k : k + 1, :]

    wide_rims = pick_dot(stack(rim((-1, 0), 3) * edge_n, rim((1, 0), 2) * edge_s), spread_cols)
    for h in range(2):
        dynr[h, 0:8, :] = jnp.broadcast_to(wide_rims[0:1, halves[h]], (8, LN))
        dynr[h, 40:48, :] = jnp.broadcast_to(wide_rims[1:2, halves[h]], (8, LN))
    body = stack(rim((0, -1), 1), ts[0:1, :], ts[1:2, :], rim((0, 1), 0))
    top = stack(rim((-1, -1), 1), rim((-1, 0), 0), rim((-1, 0), 1), rim((-1, 1), 0))
    low = stack(rim((1, -1), 1), rim((1, 0), 0), rim((1, 0), 1), rim((1, 1), 0))
    tall = jnp.where(
        lane8 == 0,
        shift(top, -31, 1),
        jnp.where(lane8 == 33, shift(low, 33, 1), jnp.where(lane8 < 33, shift(body, 1, 1), 0.0)),
    )
    spread_rows = jnp.where(iota((LN, SL), 0) == ((iota((LN, SL), 1) - (SO - 8)) >> 3), 1.0, 0.0).astype(BF16)
    tall = pick_dot(tall, spread_rows)
    for g in sides:
        dyn_s = jnp.where(sl_row < 8, tall[2 * g : 2 * g + 1, :], tall[2 * g + 1 : 2 * g + 2, :]) * keep[g]
        dys[g] = dyn_s
        srs[g] = dyn_s + drn_s[g]
    first_residual(RO - 8, None, -1, 3)
    first_residual(RO + N, None, 8, 0)

    rs = [[srs[g] for g in sides]]
    e1s = [[wgs[0, g] * srs[g] for g in sides]]
    live = 1
    zeros_s = jnp.zeros((16, SL), F32)
    edge_terms(e1s + [[zeros_s, zeros_s]] * (NL - 1), cf_e)

    ts_old = None
    balance = diag_total = sink_total = adjoint = None
    sweeps = OUTER * INNER
    for it in range(sweeps):
        first, last = it == 0, it == sweeps - 1
        fresh = (it + 1) % INNER == 0

        def second_sweep(base, sums, a, k):
            here = pl.ds(base, 8)
            mid, res = couple(e1_, base, columns(cf_e, base), live)
            for l in range(NL):
                for h in range(2):
                    if l < live:
                        u = (1.0 - DAMPING) * mid[l][h] + wg[l, h, here, :] * (r_[l, h, here, :] + res[l][h])
                    elif res[l][h] is not None:
                        u = wg[l, h, here, :] * res[l][h]
                    else:
                        u = zero8
                    if not first:
                        u = u + t_[l, h, here, :]
                    t_[l, h, here, :] = u

        over_rows(second_sweep, margins=not last)

        if not last:
            us = [[None, None] for _ in range(NL)]
            for g in sides:
                res = strip_couple([e1s[l][g] for l in range(live)], g, live)
                for l in range(NL):
                    if l < live:
                        u = (1.0 - DAMPING) * e1s[l][g] + wgs[l, g] * (rs[l][g] + res[l])
                    elif res[l] is not None:
                        u = wgs[l, g] * res[l]
                    else:
                        u = zeros_s
                    us[l][g] = u if first else ts_old[l][g] + u
            edge_terms(us, cf_t)

            def half_residual(base, sums, a, k):
                here = pl.ds(base, 8)
                mid, res = couple(t_, base, columns(cf_t, base), NL)
                for l in range(NL):
                    for h in range(2):
                        r = res[l][h] - dg[l, h, here, :] * mid[l][h]
                        if l == 0 and not fresh:
                            r = r + src[h, here, :]
                        r_[l, h, here, :] = r
                        if sums is not None:
                            sums[2 * l + h] += r

            over_rows(half_residual)
            next_c = block_rows(pick_dot(acc[...], cb[...]))

        if first:
            for _, c in cm_in.values():
                c.wait_recv()
            w_east, w_north, w_up, w_diag, w_sink = (
                assemble(cm[q], lambda d, q=q: cmr[cm_in[(-d[0], -d[1])][0], q]) for q in range(5)
            )
            gain = jnp.where((lane24 & 31) < 24, DAMPING / jnp.maximum(w_diag, 1e-30), 0.0)
            coef[0] = gain
            coef[1] = gain * w_east
            coef[2] = gain * shift(w_east, 1, 0)
            coef[3] = gain * w_north
            coef[4] = gain * shift(w_north, 1, 1)
            coef[5] = gain * w_up
            coef[6] = gain * shift(w_up, 32, 1)
            adjoint = jnp.where(own_block, coarse_sweeps(w_sink)[8:16, :], 0.0)
        if not last and not fresh:
            next_gx = sum_along_gx(it + 1, next_c - adjoint * own_c)

        for _, c in side.values():
            c.wait_recv()
        x = coarse_sweeps(assemble(own_c, lambda d: nb[it, side[(-d[0], -d[1])][0]]))
        sums = sum_end(it, sums_gy, 3 if first else 1)
        if first:
            diag_total, sink_total = sums[1], sums[2]
        total = sums[0]
        if not first and it % INNER != 0:
            total = total - balance * sink_total
        balance = BALANCE_WEIGHT * total / diag_total
        x = x + balance

        for l in range(NL):
            for h in range(2):
                at_col = l * 32 + 8 + h * 4
                cv[l, h] = jnp.take_along_axis(x, at_col + (lane24 >> 5), axis=1)
                if not last:
                    cvr[l, h] = jnp.take_along_axis(x, at_col + ((lane24 + 1) >> 5), axis=1)
                    cvl[l, h] = jnp.take_along_axis(x, at_col + ((lane24 - 1) >> 5), axis=1)

        if last:
            writes = []
            for part in range(4):

                @pl.loop(2 * part, 2 * part + 2)
                def _(a):
                    for l in range(NL):
                        for h in range(2):
                            add = cv[l, h, pl.ds(8 + a, 1), :]
                            for k in range(4):
                                rows = pl.ds(pl.multiple_of(32 * a + 8 * k, 8), 8)
                                here = pl.ds(pl.multiple_of(RO + 32 * a + 8 * k, 8), 8)
                                out[l, rows, halves[h]] = t_[l, h, here, :] + add

                span = pl.ds(64 * part, 64)
                writes.append(
                    pltpu.make_async_copy(out.at[:, span, :], out_hbm.at[:, span, :], lsem.at[3 + part])
                )
                writes[-1].start()
            break

        if fresh:

            def new_source(base, sums, a, k):
                here = pl.ds(base, 8)
                for h in range(2):
                    u = t_[0, h, here, :] + cv[0, h, pl.ds(8 + a, 1), :]
                    s = dyn_rows(base, h) + drn[h, here, :] * jnp.exp(DRAIN_SLOPE * u)
                    src[h, here, :] = s
                    if sums is not None:
                        sums[h] += s

            over_rows(new_source)
            next_c = next_c + block_rows(pick_dot(acc[:, 0 : 2 * LN], cb[0 : 2 * LN, :]))
        moved = (x - sweep_neighbours(x) * (1.0 / DAMPING))[8:16, :] * c_diag
        own_c = next_c - jnp.where(own_block, moved, 0.0)
        side = send_coarse(it + 1, own_c)
        sums_gx = sum_along_gx(it + 1, own_c) if fresh else next_gx

        def whole_residual(base, sums, a, k):
            here, above = pl.ds(base, 8), pl.ds(base - 1, 8)
            block = pl.ds(8 + a, 1)
            xs = [[cv[l, h, block, :] for h in range(2)] for l in range(NL)]
            for h in range(2):
                flow = None
                for l in range(NL):
                    v = xs[l][h]
                    t_[l, h, here, :] = t_[l, h, here, :] + v
                    r = r_[l, h, here, :]
                    if l == 0 and fresh:
                        r = r + src[h, here, :]
                    r = r - fc[l, h, here, :] * (v - cvr[l, h, block, :])
                    r = r - fl[l, h, here, :] * (v - cvl[l, h, block, :])
                    if k == 0:
                        step = v - cv[l, h, pl.ds(7 + a, 1), :]
                        r = r - jnp.where(sub8 == 0, fr[l, h, above, :] * step, 0.0)
                    if k == 3:
                        step = v - cv[l, h, pl.ds(9 + a, 1), :]
                        r = r - jnp.where(sub8 == 7, fr[l, h, here, :] * step, 0.0)
                    if l > 0:
                        r = r + flow
                    if l < NL - 1:
                        flow = fv[l, h, here, :] * (v - xs[l + 1][h])
                        r = r - flow
                    else:
                        r = r - snk[h, here, :] * v
                    r_[l, h, here, :] = r
                    e1_[l, h, here, :] = wg[l, h, here, :] * r

        over_rows(whole_residual)

        xt[...] = jnp.concatenate([x, jnp.zeros((LN - 24, LN), F32)], axis=0).T
        picked = jnp.concatenate(
            [xt[l * 32 + c : l * 32 + c + 1, :] for l in range(NL) for c in (7, 8, 15, 16)], axis=0
        )
        picked = jnp.concatenate(
            [jnp.take_along_axis(picked, 6 + 4 * k + (lane16 >> 5), axis=1) for k in range(SL // LN)], axis=1
        )
        live = NL
        ts_old = [[None, None] for _ in range(NL)]
        rs = [[None, None] for _ in range(NL)]
        e1s = [[None, None] for _ in range(NL)]
        for g in sides:
            for l in range(NL):
                k = 4 * l + 2 * g
                ts_old[l][g] = us[l][g] + jnp.where(sl_row < 8, picked[k : k + 1, :], picked[k + 1 : k + 2, :])
            if fresh:
                srs[g] = dys[g] + drn_s[g] * jnp.exp(DRAIN_SLOPE * ts_old[0][g])
            res = strip_couple([ts_old[l][g] for l in range(NL)], g, NL)
            for l in range(NL):
                r = res[l] - dgs[l, g] * ts_old[l][g]
                if l == 0:
                    r = r + srs[g]
                rs[l][g] = r
                e1s[l][g] = wgs[l, g] * r
        edge_terms(e1s, cf_e)
        sums_gy = sum_along_gy(it + 1, sums_gx, 1)

    for c in started:
        c.wait_send()
    dyn_copy.wait()
    for c in writes:
        c.wait()


def hand_over(a, b, to_a, to_b, sem):
    copies = [
        pltpu.make_async_copy(a.at[l], to_a.at[l], sem.at[l]) for l in range(NL)
    ] + [pltpu.make_async_copy(b, to_b, sem.at[NL])]
    for c in copies:
        c.start()
    for c in copies:
        c.wait()


def n_copies(nx, ny):
    setup = (ny - 1) + 2 + 6 + 2 + (nx - 1) + 8 + 8
    return setup + OUTER * INNER * (8 + (nx - 1) + (ny - 1))


def solution(mesh):
    nx, ny = mesh.shape["gx"], mesh.shape["gy"]
    its = OUTER * INNER
    devices = nx * ny

    def step(material, material_table, sink_cond, drain_current, instance_tile, instance_power):
        n_inst = instance_tile.shape[0]
        field = pltpu.VMEM((NL, 2, NR, LN), F32)
        single = pltpu.VMEM((2, NR, LN), F32)
        vm = lambda *shape: pltpu.VMEM(shape, F32)
        half = lambda *shape: pltpu.VMEM(shape, BF16)
        copies = n_copies(nx, ny)
        scratch = [
            pltpu.VMEM((NL, N, N), jnp.int32), vm(N, N), vm(N, N), vm(NL, N, N), vm(N, N),
            field, field, field, field, field, pltpu.VMEM((NL - 1, 2, NR, LN), F32), field, field,
            single, single, single, field, field, field,
            vm(SL, LN), vm(SL, LN), vm(SL, LN), vm(64, 8 * LN), vm(64, 8 * LN), vm(SL, LN),
            half(8 * LN, LN), half(8 * LN, LN),
            half(devices, n_inst), half(3, 64, n_inst), vm(devices, LN), vm(devices, LN),
            vm(nx, ny, LN), vm(devices, LN), half(32, 32 * devices), half(3, 32, 32 * devices),
            vm(8, LN), vm(8, 8, LN), vm(2, 48, LN),
            vm(2, NQ, 2, 8, LN), vm(2, NQ, 2, 8, LN), vm(2, 8, LN), vm(6, 8, LN),
            vm(2, 8 * NQ, SL), vm(2, 8 * NQ, SL),
            vm(NL, 2, 16, SL), vm(NL, 2, 16, SL), vm(NL - 1, 2, 16, SL), vm(NL, 2, 16, SL), vm(NL, 2, 16, SL),
            vm(2, 16, SL), vm(2, 16, SL), vm(2, 16, SL),
            vm(5, 8, LN), vm(8, 5, 8, LN), vm(7, 24, LN), vm(its, 8, LN), vm(its, 8, 8, LN),
            vm(its, 3, 8, LN), vm(its, nx - 1, 3, 8, LN), vm(its, 3, 8, LN), vm(its, ny - 1, 3, 8, LN),
            vm(NL, 2, 24, LN), vm(NL, 2, 24, LN), vm(NL, 2, 24, LN), vm(LN, LN),
            pltpu.SemaphoreType.DMA((copies,)), pltpu.SemaphoreType.DMA((copies,)), pltpu.SemaphoreType.DMA((7,)),
        ]
        vmem = pl.BlockSpec(memory_space=pltpu.VMEM)
        smem = pl.BlockSpec(memory_space=pltpu.SMEM)
        hbm = pl.BlockSpec(memory_space=pl.ANY)
        shapes = (jax.ShapeDtypeStruct((NL, N, N), F32), jax.ShapeDtypeStruct((N, N), F32))
        results = pl.pallas_call(
            functools.partial(kernel, nx, ny),
            out_shape=shapes,
            in_specs=[hbm, smem, hbm, hbm, vmem, vmem],
            out_specs=(hbm, hbm),
            scratch_shapes=scratch,
            compiler_params=pltpu.CompilerParams(
                collective_id=0, has_side_effects=True, vmem_limit_bytes=56 * 1024 * 1024
            ),
        )(
            material,
            material_table,
            sink_cond,
            drain_current,
            instance_tile.reshape(n_inst // LN, LN),
            instance_power.reshape(n_inst // LN, LN),
        )
        return pl.pallas_call(
            hand_over,
            out_shape=shapes,
            in_specs=[vmem, vmem],
            out_specs=(hbm, hbm),
            scratch_shapes=[pltpu.SemaphoreType.DMA((NL + 1,))],
        )(*results)

    return jax.shard_map(
        step,
        mesh=mesh,
        in_specs=(
            P(None, "gx", "gy"),
            P(),
            P("gx", "gy"),
            P("gx", "gy"),
            P(("gx", "gy")),
            P(("gx", "gy")),
        ),
        out_specs=(P(None, "gx", "gy"), P("gx", "gy")),
        check_vma=False,
    )
```

time: 65.4 us -> 61.1 us (0.934)
  Pallas kernels: 64.6 us -> 60.3 us
    pallas_call x1, Pallas kernels: 62.2 us -> 58 us  [step(): pl.pallas_call(functools.partial(kernel, nx, ny), out_shape=shapes, in_sp...]
where the time goes in v3:
time: 61.1 us; the launch traced here: 61 us
  Pallas kernels  60.3 us (99%)
  between operations  0.64 us (1%)
    pallas_call x1, Pallas kernels, step(): pl.pallas_call(functools.partial(kernel, nx, ny), out_shape=shapes, in_sp...  58 us
    pallas_call x1, Pallas kernels, step(): pl.pallas_call(hand_over, out_shape=shapes, in_specs=[vmem, vmem], out_sp...  2.36 us

profile of v3, /device:TPU:1, one launch (start us, length us, event | category | flops | bytes accessed | tf_op | source)
XLA Modules:
  0.0 61.0 jit_solution(12362490532568351920)
XLA Ops:
  0.6 58.0 %shard_map.77 = (f32[4,256,256]{2,1,0:T(8,128)}, f32[256,256]{1,0:T(8,128)}) custom-call(s32[4,256,256]{2,1,0:T(8,128)} %refs_0_.1, f32[2,16]{1,0:T(2,128)} %refs_1_.1, f32[256,256]{1,0:T(8,128)} %refs_2_.1, f32[256,256]{1,0:T(8,128)} %refs_3_.1, s32[16,128]{1,0:T(8,128)} %bitcast.2, f32[16,128]{1,0:T(8,128)} %bitcast.3), custom_call_target="tpu_custom_call" | custom-call | tf_op jit(solution)/shard_map/pallas_call | solution.py:916
  58.6 2.4 %shard_map.78 = (f32[4,256,256]{2,1,0:T(8,128)}, f32[256,256]{1,0:T(8,128)}) custom-call(f32[4,256,256]{2,1,0:T(8,128)} %get-tuple-element.4.a, f32[256,256]{1,0:T(8,128)} %get-tuple-element.5.b), custom_call_target="tpu_custom_call" | custom-call | tf_op jit(solution)/shard_map/pallas_call | solution.py:933

commit v4 on v3

--- a/solution.py
+++ b/solution.py
@@ -80,14 +80,14 @@
 
 
 def kernel(nx, ny, *refs):
-    (mat_hbm, tab, sink_hbm, drain_hbm, inst_tile, inst_power, out_hbm, dyn_hbm) = refs[:8]
+    (mat_hbm, tab_hbm, sink_hbm, drain_hbm, tile_hbm, power_hbm, out, dyn_out) = refs[:8]
     (
-        mat, sink, drain, out, dyn_out,
+        mat, sink, drain, tab, inst_tile, inst_power,
         lat, ver, fr, fc, fl, fv, dg, wg, src, drn, snk, t_, r_, e1_,
         cf_t, cf_e, cf_f, acc, acc_n, pk, cb, cbn,
         dest, slots, sout, tin1, tred, tin2, dense_a, dense_b, ts, th, dynr,
         sq_row, rq_row, sq_c, rq_c, sq_s, rq_s,
-        fcs, frs, fvs, dgs, wgs, drn_s, dys, srs,
+        fcs, frs, fvs, dgs, wgs, drn_s, dys, srs, sks, gs, gr,
         cm, cmr, coef, ct, nb, s1, ls1, s2, ls2, cv, cvr, cvl, xt,
         ssem, rsem, lsem,
     ) = refs[8:]
@@ -95,6 +95,13 @@
 
     def at(dx, dy):
         return {"gx": lax.rem(mx + (dx + nx), nx), "gy": lax.rem(my + (dy + ny), ny)}
+
+    fetch_small = [
+        pltpu.make_async_copy(a, b, lsem.at[3 + k])
+        for k, (a, b) in enumerate(((tile_hbm, inst_tile), (power_hbm, inst_power), (tab_hbm, tab)))
+    ]
+    for c in fetch_small:
+        c.start()
 
     partners = [(d, 0) for d in range(1, nx)] + [(0, d) for d in range(1, ny)] + list(DIAG)
     barrier = pltpu.get_barrier_semaphore()
@@ -128,6 +135,8 @@
 
     devices = nx * ny
     chunks = inst_tile.shape[0]
+    for c in fetch_small:
+        c.wait()
     sub_d = iota((devices, LN), 0)
     lane_d = iota((devices, LN), 1)
     up_to = jnp.where(iota((LN, LN), 0) <= iota((LN, LN), 1), 1.0, 0.0).astype(BF16)
@@ -226,25 +235,26 @@
     table = [[tab[q, k] for k in range(16)] for q in range(2)]
 
     zero8 = jnp.zeros((8, LN), F32)
-    for ref, places in ((t_, (0, NR - 8)), (e1_, (0, NR - 8)), (fr, (0,)), (lat, (NR - 8,))):
+    for ref, places in ((t_, (0, NR - 8)), (e1_, (0, 8, NR - 16, NR - 8)), (fr, (0,)), (lat, (NR - 8,))):
         for l in range(NL):
             for h in range(2):
                 for place in places:
                     ref[l, h, place : place + 8, :] = zero8
 
-    @pl.loop(0, N // 8, init_carry=power_sum)
-    def source_sum(k, source_sum):
-        rows = pl.ds(pl.multiple_of(k * 8, 8), 8)
-        into = pl.ds(pl.multiple_of(k * 8 + RO, 8), 8)
-        for h in range(2):
-            for l in range(NL):
-                ids = mat[l, rows, halves[h]]
-                lat[l, h, into, :] = lookup(ids, table[0])
-                ver[l, h, into, :] = lookup(ids, table[1])
-            snk[h, into, :] = sink[rows, halves[h]]
-            d = drain[rows, halves[h]]
-            drn[h, into, :] = d
-            source_sum = source_sum + d
+    @pl.loop(0, N // 32, init_carry=power_sum)
+    def source_sum(a, source_sum):
+        for k in range(4):
+            rows = pl.ds(pl.multiple_of(a * 32 + k * 8, 8), 8)
+            into = pl.ds(pl.multiple_of(a * 32 + k * 8 + RO, 8), 8)
+            for h in range(2):
+                for l in range(NL):
+                    ids = mat[l, rows, halves[h]]
+                    lat[l, h, into, :] = lookup(ids, table[0])
+                    ver[l, h, into, :] = lookup(ids, table[1])
+                snk[h, into, :] = sink[rows, halves[h]]
+                d = drain[rows, halves[h]]
+                drn[h, into, :] = d
+                source_sum = source_sum + d
         return source_sum
 
     for c in tile_in:
@@ -320,6 +330,7 @@
             lats.append(lookup(ids, table[0]) * keep[g])
             vers.append(lookup(ids, table[1]) * keep[g])
         sink_s = raw_strip(4, g) * keep[g]
+        sks[g] = sink_s
         drn_s[g] = raw_strip(5, g) * keep[g]
         up = None
         for l in range(NL):
@@ -345,7 +356,8 @@
     def column_form(west, east, ref):
         z = jnp.zeros((8, SL), F32)
         for l in range(NL):
-            z = jnp.where(row_z == 2 * l + 1, west[l], jnp.where(row_z == 2 * l, east[l], z))
+            if west[l] is not None:
+                z = jnp.where(row_z == 2 * l + 1, west[l], jnp.where(row_z == 2 * l, east[l], z))
         for k in range(SL // LN):
             block = jnp.concatenate([z[:, k * LN : (k + 1) * LN], jnp.zeros((LN - 8, LN), F32)], axis=0)
             ref[k * LN : (k + 1) * LN, :] = block.T
@@ -403,80 +415,6 @@
         for q in range(8):
             acc_n[rows, q * LN : (q + 1) * LN] = sums[0][q]
             acc[rows, q * LN : (q + 1) * LN] = sums[1][q]
-
-    block_lane = lane8 & 31
-    own_block = (block_lane >= 8) & (block_lane < 16)
-
-    def block_rows(x):
-        return x.reshape(8, 8, LN).sum(axis=1)
-
-    def edge_sums(start):
-        rows = [fr[l, h, pl.ds(start, 8, stride=32), :] for l in range(NL) for h in range(2)]
-        return pick_dot(jnp.concatenate(rows, axis=1), cb[...])
-
-    c_east = edge_sums(RO + 31)
-    c_east_prev = edge_sums(RO - 1)
-    c_north_wide = block_rows(pick_dot(acc_n[...], cbn[...]))
-    c_north = jnp.where(own_block, c_north_wide, 0.0)
-    c_north_prev = jnp.where(own_block, shift(c_north_wide, 1, 1), 0.0)
-    up_sink = block_rows(pick_dot(acc[...], cb[...]))
-    c_up = jnp.where(lane8 < 96, up_sink, 0.0)
-    c_sink = jnp.where(lane8 >= 96, up_sink, 0.0)
-    c_diag = c_east + c_east_prev + c_north + c_north_prev + c_up + shift(c_up, 32, 1) + c_sink
-    for q, x in enumerate((c_east, c_north, c_up, c_diag, c_sink)):
-        cm[q] = x
-    cm_in = {d: (k, send(cm, cmr.at[k], d)) for k, d in enumerate(DIRS)}
-
-    def sum_along_gx(it, *tiles):
-        parts = len(tiles)
-        for q, x in enumerate(tiles):
-            s1[it, q] = x
-        span = pl.ds(0, parts)
-        return [send(s1.at[it, span], ls1.at[it, d - 1, span], (d, 0)) for d in range(1, nx)]
-
-    def sum_along_gy(it, arriving, parts):
-        span = pl.ds(0, parts)
-        total = [s1[it, q] for q in range(parts)]
-        for d in range(1, nx):
-            arriving[d - 1].wait_recv()
-            for q in range(parts):
-                total[q] = total[q] + ls1[it, d - 1, q]
-        for q in range(parts):
-            s2[it, q] = total[q]
-        return [send(s2.at[it, span], ls2.at[it, d - 1, span], (0, d)) for d in range(1, ny)]
-
-    def sum_end(it, arriving, parts):
-        total = [s2[it, q] for q in range(parts)]
-        for d in range(1, ny):
-            arriving[d - 1].wait_recv()
-            for q in range(parts):
-                total[q] = total[q] + ls2[it, d - 1, q]
-        return [x.sum(axis=0, keepdims=True).sum(axis=1, keepdims=True) for x in total]
-
-    sums_gx = sum_along_gx(0, source_sum, c_diag, c_sink)
-
-    def diagonal(base):
-        here, above = pl.ds(base, 8), pl.ds(base - 1, 8)
-        for l in range(NL):
-            for h in range(2):
-                d = fr[l, h, above, :] + fr[l, h, here, :] + fl[l, h, here, :] + fc[l, h, here, :]
-                if l > 0:
-                    d = d + fv[l - 1, h, here, :]
-                if l < NL - 1:
-                    d = d + fv[l, h, here, :]
-                else:
-                    d = d + snk[h, here, :]
-                d = jnp.maximum(d, FACE_FLOOR)
-                dg[l, h, here, :] = d
-                wg[l, h, here, :] = DAMPING / d
-
-    diagonal(RO - 8)
-    diagonal(RO + N)
-
-    @pl.loop(0, N // 32)
-    def _(a):
-        for k in range(4):
-            diagonal(pl.multiple_of(RO + 32 * a + 8 * k, 8))
 
     for c in tile_in2:
         c.wait_recv()
@@ -522,6 +460,80 @@
     for h in range(2):
         dynr[h, 8:40, :] = wide[:, halves[h]]
 
+    block_lane = lane8 & 31
+    own_block = (block_lane >= 8) & (block_lane < 16)
+
+    def block_rows(x):
+        return x.reshape(8, 8, LN).sum(axis=1)
+
+    def edge_sums(start):
+        rows = [fr[l, h, pl.ds(start, 8, stride=32), :] for l in range(NL) for h in range(2)]
+        return pick_dot(jnp.concatenate(rows, axis=1), cb[...])
+
+    c_east = edge_sums(RO + 31)
+    c_east_prev = edge_sums(RO - 1)
+    c_north_wide = block_rows(pick_dot(acc_n[...], cbn[...]))
+    c_north = jnp.where(own_block, c_north_wide, 0.0)
+    c_north_prev = jnp.where(own_block, shift(c_north_wide, 1, 1), 0.0)
+    up_sink = block_rows(pick_dot(acc[...], cb[...]))
+    c_up = jnp.where(lane8 < 96, up_sink, 0.0)
+    c_sink = jnp.where(lane8 >= 96, up_sink, 0.0)
+    c_diag = c_east + c_east_prev + c_north + c_north_prev + c_up + shift(c_up, 32, 1) + c_sink
+    for q, x in enumerate((c_east, c_north, c_up, c_diag, c_sink)):
+        cm[q] = x
+    cm_in = {d: (k, send(cm, cmr.at[k], d)) for k, d in enumerate(DIRS)}
+
+    def sum_along_gx(it, *tiles):
+        parts = len(tiles)
+        for q, x in enumerate(tiles):
+            s1[it, q] = x
+        span = pl.ds(0, parts)
+        return [send(s1.at[it, span], ls1.at[it, d - 1, span], (d, 0)) for d in range(1, nx)]
+
+    def sum_along_gy(it, arriving, parts):
+        span = pl.ds(0, parts)
+        total = [s1[it, q] for q in range(parts)]
+        for d in range(1, nx):
+            arriving[d - 1].wait_recv()
+            for q in range(parts):
+                total[q] = total[q] + ls1[it, d - 1, q]
+        for q in range(parts):
+            s2[it, q] = total[q]
+        return [send(s2.at[it, span], ls2.at[it, d - 1, span], (0, d)) for d in range(1, ny)]
+
+    def sum_end(it, arriving, parts):
+        total = [s2[it, q] for q in range(parts)]
+        for d in range(1, ny):
+            arriving[d - 1].wait_recv()
+            for q in range(parts):
+                total[q] = total[q] + ls2[it, d - 1, q]
+        return [x.sum(axis=0, keepdims=True).sum(axis=1, keepdims=True) for x in total]
+
+    sums_gx = sum_along_gx(0, source_sum, c_diag, c_sink)
+
+    def diagonal(base):
+        here, above = pl.ds(base, 8), pl.ds(base - 1, 8)
+        for l in range(NL):
+            for h in range(2):
+                d = fr[l, h, above, :] + fr[l, h, here, :] + fl[l, h, here, :] + fc[l, h, here, :]
+                if l > 0:
+                    d = d + fv[l - 1, h, here, :]
+                if l < NL - 1:
+                    d = d + fv[l, h, here, :]
+                else:
+                    d = d + snk[h, here, :]
+                d = jnp.maximum(d, FACE_FLOOR)
+                dg[l, h, here, :] = d
+                wg[l, h, here, :] = DAMPING / d
+
+    diagonal(RO - 8)
+    diagonal(RO + N)
+
+    @pl.loop(0, N // 32)
+    def _(a):
+        for k in range(4):
+            diagonal(pl.multiple_of(RO + 32 * a + 8 * k, 8))
+
     def couple(ref, base, edge, live):
         here, above, below = pl.ds(base, 8), pl.ds(base - 1, 8), pl.ds(base + 1, 8)
         res = [[None, None] for _ in range(NL)]
@@ -572,15 +584,16 @@
             body(RO - 8, None, -1, 3)
             body(RO + N, None, 8, 0)
 
-        @pl.loop(0, N // 32)
-        def _(a):
-            sums = [zero8] * 8
-            for k in range(4):
-                body(pl.multiple_of(RO + 32 * a + 8 * k, 8), sums, a, k)
-            rows = pl.ds(pl.multiple_of(a * 8, 8), 8)
-            for q in range(8):
-                if sums[q] is not zero8:
-                    acc[rows, q * LN : (q + 1) * LN] = sums[q]
+        @pl.loop(0, N // 64)
+        def _(pair):
+            for a in (2 * pair, 2 * pair + 1):
+                sums = [zero8] * 8
+                for k in range(4):
+                    body(pl.multiple_of(RO + 32 * a + 8 * k, 8), sums, a, k)
+                rows = pl.ds(pl.multiple_of(a * 8, 8), 8)
+                for q in range(8):
+                    if sums[q] is not zero8:
+                        acc[rows, q * LN : (q + 1) * LN] = sums[q]
 
     lane16 = iota((16, LN), 1)
     lane24 = iota((24, LN), 1)
@@ -623,6 +636,60 @@
     over_rows(first_residual, margins=False)
     own_c = block_rows(pick_dot(acc[:, 0 : 2 * LN], cb[0 : 2 * LN, :]))
     side = send_coarse(0, own_c)
+
+    def second_sweep(base, live, edge, first):
+        here = pl.ds(base, 8)
+        mid, res = couple(e1_, base, edge, live)
+        for l in range(NL):
+            for h in range(2):
+                if l < live:
+                    u = (1.0 - DAMPING) * mid[l][h] + wg[l, h, here, :] * (r_[l, h, here, :] + res[l][h])
+                elif res[l][h] is not None:
+                    u = wg[l, h, here, :] * res[l][h]
+                else:
+                    u = zero8
+                if not first:
+                    u = u + t_[l, h, here, :]
+                t_[l, h, here, :] = u
+
+    over_rows(lambda base, sums, a, k: second_sweep(base, 1, [zero8], True), margins=False)
+
+    snk_e1 = [wgs[NL - 1, g] * sks[g] for g in sides]
+    column_form(
+        [None] * (NL - 1) + [(fcs[NL - 1, 0] * snk_e1[0])[7:8, :]],
+        [None] * (NL - 1) + [fcs[NL - 1, 1][7:8, :] * snk_e1[1][8:9, :]],
+        cf_t,
+    )
+
+    def sink_first(base, sums, a, k):
+        here = pl.ds(base, 8)
+        for h in range(2):
+            gs[h, here, :] = wg[NL - 1, h, here, :] * snk[h, here, :]
+
+    over_rows(sink_first)
+
+    def sink_second(base, sums, a, k):
+        here, above, below = pl.ds(base, 8), pl.ds(base - 1, 8), pl.ds(base + 1, 8)
+        top = NL - 1
+        edge = columns(cf_t, base)[top]
+        a0, a1 = gs[0, here, :], gs[1, here, :]
+        f0, f1 = fc[top, 0, here, :], fc[top, 1, here, :]
+        ra0, ra1 = shift(a0, -1, 1), shift(a1, -1, 1)
+        p0, p1 = shift(f0 * a0, 1, 1), shift(f1 * a1, 1, 1)
+        lateral = (
+            f0 * jnp.where(last_lane, ra1, ra0) + jnp.where(first_lane, edge, p0),
+            jnp.where(last_lane, edge, f1 * ra1) + jnp.where(first_lane, p0, p1),
+        )
+        for h, e in ((0, a0), (1, a1)):
+            flow = (
+                lateral[h]
+                + fr[top, h, above, :] * gs[h, above, :]
+                + fr[top, h, here, :] * gs[h, below, :]
+            )
+            gr[1, h, here, :] = (1.0 - DAMPING) * e + wg[top, h, here, :] * (snk[h, here, :] + flow)
+            gr[0, h, here, :] = wg[top - 1, h, here, :] * (fv[top - 1, h, here, :] * e)
+
+    over_rows(sink_second, margins=False)
     sums_gy = sum_along_gy(0, sums_gx, 3)
 
     @pl.loop(0, N // 32)
@@ -632,9 +699,6 @@
                 dyn_out[pl.ds(pl.multiple_of(a * 32 + k * 8, 8), 8), halves[h]] = jnp.broadcast_to(
                     dynr[h, pl.ds(8 + 4 * a + k, 1), :], (8, LN)
                 )
-
-    dyn_copy = pltpu.make_async_copy(dyn_out, dyn_hbm, lsem.at[0])
-    dyn_copy.start()
     for _, c in th_in.values():
         c.wait_recv()
 
@@ -667,30 +731,50 @@
     live = 1
     zeros_s = jnp.zeros((16, SL), F32)
     edge_terms(e1s + [[zeros_s, zeros_s]] * (NL - 1), cf_e)
+    second_sweep(RO - 8, 1, columns(cf_e, RO - 8), True)
+    second_sweep(RO + N, 1, columns(cf_e, RO + N), True)
+
+    def over_edges(base, sums, a, k):
+        here = pl.ds(base, 8)
+        edge = columns(cf_e, base)[0]
+        for h, lane in ((0, first_lane), (1, last_lane)):
+            t_[0, h, here, :] = t_[0, h, here, :] + jnp.where(lane, wg[0, h, here, :] * edge, 0.0)
+
+    over_rows(over_edges, margins=False)
+    for h in range(2):
+        for row, beyond, face in ((RO, RO - 1, RO - 1), (RO + N - 1, RO + N, RO + N - 1)):
+            t_[0, h, row : row + 1, :] = t_[0, h, row : row + 1, :] + wg[0, h, row : row + 1, :] * (
+                fr[0, h, face : face + 1, :] * e1_[0, h, beyond : beyond + 1, :]
+            )
+
+    for _, c in cm_in.values():
+        c.wait_recv()
+    w_east, w_north, w_up, w_diag, w_sink = (
+        assemble(cm[q], lambda d, q=q: cmr[cm_in[(-d[0], -d[1])][0], q]) for q in range(5)
+    )
+    gain = jnp.where((lane24 & 31) < 24, DAMPING / jnp.maximum(w_diag, 1e-30), 0.0)
+    coef[0] = gain
+    coef[1] = gain * w_east
+    coef[2] = gain * shift(w_east, 1, 0)
+    coef[3] = gain * w_north
+    coef[4] = gain * shift(w_north, 1, 1)
+    coef[5] = gain * w_up
+    coef[6] = gain * shift(w_up, 32, 1)
+    adjoint = coarse_sweeps(w_sink)
+    own_adjoint = jnp.where(own_block, adjoint[8:16, :], 0.0)
+    sums_gx = sum_along_gx(1, own_adjoint * own_c)
 
     ts_old = None
-    balance = diag_total = sink_total = adjoint = None
+    balance = diag_total = sink_total = source_total = None
     sweeps = OUTER * INNER
     for it in range(sweeps):
         first, last = it == 0, it == sweeps - 1
         fresh = (it + 1) % INNER == 0
 
-        def second_sweep(base, sums, a, k):
-            here = pl.ds(base, 8)
-            mid, res = couple(e1_, base, columns(cf_e, base), live)
-            for l in range(NL):
-                for h in range(2):
-                    if l < live:
-                        u = (1.0 - DAMPING) * mid[l][h] + wg[l, h, here, :] * (r_[l, h, here, :] + res[l][h])
-                    elif res[l][h] is not None:
-                        u = wg[l, h, here, :] * res[l][h]
-                    else:
-                        u = zero8
-                    if not first:
-                        u = u + t_[l, h, here, :]
-                    t_[l, h, here, :] = u
-
-        over_rows(second_sweep, margins=not last)
+        if not first:
+            over_rows(
+                lambda base, sums, a, k: second_sweep(base, NL, columns(cf_e, base), False), margins=not last
+            )
 
         if not last:
             us = [[None, None] for _ in range(NL)]
@@ -719,37 +803,25 @@
                             sums[2 * l + h] += r
 
             over_rows(half_residual)
+            if it == 2:
+                sums_gy = sum_along_gy(2, sums_gx, 2)
             next_c = block_rows(pick_dot(acc[...], cb[...]))
-
-        if first:
-            for _, c in cm_in.values():
-                c.wait_recv()
-            w_east, w_north, w_up, w_diag, w_sink = (
-                assemble(cm[q], lambda d, q=q: cmr[cm_in[(-d[0], -d[1])][0], q]) for q in range(5)
-            )
-            gain = jnp.where((lane24 & 31) < 24, DAMPING / jnp.maximum(w_diag, 1e-30), 0.0)
-            coef[0] = gain
-            coef[1] = gain * w_east
-            coef[2] = gain * shift(w_east, 1, 0)
-            coef[3] = gain * w_north
-            coef[4] = gain * shift(w_north, 1, 1)
-            coef[5] = gain * w_up
-            coef[6] = gain * shift(w_up, 32, 1)
-            adjoint = jnp.where(own_block, coarse_sweeps(w_sink)[8:16, :], 0.0)
-        if not last and not fresh:
-            next_gx = sum_along_gx(it + 1, next_c - adjoint * own_c)
 
         for _, c in side.values():
             c.wait_recv()
         x = coarse_sweeps(assemble(own_c, lambda d: nb[it, side[(-d[0], -d[1])][0]]))
-        sums = sum_end(it, sums_gy, 3 if first else 1)
         if first:
-            diag_total, sink_total = sums[1], sums[2]
-        total = sums[0]
-        if not first and it % INNER != 0:
-            total = total - balance * sink_total
-        balance = BALANCE_WEIGHT * total / diag_total
-        x = x + balance
+            source_total, diag_total, sink_total = sum_end(0, sums_gy, 3)
+        elif it == 1:
+            source_total = source_total - sum_end(1, sums_gy, 1)[0] - balance * sink_total
+        elif last:
+            source_total, less = sum_end(2, sums_gy, 2)
+            former = BALANCE_WEIGHT * source_total / diag_total
+            source_total = source_total - less - former * sink_total
+            x = x + former * (1.0 - adjoint)
+        if it != 2:
+            balance = BALANCE_WEIGHT * source_total / diag_total
+            x = x + balance
 
         for l in range(NL):
             for h in range(2):
@@ -760,24 +832,20 @@
                     cvl[l, h] = jnp.take_along_axis(x, at_col + ((lane24 - 1) >> 5), axis=1)
 
         if last:
-            writes = []
-            for part in range(4):
-
-                @pl.loop(2 * part, 2 * part + 2)
-                def _(a):
-                    for l in range(NL):
-                        for h in range(2):
-                            add = cv[l, h, pl.ds(8 + a, 1), :]
-                            for k in range(4):
-                                rows = pl.ds(pl.multiple_of(32 * a + 8 * k, 8), 8)
-                                here = pl.ds(pl.multiple_of(RO + 32 * a + 8 * k, 8), 8)
-                                out[l, rows, halves[h]] = t_[l, h, here, :] + add
-
-                span = pl.ds(64 * part, 64)
-                writes.append(
-                    pltpu.make_async_copy(out.at[:, span, :], out_hbm.at[:, span, :], lsem.at[3 + part])
-                )
-                writes[-1].start()
+
+            @pl.loop(0, N // 32)
+            def _(a):
+                for l in range(NL):
+                    for h in range(2):
+                        add = cv[l, h, pl.ds(8 + a, 1), :]
+                        for k in range(4):
+                            rows = pl.ds(pl.multiple_of(32 * a + 8 * k, 8), 8)
+                            here = pl.ds(pl.multiple_of(RO + 32 * a + 8 * k, 8), 8)
+                            u = t_[l, h, here, :] + add
+                            if l >= NL - 2:
+                                u = u - former * gr[l - (NL - 2), h, here, :]
+                            out[l, rows, halves[h]] = u
+
             break
 
         if fresh:
@@ -796,7 +864,8 @@
         moved = (x - sweep_neighbours(x) * (1.0 / DAMPING))[8:16, :] * c_diag
         own_c = next_c - jnp.where(own_block, moved, 0.0)
         side = send_coarse(it + 1, own_c)
-        sums_gx = sum_along_gx(it + 1, own_c) if fresh else next_gx
+        if first:
+            sums_gy = sum_along_gy(1, sums_gx, 1)
 
         def whole_residual(base, sums, a, k):
             here, above = pl.ds(base, 8), pl.ds(base - 1, 8)
@@ -827,8 +896,15 @@
                         r = r - snk[h, here, :] * v
                     r_[l, h, here, :] = r
                     e1_[l, h, here, :] = wg[l, h, here, :] * r
+                    if it == 1 and l >= NL - 2 and sums is not None:
+                        sums[0] += gr[l - (NL - 2), h, here, :] * r
 
         over_rows(whole_residual)
+        if it == 1:
+            response = acc[0:8, 0:LN]
+            for a in range(1, 8):
+                response = response + acc[8 * a : 8 * a + 8, 0:LN]
+            sums_gx = sum_along_gx(2, own_c, response + own_adjoint * own_c)
 
         xt[...] = jnp.concatenate([x, jnp.zeros((LN - 24, LN), F32)], axis=0).T
         picked = jnp.concatenate(
@@ -855,13 +931,9 @@
                 rs[l][g] = r
                 e1s[l][g] = wgs[l, g] * r
         edge_terms(e1s, cf_e)
-        sums_gy = sum_along_gy(it + 1, sums_gx, 1)
 
     for c in started:
         c.wait_send()
-    dyn_copy.wait()
-    for c in writes:
-        c.wait()
 
 
 def hand_over(a, b, to_a, to_b, sem):
@@ -876,7 +948,7 @@
 
 def n_copies(nx, ny):
     setup = (ny - 1) + 2 + 6 + 2 + (nx - 1) + 8 + 8
-    return setup + OUTER * INNER * (8 + (nx - 1) + (ny - 1))
+    return setup + OUTER * INNER * 8 + 3 * (nx - 1 + ny - 1)
 
 
 def solution(mesh):
@@ -892,7 +964,8 @@
         half = lambda *shape: pltpu.VMEM(shape, BF16)
         copies = n_copies(nx, ny)
         scratch = [
-            pltpu.VMEM((NL, N, N), jnp.int32), vm(N, N), vm(N, N), vm(NL, N, N), vm(N, N),
+            pltpu.VMEM((NL, N, N), jnp.int32), vm(N, N), vm(N, N),
+            pltpu.SMEM((2, 16), F32), pltpu.VMEM((n_inst // LN, LN), jnp.int32), vm(n_inst // LN, LN),
             field, field, field, field, field, pltpu.VMEM((NL - 1, 2, NR, LN), F32), field, field,
             single, single, single, field, field, field,
             vm(SL, LN), vm(SL, LN), vm(SL, LN), vm(64, 8 * LN), vm(64, 8 * LN), vm(SL, LN),
@@ -903,21 +976,21 @@
             vm(2, NQ, 2, 8, LN), vm(2, NQ, 2, 8, LN), vm(2, 8, LN), vm(6, 8, LN),
             vm(2, 8 * NQ, SL), vm(2, 8 * NQ, SL),
             vm(NL, 2, 16, SL), vm(NL, 2, 16, SL), vm(NL - 1, 2, 16, SL), vm(NL, 2, 16, SL), vm(NL, 2, 16, SL),
-            vm(2, 16, SL), vm(2, 16, SL), vm(2, 16, SL),
+            vm(2, 16, SL), vm(2, 16, SL), vm(2, 16, SL), vm(2, 16, SL), single, pltpu.VMEM((2, 2, NR, LN), F32),
             vm(5, 8, LN), vm(8, 5, 8, LN), vm(7, 24, LN), vm(its, 8, LN), vm(its, 8, 8, LN),
-            vm(its, 3, 8, LN), vm(its, nx - 1, 3, 8, LN), vm(its, 3, 8, LN), vm(its, ny - 1, 3, 8, LN),
+            vm(3, 3, 8, LN), vm(3, nx - 1, 3, 8, LN), vm(3, 3, 8, LN), vm(3, ny - 1, 3, 8, LN),
             vm(NL, 2, 24, LN), vm(NL, 2, 24, LN), vm(NL, 2, 24, LN), vm(LN, LN),
-            pltpu.SemaphoreType.DMA((copies,)), pltpu.SemaphoreType.DMA((copies,)), pltpu.SemaphoreType.DMA((7,)),
+            pltpu.SemaphoreType.DMA((copies,)), pltpu.SemaphoreType.DMA((copies,)), pltpu.SemaphoreType.DMA((6,)),
         ]
         vmem = pl.BlockSpec(memory_space=pltpu.VMEM)
-        smem = pl.BlockSpec(memory_space=pltpu.SMEM)
-        hbm = pl.BlockSpec(memory_space=pl.ANY)
+        hbm = pl.BlockSpec(memory_space=pltpu.HBM)
         shapes = (jax.ShapeDtypeStruct((NL, N, N), F32), jax.ShapeDtypeStruct((N, N), F32))
+        inside = (vm(NL, N, N), vm(N, N))
         results = pl.pallas_call(
             functools.partial(kernel, nx, ny),
-            out_shape=shapes,
-            in_specs=[hbm, smem, hbm, hbm, vmem, vmem],
-            out_specs=(hbm, hbm),
+            out_shape=inside,
+            in_specs=[hbm] * 6,
+            out_specs=(vmem, vmem),
             scratch_shapes=scratch,
             compiler_params=pltpu.CompilerParams(
                 collective_id=0, has_side_effects=True, vmem_limit_bytes=56 * 1024 * 1024
@@ -933,8 +1006,9 @@
         return pl.pallas_call(
             hand_over,
             out_shape=shapes,
-            in_specs=[vmem, vmem],
+            in_specs=[pl.BlockSpec(memory_space=pl.ANY)] * 2,
             out_specs=(hbm, hbm),
+            compiler_params=pltpu.CompilerParams(vmem_limit_bytes=1024 * 1024),
             scratch_shapes=[pltpu.SemaphoreType.DMA((NL + 1,))],
         )(*results)
 

time: 61.1 us -> 51.9 us (0.85)
  Pallas kernels: 60.3 us -> 50.9 us
    pallas_call x2, Pallas kernels: 60.3 us -> 50.9 us  [the longest x1 49.8 us: step(): pl.pallas_call(functools.partial(kernel, nx, ny), out_shape=inside, in_sp...]
where the time goes in v4:
time: 51.9 us; the launch traced here: 51.6 us
  Pallas kernels  50.9 us (98%)
  between operations  0.64 us (1%)
    pallas_call x1, Pallas kernels, step(): pl.pallas_call(functools.partial(kernel, nx, ny), out_shape=inside, in_sp...  49.8 us
    pallas_call x1, Pallas kernels, step(): pl.pallas_call(hand_over, out_shape=shapes, in_specs=[pl.BlockSpec(memory...  1.09 us

profile of v4, /device:TPU:1, one launch (start us, length us, event | category | flops | bytes accessed | tf_op | source)
XLA Modules:
  0.0 51.6 jit_solution(16957074219310814704)
XLA Ops:
  0.6 49.8 %shard_map.77 = (f32[4,256,256]{2,1,0:T(8,128)S(1)}, f32[256,256]{1,0:T(8,128)S(1)}) custom-call(s32[4,256,256]{2,1,0:T(8,128)} %refs_0_.1, f32[2,16]{1,0:T(2,128)} %refs_1_.1, f32[256,256]{1,0:T(8,128)} %refs_2_.1, f32[256,256]{1,0:T(8,128)} %refs_3_.1, s32[16,128]{1,0:T(8,128)} %bitcast.2, f32[16,128]{1,0:T(8,128)} %bitcast.3), custom_call_target="tpu_custom_call" | custom-call | tf_op jit(solution)/shard_map/pallas_call | solution.py:989
  50.5 1.1 %shard_map.78 = (f32[4,256,256]{2,1,0:T(8,128)}, f32[256,256]{1,0:T(8,128)}) custom-call(f32[4,256,256]{2,1,0:T(8,128)S(1)} %get-tuple-element.4.a, f32[256,256]{1,0:T(8,128)S(1)} %get-tuple-element.5.b), custom_call_target="tpu_custom_call" | custom-call | tf_op jit(solution)/shard_map/pallas_call | solution.py:1006

commit v5 on v4

--- a/solution.py
+++ b/solution.py
@@ -144,14 +144,15 @@
         s = inst_tile[k : k + 1, :] >> 10
         owner = (s % ny) * nx + s // ny
         dest[:, k * LN : (k + 1) * LN] = jnp.where(sub_d == owner, 1.0, 0.0).astype(BF16)
-    before = jnp.zeros((devices, 1), F32)
+    before = jnp.zeros((devices, LN), F32)
+    all_ones = jnp.ones((LN, LN), BF16)
     slot_row = iota((64, LN), 0)
     for k in range(chunks):
         span = slice(k * LN, (k + 1) * LN)
         d = dest[:, span]
         within = jnp.dot(d, up_to, preferred_element_type=F32)
         rank = jnp.sum(d.astype(F32) * (within + before), axis=0, keepdims=True)
-        before = before + within[:, LN - 1 : LN]
+        before = before + jnp.dot(d, all_ones, preferred_element_type=F32)
         at_slot = (slot_row & 31) == rank.astype(jnp.int32) - 1
         t = inst_tile[k : k + 1, :]
         ids = ((t & 992).astype(F32), (t & 31).astype(F32), jnp.zeros((1, LN), F32))
@@ -235,7 +236,7 @@
     table = [[tab[q, k] for k in range(16)] for q in range(2)]
 
     zero8 = jnp.zeros((8, LN), F32)
-    for ref, places in ((t_, (0, NR - 8)), (e1_, (0, 8, NR - 16, NR - 8)), (fr, (0,)), (lat, (NR - 8,))):
+    for ref, places in ((t_, (0, NR - 8)), (e1_, (0, 8, NR - 16, NR - 8)), (fr, (0,)), (lat, (NR - 16, NR - 8))):
         for l in range(NL):
             for h in range(2):
                 for place in places:
@@ -256,6 +257,36 @@
                 drn[h, into, :] = d
                 source_sum = source_sum + d
         return source_sum
+
+    def row_faces(base):
+        here, below = pl.ds(base, 8), pl.ds(base + 1, 8)
+        for l in range(NL):
+            for h in range(2):
+                fr[l, h, here, :] = harmonic(lat[l, h, here, :], lat[l, h, below, :])
+
+    def layer_faces(base, sums):
+        here = pl.ds(base, 8)
+        for h in range(2):
+            vs = [ver[l, h, here, :] for l in range(NL)]
+            for l in range(NL):
+                if l < NL - 1:
+                    v = harmonic(vs[l], vs[l + 1])
+                    fv[l, h, here, :] = v
+                else:
+                    v = snk[h, here, :]
+                if sums is not None:
+                    sums[2 * l + h] += v
+
+    @pl.loop(0, N // 32)
+    def _(a):
+        sums = [zero8] * 8
+        for k in range(4):
+            base = pl.multiple_of(RO + 32 * a + 8 * k, 8)
+            row_faces(base)
+            layer_faces(base, sums)
+        rows = pl.ds(pl.multiple_of(a * 8, 8), 8)
+        for q in range(8):
+            acc[rows, q * LN : (q + 1) * LN] = sums[q]
 
     for c in tile_in:
         c.wait_recv()
@@ -375,10 +406,9 @@
 
     column_form([fcs[l, 0, 7:8, :] for l in range(NL)], [fcs[l, 1, 7:8, :] for l in range(NL)], cf_f)
 
-    def faces(base, sums):
+    def column_faces(base, sums):
         bf = columns(cf_f, base)
-        here, below = pl.ds(base, 8), pl.ds(base + 1, 8)
-        vs = [[ver[l, h, here, :] for h in range(2)] for l in range(NL)]
+        here = pl.ds(base, 8)
         for l in range(NL):
             a0, a1 = lat[l, 0, here, :], lat[l, 1, here, :]
             ra0, ra1 = shift(a0, -1, 1), shift(a1, -1, 1)
@@ -389,32 +419,80 @@
             fc[l, 1, here, :] = c1
             fl[l, 0, here, :] = jnp.where(first_lane, bf[l], rc0)
             fl[l, 1, here, :] = jnp.where(first_lane, rc0, rc1)
-            for h, a in ((0, a0), (1, a1)):
-                fr[l, h, here, :] = harmonic(a, lat[l, h, below, :])
             if sums is not None:
-                sums[0][2 * l] += jnp.where(first_lane, bf[l], c0)
-                sums[0][2 * l + 1] += c1
-            for h in range(2):
-                if l < NL - 1:
-                    v = harmonic(vs[l][h], vs[l + 1][h])
-                    fv[l, h, here, :] = v
-                else:
-                    v = snk[h, here, :]
-                if sums is not None:
-                    sums[1][2 * l + h] += v
-
-    faces(RO - 8, None)
-    faces(RO + N, None)
-
-    @pl.loop(0, N // 32)
-    def _(a):
-        sums = [[zero8] * 8, [zero8] * 8]
-        for k in range(4):
-            faces(pl.multiple_of(RO + 32 * a + 8 * k, 8), sums)
-        rows = pl.ds(pl.multiple_of(a * 8, 8), 8)
-        for q in range(8):
-            acc_n[rows, q * LN : (q + 1) * LN] = sums[0][q]
-            acc[rows, q * LN : (q + 1) * LN] = sums[1][q]
+                sums[2 * l] += jnp.where(first_lane, bf[l], c0)
+                sums[2 * l + 1] += c1
+
+    for base in (RO - 8, RO + N):
+        column_faces(base, None)
+        row_faces(base)
+        layer_faces(base, None)
+    row_faces(RO + N - 8)
+
+    @pl.loop(0, N // 64)
+    def _(pair):
+        for a in (2 * pair, 2 * pair + 1):
+            sums = [zero8] * 8
+            for k in range(4):
+                column_faces(pl.multiple_of(RO + 32 * a + 8 * k, 8), sums)
+            rows = pl.ds(pl.multiple_of(a * 8, 8), 8)
+            for q in range(8):
+                acc_n[rows, q * LN : (q + 1) * LN] = sums[q]
+
+    block_lane = lane8 & 31
+    own_block = (block_lane >= 8) & (block_lane < 16)
+
+    def block_rows(x):
+        return x.reshape(8, 8, LN).sum(axis=1)
+
+    def edge_sums(start):
+        rows = [fr[l, h, pl.ds(start, 8, stride=32), :] for l in range(NL) for h in range(2)]
+        return pick_dot(jnp.concatenate(rows, axis=1), cb[...])
+
+    c_east = edge_sums(RO + 31)
+    c_east_prev = edge_sums(RO - 1)
+    c_north_wide = block_rows(pick_dot(acc_n[...], cbn[...]))
+    c_north = jnp.where(own_block, c_north_wide, 0.0)
+    c_north_prev = jnp.where(own_block, shift(c_north_wide, 1, 1), 0.0)
+    up_sink = block_rows(pick_dot(acc[...], cb[...]))
+    c_up = jnp.where(lane8 < 96, up_sink, 0.0)
+    c_sink = jnp.where(lane8 >= 96, up_sink, 0.0)
+    c_diag = c_east + c_east_prev + c_north + c_north_prev + c_up + shift(c_up, 32, 1) + c_sink
+    tile = zero8
+    for q, x in enumerate((c_east, c_north, c_up + c_sink, c_diag)):
+        tile = tile + shift(jnp.where(own_block, x, 0.0), 8 * q, 1)
+    cm[...] = tile
+    cm_in = {d: (k, send(cm, cmr.at[k], d)) for k, d in enumerate(DIRS)}
+
+    sub8 = iota((8, LN), 0)
+
+    def stack(*rows):
+        out8 = zero8
+        for k, x in enumerate(rows):
+            out8 = jnp.where(sub8 == k, x, out8)
+        return out8
+
+    def sum_along_gx(it, *tiles):
+        s1[it] = stack(*(x.sum(axis=0, keepdims=True) for x in tiles))
+        return [send(s1.at[it], ls1.at[it, d - 1], (d, 0)) for d in range(1, nx)]
+
+    def sum_along_gy(it, arriving):
+        total = s1[it]
+        for d in range(1, nx):
+            arriving[d - 1].wait_recv()
+            total = total + ls1[it, d - 1]
+        s2[it] = total
+        return [send(s2.at[it], ls2.at[it, d - 1], (0, d)) for d in range(1, ny)]
+
+    def sum_end(it, arriving, parts):
+        total = s2[it]
+        for d in range(1, ny):
+            arriving[d - 1].wait_recv()
+            total = total + ls2[it, d - 1]
+        total = total.sum(axis=1, keepdims=True)
+        return [total[q : q + 1, :] for q in range(parts)]
+
+    sums_gx = sum_along_gx(0, source_sum, c_diag, c_sink)
 
     for c in tile_in2:
         c.wait_recv()
@@ -445,71 +523,12 @@
         total = term if total is None else total + term
     total = jnp.concatenate([total * (1.0 / 64.0), jnp.zeros((32, LN - 32), F32)], axis=1)
     total_t = jnp.concatenate([total, jnp.zeros((LN - 32, LN), F32)], axis=0).T
-    sub8 = iota((8, LN), 0)
-
-    def stack(*rows):
-        out8 = zero8
-        for k, x in enumerate(rows):
-            out8 = jnp.where(sub8 == k, x, out8)
-        return out8
-
     ts[...] = stack(total_t[0:1, :], total_t[31:32, :], total[0:1, :], total[31:32, :])
     th_in = {d: (k, send(ts, th.at[k], d)) for k, d in enumerate(DIRS)}
     spread_cols = jnp.where(iota((LN, N), 0) == (iota((LN, N), 1) >> 3), 1.0, 0.0).astype(BF16)
     wide = pick_dot(total, spread_cols)
     for h in range(2):
         dynr[h, 8:40, :] = wide[:, halves[h]]
-
-    block_lane = lane8 & 31
-    own_block = (block_lane >= 8) & (block_lane < 16)
-
-    def block_rows(x):
-        return x.reshape(8, 8, LN).sum(axis=1)
-
-    def edge_sums(start):
-        rows = [fr[l, h, pl.ds(start, 8, stride=32), :] for l in range(NL) for h in range(2)]
-        return pick_dot(jnp.concatenate(rows, axis=1), cb[...])
-
-    c_east = edge_sums(RO + 31)
-    c_east_prev = edge_sums(RO - 1)
-    c_north_wide = block_rows(pick_dot(acc_n[...], cbn[...]))
-    c_north = jnp.where(own_block, c_north_wide, 0.0)
-    c_north_prev = jnp.where(own_block, shift(c_north_wide, 1, 1), 0.0)
-    up_sink = block_rows(pick_dot(acc[...], cb[...]))
-    c_up = jnp.where(lane8 < 96, up_sink, 0.0)
-    c_sink = jnp.where(lane8 >= 96, up_sink, 0.0)
-    c_diag = c_east + c_east_prev + c_north + c_north_prev + c_up + shift(c_up, 32, 1) + c_sink
-    for q, x in enumerate((c_east, c_north, c_up, c_diag, c_sink)):
-        cm[q] = x
-    cm_in = {d: (k, send(cm, cmr.at[k], d)) for k, d in enumerate(DIRS)}
-
-    def sum_along_gx(it, *tiles):
-        parts = len(tiles)
-        for q, x in enumerate(tiles):
-            s1[it, q] = x
-        span = pl.ds(0, parts)
-        return [send(s1.at[it, span], ls1.at[it, d - 1, span], (d, 0)) for d in range(1, nx)]
-
-    def sum_along_gy(it, arriving, parts):
-        span = pl.ds(0, parts)
-        total = [s1[it, q] for q in range(parts)]
-        for d in range(1, nx):
-            arriving[d - 1].wait_recv()
-            for q in range(parts):
-                total[q] = total[q] + ls1[it, d - 1, q]
-        for q in range(parts):
-            s2[it, q] = total[q]
-        return [send(s2.at[it, span], ls2.at[it, d - 1, span], (0, d)) for d in range(1, ny)]
-
-    def sum_end(it, arriving, parts):
-        total = [s2[it, q] for q in range(parts)]
-        for d in range(1, ny):
-            arriving[d - 1].wait_recv()
-            for q in range(parts):
-                total[q] = total[q] + ls2[it, d - 1, q]
-        return [x.sum(axis=0, keepdims=True).sum(axis=1, keepdims=True) for x in total]
-
-    sums_gx = sum_along_gx(0, source_sum, c_diag, c_sink)
 
     def diagonal(base):
         here, above = pl.ds(base, 8), pl.ds(base - 1, 8)
@@ -584,9 +603,9 @@
             body(RO - 8, None, -1, 3)
             body(RO + N, None, 8, 0)
 
-        @pl.loop(0, N // 64)
+        @pl.loop(0, N // 128)
         def _(pair):
-            for a in (2 * pair, 2 * pair + 1):
+            for a in (4 * pair, 4 * pair + 1, 4 * pair + 2, 4 * pair + 3):
                 sums = [zero8] * 8
                 for k in range(4):
                     body(pl.multiple_of(RO + 32 * a + 8 * k, 8), sums, a, k)
@@ -599,17 +618,16 @@
     lane24 = iota((24, LN), 1)
 
     def sweep_neighbours(x):
-        return (
-            coef[1] * shift(x, -1, 0) + coef[2] * shift(x, 1, 0)
-            + coef[3] * shift(x, -1, 1) + coef[4] * shift(x, 1, 1)
-            + coef[5] * shift(x, -32, 1) + coef[6] * shift(x, 32, 1)
-        )
+        lanes = [shift(x, by, 1) for by in (-1, 1, -32, 32)]
+        rows = coef[1] * shift(x, -1, 0) + coef[2] * shift(x, 1, 0)
+        return rows, (coef[3] * lanes[0] + coef[4] * lanes[1]) + (coef[5] * lanes[2] + coef[6] * lanes[3])
 
     def coarse_sweeps(right):
         rw = coef[0] * right
         x = rw
         for _ in range(CJ - 1):
-            x = (1.0 - DAMPING) * x + rw + sweep_neighbours(x)
+            rows, lanes = sweep_neighbours(x)
+            x = ((1.0 - DAMPING) * x + rw + rows) + lanes
         return x
 
     def assemble(own, other):
@@ -690,7 +708,34 @@
             gr[0, h, here, :] = wg[top - 1, h, here, :] * (fv[top - 1, h, here, :] * e)
 
     over_rows(sink_second, margins=False)
-    sums_gy = sum_along_gy(0, sums_gx, 3)
+    first_gy = sum_along_gy(0, sums_gx)
+
+    for _, c in cm_in.values():
+        c.wait_recv()
+    def coupling(q):
+        def of(tile):
+            return jnp.where((lane8 >> 3) & 3 == (q + 1) % 4, tile, 0.0)
+
+        rows = []
+        for dx in (-1, 0, 1):
+            tiles = [cm[...] if (dx, dy) == (0, 0) else cmr[cm_in[(-dx, -dy)][0]] for dy in (-1, 0, 1)]
+            rows.append(sum(shift(of(tile), 8 * (dy - q), 1) for dy, tile in zip((-1, 0, 1), tiles, strict=True)))
+        return jnp.concatenate(rows, axis=0)
+
+    w_east, w_north, w_up, w_diag = (coupling(q) for q in range(4))
+    w_sink = jnp.where(lane24 >= 96, w_up, 0.0)
+    w_up = jnp.where(lane24 < 96, w_up, 0.0)
+    gain = jnp.where((lane24 & 31) < 24, DAMPING / jnp.maximum(w_diag, 1e-30), 0.0)
+    coef[0] = gain
+    coef[1] = gain * w_east
+    coef[2] = gain * shift(w_east, 1, 0)
+    coef[3] = gain * w_north
+    coef[4] = gain * shift(w_north, 1, 1)
+    coef[5] = gain * w_up
+    coef[6] = gain * shift(w_up, 32, 1)
+    adjoint = coarse_sweeps(w_sink)
+    own_adjoint = jnp.where(own_block, adjoint[8:16, :], 0.0)
+    sums_gx = sum_along_gx(1, own_adjoint * own_c)
 
     @pl.loop(0, N // 32)
     def _(a):
@@ -747,25 +792,8 @@
                 fr[0, h, face : face + 1, :] * e1_[0, h, beyond : beyond + 1, :]
             )
 
-    for _, c in cm_in.values():
-        c.wait_recv()
-    w_east, w_north, w_up, w_diag, w_sink = (
-        assemble(cm[q], lambda d, q=q: cmr[cm_in[(-d[0], -d[1])][0], q]) for q in range(5)
-    )
-    gain = jnp.where((lane24 & 31) < 24, DAMPING / jnp.maximum(w_diag, 1e-30), 0.0)
-    coef[0] = gain
-    coef[1] = gain * w_east
-    coef[2] = gain * shift(w_east, 1, 0)
-    coef[3] = gain * w_north
-    coef[4] = gain * shift(w_north, 1, 1)
-    coef[5] = gain * w_up
-    coef[6] = gain * shift(w_up, 32, 1)
-    adjoint = coarse_sweeps(w_sink)
-    own_adjoint = jnp.where(own_block, adjoint[8:16, :], 0.0)
-    sums_gx = sum_along_gx(1, own_adjoint * own_c)
-
     ts_old = None
-    balance = diag_total = sink_total = source_total = None
+    former = diag_total = sink_total = source_total = None
     sweeps = OUTER * INNER
     for it in range(sweeps):
         first, last = it == 0, it == sweeps - 1
@@ -790,12 +818,15 @@
                     us[l][g] = u if first else ts_old[l][g] + u
             edge_terms(us, cf_t)
 
+            held = 2 if first else NL
             def half_residual(base, sums, a, k):
                 here = pl.ds(base, 8)
-                mid, res = couple(t_, base, columns(cf_t, base), NL)
+                mid, res = couple(t_, base, columns(cf_t, base), held)
                 for l in range(NL):
                     for h in range(2):
-                        r = res[l][h] - dg[l, h, here, :] * mid[l][h]
+                        r = zero8 if res[l][h] is None else res[l][h]
+                        if l < held:
+                            r = r - dg[l, h, here, :] * mid[l][h]
                         if l == 0 and not fresh:
                             r = r + src[h, here, :]
                         r_[l, h, here, :] = r
@@ -804,24 +835,33 @@
 
             over_rows(half_residual)
             if it == 2:
-                sums_gy = sum_along_gy(2, sums_gx, 2)
+                sums_gy = sum_along_gy(2, sums_gx)
             next_c = block_rows(pick_dot(acc[...], cb[...]))
 
+        if last:
+            for c in started[: -len(DIRS)]:
+                c.wait_send()
         for _, c in side.values():
             c.wait_recv()
         x = coarse_sweeps(assemble(own_c, lambda d: nb[it, side[(-d[0], -d[1])][0]]))
-        if first:
-            source_total, diag_total, sink_total = sum_end(0, sums_gy, 3)
-        elif it == 1:
-            source_total = source_total - sum_end(1, sums_gy, 1)[0] - balance * sink_total
+        if it == 1:
+            source_total = source_total - sum_end(1, sums_gy, 1)[0] - former * sink_total
+            x = x + former * (1.0 - adjoint)
         elif last:
             source_total, less = sum_end(2, sums_gy, 2)
             former = BALANCE_WEIGHT * source_total / diag_total
             source_total = source_total - less - former * sink_total
             x = x + former * (1.0 - adjoint)
-        if it != 2:
-            balance = BALANCE_WEIGHT * source_total / diag_total
-            x = x + balance
+        if it % INNER == 1:
+            x = x + BALANCE_WEIGHT * source_total / diag_total
+
+        def send_next(total_c):
+            moved = (x - sum(sweep_neighbours(x)) * (1.0 / DAMPING))[8:16, :] * c_diag
+            own = total_c - jnp.where(own_block, moved, 0.0)
+            return own, send_coarse(it + 1, own)
+
+        if not last and not fresh:
+            own_c, side = send_next(next_c)
 
         for l in range(NL):
             for h in range(2):
@@ -861,11 +901,9 @@
 
             over_rows(new_source)
             next_c = next_c + block_rows(pick_dot(acc[:, 0 : 2 * LN], cb[0 : 2 * LN, :]))
-        moved = (x - sweep_neighbours(x) * (1.0 / DAMPING))[8:16, :] * c_diag
-        own_c = next_c - jnp.where(own_block, moved, 0.0)
-        side = send_coarse(it + 1, own_c)
+            own_c, side = send_next(next_c)
         if first:
-            sums_gy = sum_along_gy(1, sums_gx, 1)
+            sums_gy = sum_along_gy(1, sums_gx)
 
         def whole_residual(base, sums, a, k):
             here, above = pl.ds(base, 8), pl.ds(base - 1, 8)
@@ -930,9 +968,24 @@
                     r = r + srs[g]
                 rs[l][g] = r
                 e1s[l][g] = wgs[l, g] * r
+        if first:
+            source_total, diag_total, sink_total = sum_end(0, first_gy, 3)
+            former = BALANCE_WEIGHT * source_total / diag_total
+
+            def sink_part(base, sums, a, k):
+                here = pl.ds(base, 8)
+                for h in range(2):
+                    r = r_[NL - 1, h, here, :] - former * snk[h, here, :]
+                    r_[NL - 1, h, here, :] = r
+                    e1_[NL - 1, h, here, :] = wg[NL - 1, h, here, :] * r
+
+            over_rows(sink_part)
+            for g in sides:
+                rs[NL - 1][g] = rs[NL - 1][g] - former * sks[g]
+                e1s[NL - 1][g] = wgs[NL - 1, g] * rs[NL - 1][g]
         edge_terms(e1s, cf_e)
 
-    for c in started:
+    for c in started[-len(DIRS) :]:
         c.wait_send()
 
 
@@ -977,8 +1030,8 @@
             vm(2, 8 * NQ, SL), vm(2, 8 * NQ, SL),
             vm(NL, 2, 16, SL), vm(NL, 2, 16, SL), vm(NL - 1, 2, 16, SL), vm(NL, 2, 16, SL), vm(NL, 2, 16, SL),
             vm(2, 16, SL), vm(2, 16, SL), vm(2, 16, SL), vm(2, 16, SL), single, pltpu.VMEM((2, 2, NR, LN), F32),
-            vm(5, 8, LN), vm(8, 5, 8, LN), vm(7, 24, LN), vm(its, 8, LN), vm(its, 8, 8, LN),
-            vm(3, 3, 8, LN), vm(3, nx - 1, 3, 8, LN), vm(3, 3, 8, LN), vm(3, ny - 1, 3, 8, LN),
+            vm(8, LN), vm(8, 8, LN), vm(7, 24, LN), vm(its, 8, LN), vm(its, 8, 8, LN),
+            vm(3, 8, LN), vm(3, nx - 1, 8, LN), vm(3, 8, LN), vm(3, ny - 1, 8, LN),
             vm(NL, 2, 24, LN), vm(NL, 2, 24, LN), vm(NL, 2, 24, LN), vm(LN, LN),
             pltpu.SemaphoreType.DMA((copies,)), pltpu.SemaphoreType.DMA((copies,)), pltpu.SemaphoreType.DMA((6,)),
         ]

time: 51.9 us -> 49.6 us (0.956)
  Pallas kernels: 50.9 us -> 48.8 us
    pallas_call x1, Pallas kernels: 49.8 us -> 47.7 us  [step(): pl.pallas_call(functools.partial(kernel, nx, ny), out_shape=inside, in_sp...]
where the time goes in v5:
time: 49.6 us; the launch traced here: 49.4 us
  Pallas kernels  48.8 us (98%)
  between operations  0.64 us (1%)
    pallas_call x1, Pallas kernels, step(): pl.pallas_call(functools.partial(kernel, nx, ny), out_shape=inside, in_sp...  47.7 us
    pallas_call x1, Pallas kernels, step(): pl.pallas_call(hand_over, out_shape=shapes, in_specs=[pl.BlockSpec(memory...  1.09 us

profile of v5, /device:TPU:1, one launch (start us, length us, event | category | flops | bytes accessed | tf_op | source)
XLA Modules:
  0.0 49.4 jit_solution(3970459157679825789)
XLA Ops:
  0.6 47.7 %shard_map.77 = (f32[4,256,256]{2,1,0:T(8,128)S(1)}, f32[256,256]{1,0:T(8,128)S(1)}) custom-call(s32[4,256,256]{2,1,0:T(8,128)} %refs_0_.1, f32[2,16]{1,0:T(2,128)} %refs_1_.1, f32[256,256]{1,0:T(8,128)} %refs_2_.1, f32[256,256]{1,0:T(8,128)} %refs_3_.1, s32[16,128]{1,0:T(8,128)} %bitcast.2, f32[16,128]{1,0:T(8,128)} %bitcast.3), custom_call_target="tpu_custom_call" | custom-call | tf_op jit(solution)/shard_map/pallas_call | solution.py:1042
  48.3 1.1 %shard_map.78 = (f32[4,256,256]{2,1,0:T(8,128)}, f32[256,256]{1,0:T(8,128)}) custom-call(f32[4,256,256]{2,1,0:T(8,128)S(1)} %get-tuple-element.4.a, f32[256,256]{1,0:T(8,128)S(1)} %get-tuple-element.5.b), custom_call_target="tpu_custom_call" | custom-call | tf_op jit(solution)/shard_map/pallas_call | solution.py:1059

commit v6 on v5

--- a/solution.py
+++ b/solution.py
@@ -277,16 +277,35 @@
                 if sums is not None:
                     sums[2 * l + h] += v
 
-    @pl.loop(0, N // 32)
-    def _(a):
-        sums = [zero8] * 8
-        for k in range(4):
-            base = pl.multiple_of(RO + 32 * a + 8 * k, 8)
-            row_faces(base)
-            layer_faces(base, sums)
-        rows = pl.ds(pl.multiple_of(a * 8, 8), 8)
-        for q in range(8):
-            acc[rows, q * LN : (q + 1) * LN] = sums[q]
+    def column_faces(base, sums):
+        here = pl.ds(base, 8)
+        for l in range(NL):
+            a0, a1 = lat[l, 0, here, :], lat[l, 1, here, :]
+            ra0, ra1 = shift(a0, -1, 1), shift(a1, -1, 1)
+            c0 = harmonic(a0, jnp.where(last_lane, ra1, ra0))
+            c1 = harmonic(a1, ra1)
+            rc0, rc1 = shift(c0, 1, 1), shift(c1, 1, 1)
+            fc[l, 0, here, :] = c0
+            fc[l, 1, here, :] = c1
+            fl[l, 0, here, :] = rc0
+            fl[l, 1, here, :] = jnp.where(first_lane, rc0, rc1)
+            if sums is not None:
+                sums[2 * l] += c0
+                sums[2 * l + 1] += c1
+
+    @pl.loop(0, N // 64)
+    def _(pair):
+        for a in (2 * pair, 2 * pair + 1):
+            sums, sums_n = [zero8] * 8, [zero8] * 8
+            for k in range(4):
+                base = pl.multiple_of(RO + 32 * a + 8 * k, 8)
+                row_faces(base)
+                layer_faces(base, sums)
+                column_faces(base, sums_n)
+            rows = pl.ds(pl.multiple_of(a * 8, 8), 8)
+            for q in range(8):
+                acc[rows, q * LN : (q + 1) * LN] = sums[q]
+                acc_n[rows, q * LN : (q + 1) * LN] = sums_n[q]
 
     for c in tile_in:
         c.wait_recv()
@@ -406,38 +425,33 @@
 
     column_form([fcs[l, 0, 7:8, :] for l in range(NL)], [fcs[l, 1, 7:8, :] for l in range(NL)], cf_f)
 
-    def column_faces(base, sums):
+    def edge_faces(base, sums):
         bf = columns(cf_f, base)
         here = pl.ds(base, 8)
         for l in range(NL):
-            a0, a1 = lat[l, 0, here, :], lat[l, 1, here, :]
-            ra0, ra1 = shift(a0, -1, 1), shift(a1, -1, 1)
-            c0 = harmonic(a0, jnp.where(last_lane, ra1, ra0))
-            c1 = jnp.where(last_lane, bf[l], harmonic(a1, ra1))
-            rc0, rc1 = shift(c0, 1, 1), shift(c1, 1, 1)
-            fc[l, 0, here, :] = c0
-            fc[l, 1, here, :] = c1
-            fl[l, 0, here, :] = jnp.where(first_lane, bf[l], rc0)
-            fl[l, 1, here, :] = jnp.where(first_lane, rc0, rc1)
+            fc[l, 1, here, :] = jnp.where(last_lane, bf[l], fc[l, 1, here, :])
+            fl[l, 0, here, :] = jnp.where(first_lane, bf[l], fl[l, 0, here, :])
             if sums is not None:
-                sums[2 * l] += jnp.where(first_lane, bf[l], c0)
-                sums[2 * l + 1] += c1
+                sums[l] += bf[l]
 
     for base in (RO - 8, RO + N):
         column_faces(base, None)
         row_faces(base)
         layer_faces(base, None)
+        edge_faces(base, None)
     row_faces(RO + N - 8)
 
     @pl.loop(0, N // 64)
     def _(pair):
         for a in (2 * pair, 2 * pair + 1):
-            sums = [zero8] * 8
+            sums = [zero8] * NL
             for k in range(4):
-                column_faces(pl.multiple_of(RO + 32 * a + 8 * k, 8), sums)
+                edge_faces(pl.multiple_of(RO + 32 * a + 8 * k, 8), sums)
             rows = pl.ds(pl.multiple_of(a * 8, 8), 8)
-            for q in range(8):
-                acc_n[rows, q * LN : (q + 1) * LN] = sums[q]
+            for l in range(NL):
+                for h, lane in ((0, first_lane), (1, last_lane)):
+                    span = slice((2 * l + h) * LN, (2 * l + h + 1) * LN)
+                    acc_n[rows, span] = jnp.where(lane, sums[l], acc_n[rows, span])
 
     block_lane = lane8 & 31
     own_block = (block_lane >= 8) & (block_lane < 16)

time: 49.6 us -> 48.7 us (0.982)
  Pallas kernels: 48.8 us -> 48 us
    pallas_call x1, Pallas kernels: 47.7 us -> 46.9 us  [step(): pl.pallas_call(functools.partial(kernel, nx, ny), out_shape=inside, in_sp...]
where the time goes in v6:
time: 48.7 us; the launch traced here: 48.6 us
  Pallas kernels  48 us (99%)
  between operations  0.64 us (1%)
    pallas_call x1, Pallas kernels, step(): pl.pallas_call(functools.partial(kernel, nx, ny), out_shape=inside, in_sp...  46.9 us
    pallas_call x1, Pallas kernels, step(): pl.pallas_call(hand_over, out_shape=shapes, in_specs=[pl.BlockSpec(memory...  1.09 us

profile of v6, /device:TPU:1, one launch (start us, length us, event | category | flops | bytes accessed | tf_op | source)
XLA Modules:
  0.0 48.6 jit_solution(17469750372397739841)
XLA Ops:
  0.6 46.9 %shard_map.77 = (f32[4,256,256]{2,1,0:T(8,128)S(1)}, f32[256,256]{1,0:T(8,128)S(1)}) custom-call(s32[4,256,256]{2,1,0:T(8,128)} %refs_0_.1, f32[2,16]{1,0:T(2,128)} %refs_1_.1, f32[256,256]{1,0:T(8,128)} %refs_2_.1, f32[256,256]{1,0:T(8,128)} %refs_3_.1, s32[16,128]{1,0:T(8,128)} %bitcast.2, f32[16,128]{1,0:T(8,128)} %bitcast.3), custom_call_target="tpu_custom_call" | custom-call | tf_op jit(solution)/shard_map/pallas_call | solution.py:1056
  47.5 1.1 %shard_map.78 = (f32[4,256,256]{2,1,0:T(8,128)}, f32[256,256]{1,0:T(8,128)}) custom-call(f32[4,256,256]{2,1,0:T(8,128)S(1)} %get-tuple-element.4.a, f32[256,256]{1,0:T(8,128)S(1)} %get-tuple-element.5.b), custom_call_target="tpu_custom_call" | custom-call | tf_op jit(solution)/shard_map/pallas_call | solution.py:1073

commit v7 on v6

--- a/solution.py
+++ b/solution.py
@@ -66,8 +66,8 @@
     return out + [x.astype(BF16)]
 
 
-def pick_dot(x, ones):
-    return sum(jnp.dot(part, ones, preferred_element_type=F32) for part in pieces(x, 3))
+def pick_dot(x, ones, parts=3):
+    return sum(jnp.dot(part, ones, preferred_element_type=F32) for part in pieces(x, parts))
 
 
 class Layout:
@@ -135,6 +135,23 @@
 
     devices = nx * ny
     chunks = inst_tile.shape[0]
+    col_n = iota((LN, LN), 1)
+    row_n = iota((LN, LN), 0)
+    for l in range(NL):
+        for h in range(2):
+            span = pl.ds((2 * l + h) * LN, LN)
+            goal = l * 32 + 8 + h * 4 + (row_n >> 5)
+            cb[span, :] = jnp.where(col_n == goal, 1.0, 0.0).astype(BF16)
+            hit = ((row_n & 31) == 31) & (col_n == goal)
+            if h == 0:
+                hit = hit | ((row_n == 0) & (col_n == l * 32 + 7))
+            cbn[span, :] = jnp.where(hit, 1.0, 0.0).astype(BF16)
+    zero8 = jnp.zeros((8, LN), F32)
+    for ref, places in ((t_, (0, NR - 8)), (e1_, (0, 8, NR - 16, NR - 8)), (fr, (0,)), (lat, (NR - 16, NR - 8))):
+        for l in range(NL):
+            for h in range(2):
+                for place in places:
+                    ref[l, h, place : place + 8, :] = zero8
     for c in fetch_small:
         c.wait()
     sub_d = iota((devices, LN), 0)
@@ -222,25 +239,7 @@
             sq_s[1, 8 * q : 8 * q + 8, span] = block[16 * q : 16 * q + 8, :]
     margin_we = [send(sq_s.at[s], rq_s.at[s], (0, 2 * s - 1)) for s in range(2)]
 
-    col_n = iota((LN, LN), 1)
-    row_n = iota((LN, LN), 0)
-    for l in range(NL):
-        for h in range(2):
-            span = pl.ds((2 * l + h) * LN, LN)
-            goal = l * 32 + 8 + h * 4 + (row_n >> 5)
-            cb[span, :] = jnp.where(col_n == goal, 1.0, 0.0).astype(BF16)
-            hit = ((row_n & 31) == 31) & (col_n == goal)
-            if h == 0:
-                hit = hit | ((row_n == 0) & (col_n == l * 32 + 7))
-            cbn[span, :] = jnp.where(hit, 1.0, 0.0).astype(BF16)
     table = [[tab[q, k] for k in range(16)] for q in range(2)]
-
-    zero8 = jnp.zeros((8, LN), F32)
-    for ref, places in ((t_, (0, NR - 8)), (e1_, (0, 8, NR - 16, NR - 8)), (fr, (0,)), (lat, (NR - 16, NR - 8))):
-        for l in range(NL):
-            for h in range(2):
-                for place in places:
-                    ref[l, h, place : place + 8, :] = zero8
 
     @pl.loop(0, N // 32, init_carry=power_sum)
     def source_sum(a, source_sum):
@@ -850,7 +849,7 @@
             over_rows(half_residual)
             if it == 2:
                 sums_gy = sum_along_gy(2, sums_gx)
-            next_c = block_rows(pick_dot(acc[...], cb[...]))
+            next_c = block_rows(pick_dot(acc[...], cb[...], 2))
 
         if last:
             for c in started[: -len(DIRS)]:

time: 48.7 us -> 48.6 us (level)
  no operation moved by 1% of the time
where the time goes in v7:
time: 48.6 us; the launch traced here: 48.5 us
  Pallas kernels  47.9 us (99%)
  between operations  0.64 us (1%)
    pallas_call x1, Pallas kernels, step(): pl.pallas_call(functools.partial(kernel, nx, ny), out_shape=inside, in_sp...  46.8 us
    pallas_call x1, Pallas kernels, step(): pl.pallas_call(hand_over, out_shape=shapes, in_specs=[pl.BlockSpec(memory...  1.09 us

profile of v7, /device:TPU:1, one launch (start us, length us, event | category | flops | bytes accessed | tf_op | source)
XLA Modules:
  0.0 48.5 jit_solution(7285302231279906633)
XLA Ops:
  0.6 46.8 %shard_map.77 = (f32[4,256,256]{2,1,0:T(8,128)S(1)}, f32[256,256]{1,0:T(8,128)S(1)}) custom-call(s32[4,256,256]{2,1,0:T(8,128)} %refs_0_.1, f32[2,16]{1,0:T(2,128)} %refs_1_.1, f32[256,256]{1,0:T(8,128)} %refs_2_.1, f32[256,256]{1,0:T(8,128)} %refs_3_.1, s32[16,128]{1,0:T(8,128)} %bitcast.2, f32[16,128]{1,0:T(8,128)} %bitcast.3), custom_call_target="tpu_custom_call" | custom-call | tf_op jit(solution)/shard_map/pallas_call | solution.py:1055
  47.4 1.1 %shard_map.78 = (f32[4,256,256]{2,1,0:T(8,128)}, f32[256,256]{1,0:T(8,128)}) custom-call(f32[4,256,256]{2,1,0:T(8,128)S(1)} %get-tuple-element.4.a, f32[256,256]{1,0:T(8,128)S(1)} %get-tuple-element.5.b), custom_call_target="tpu_custom_call" | custom-call | tf_op jit(solution)/shard_map/pallas_call | solution.py:1072
